TPU v7x, 256 devices: a whole 4x4x8 slice. The times are simulated.
256 devices in a mesh: seq: 32 (over y_hi, z, core), chan: 8 (over y_lo, x).
Axes of the slice: x: 4, y: 4 (y_hi: 2, y_lo: 2; y = y_hi * 2 + y_lo), z: 8, core: 2. Of those that a mesh axis runs over, the one named last changes fastest.
Arguments:
- tokens: bfloat16 [65536, 2048], P('seq', 'chan'), may hold values from -6 to 6
- spectrum: bfloat16 [2, 256, 512, 2048], P(None, 'seq', None, 'chan'), may hold values from -6 to 6
- skip_gain: float32 [2048], P('chan'), may hold values from -1 to 1
- norm_gain: float32 [2048], P('chan'), may hold values from 0.1 to 1.9
- gate_first: bfloat16 [8, 256, 256], P('chan'), may hold values from -0.375 to 0.375
- up_first: bfloat16 [8, 256, 256], P('chan'), may hold values from -0.375 to 0.375
- gate_second: bfloat16 [8, 256, 1024], P('chan'), may hold values from -0.375 to 0.375
- up_second: bfloat16 [8, 256, 1024], P('chan'), may hold values from -0.375 to 0.375
- down_first: bfloat16 [8, 1024, 256], P('chan'), may hold values from -0.1875 to 0.1875
- down_second: bfloat16 [8, 256, 256], P('chan'), may hold values from -0.375 to 0.375
Outputs:
- layer_out: bfloat16 [65536, 2048], P('seq', 'chan')
All inputs are finite; a program needn't handle non-finite values.
Results may differ from a plain program's by a relative error of at most 0.017.
Values may be sent and summed in bfloat16 or wider, within the bound.
No kernel may reach another device: no remote copies, remote signals or barrier semaphores. Data moves between devices by JAX's collectives and lax.ppermute only.
A program may use at most 128 MiB of HBM per device.

v0:
```python
import math

import jax
import jax.numpy as jnp
from jax import lax
from jax.sharding import PartitionSpec as P

D = 2048
COLS = 512
ROWS_DEV = 4
BLOCKS = 8
PB = 256
HB = 1024
PIECE = 32


def row_table(total_rows, real_rows):
    crow = lax.broadcasted_iota(jnp.int32, (total_rows, real_rows), 0)
    arow = lax.broadcasted_iota(jnp.int32, (total_rows, real_rows), 1)
    angles = 2.0 * math.pi / total_rows * (crow * arow % total_rows).astype(jnp.float32)
    return jnp.stack([jnp.cos(angles), -jnp.sin(angles)]).astype(jnp.bfloat16)


def column_tables(width):
    first = lax.broadcasted_iota(jnp.int32, (width, width), 0)
    second = lax.broadcasted_iota(jnp.int32, (width, width), 1)
    angles = 2.0 * math.pi / width * (first * second % width).astype(jnp.float32)
    cosine = jnp.cos(angles)
    sine = jnp.sin(angles)
    forward = jnp.stack([jnp.stack([cosine, -sine]), jnp.stack([sine, cosine])]).astype(
        jnp.bfloat16
    )
    inverse = jnp.stack([jnp.stack([cosine, sine]), jnp.stack([-sine, cosine])]).astype(
        jnp.bfloat16
    )
    return (forward, inverse)


def twiddle(row_start, rows, col_start, cols, span):
    crow = row_start + lax.broadcasted_iota(jnp.int32, (rows, cols), 0)
    bcol = col_start + lax.broadcasted_iota(jnp.int32, (rows, cols), 1)
    angles = 2.0 * math.pi / span * (crow * bcol % span).astype(jnp.float32)
    return (jnp.cos(angles)[:, :, None], jnp.sin(angles)[:, :, None])


def forward_rows(block, col_start, span):
    real_rows, width = (block.shape[0], block.shape[1])
    table = row_table(2 * real_rows, real_rows)
    spectra = jnp.einsum("kca,abh->kcbh", table, block, preferred_element_type=jnp.float32)
    cosine, sine = twiddle(0, 2 * real_rows, col_start, width, span)
    real_part = spectra[0] * cosine + spectra[1] * sine
    imag_part = spectra[1] * cosine - spectra[0] * sine
    return jnp.stack([real_part, imag_part]).astype(jnp.bfloat16)


def middle_part(freq, kernel, row_start, span):
    rows, width = (freq.shape[1], freq.shape[2])
    forward, inverse = column_tables(width)
    spectra = jnp.einsum("kcbh,kjbd->jcdh", freq, forward, preferred_element_type=jnp.float32)
    kernel_f = kernel.astype(jnp.float32)
    prod_real = spectra[0] * kernel_f[0] - spectra[1] * kernel_f[1]
    prod_imag = spectra[0] * kernel_f[1] + spectra[1] * kernel_f[0]
    product = jnp.stack([prod_real, prod_imag]).astype(jnp.bfloat16)
    back = jnp.einsum("kcdh,kjdb->jcbh", product, inverse, preferred_element_type=jnp.float32)
    cosine, sine = twiddle(row_start, rows, 0, width, span)
    real_part = back[0] * cosine - back[1] * sine
    imag_part = back[1] * cosine + back[0] * sine
    return jnp.stack([real_part, imag_part]).astype(jnp.bfloat16)


def final_rows(freq, span):
    total_rows = freq.shape[1]
    table = row_table(total_rows, total_rows // 2)
    summed = jnp.einsum("kcbh,kca->abh", freq, table, preferred_element_type=jnp.float32)
    return (summed * (1.0 / span)).astype(jnp.bfloat16)


def per_device(
    tokens,
    spectrum,
    skip_gain,
    norm_gain,
    gate_first,
    up_first,
    gate_second,
    up_second,
    down_first,
    down_second,
):
    seq_count = lax.axis_size("seq")
    tok_dev, chan_dev = tokens.shape
    span = 2 * ROWS_DEV * seq_count * COLS
    grid = tokens.reshape(ROWS_DEV, COLS, chan_dev)
    col_dev = COLS // seq_count
    col_start = lax.axis_index("seq") * col_dev
    freq = forward_rows(
        lax.all_to_all(grid, "seq", split_axis=1, concat_axis=0, tiled=True), col_start, span
    )
    split = lax.all_to_all(freq, "seq", split_axis=1, concat_axis=2, tiled=True)
    row_dev = split.shape[1]
    mixed = middle_part(split, spectrum, lax.axis_index("seq") * row_dev, span)
    conv_cols = final_rows(
        lax.all_to_all(mixed, "seq", split_axis=2, concat_axis=1, tiled=True), span
    )
    conv = lax.all_to_all(conv_cols, "seq", split_axis=0, concat_axis=1, tiled=True).reshape(
        tok_dev, chan_dev
    )
    stream = (conv.astype(jnp.float32) + skip_gain * tokens.astype(jnp.float32)).astype(
        jnp.bfloat16
    )
    stream_f = stream.astype(jnp.float32)
    squares = lax.psum(jnp.sum(stream_f * stream_f, axis=1), "chan")
    normed = (stream_f * lax.rsqrt(squares / D + 1e-05)[:, None] * norm_gain).astype(jnp.bfloat16)
    chan_count = lax.axis_size("chan")
    local_blocks = BLOCKS // chan_count
    normed = normed.reshape(tok_dev, local_blocks, PB)

    def permuted(first_section):
        shaped = first_section.reshape(local_blocks, chan_count, local_blocks * PIECE, tok_dev)
        return shaped.transpose(1, 0, 2, 3)

    gate_mid = jnp.einsum(
        "tip,ipq->iqt", normed, gate_first, preferred_element_type=jnp.float32
    ).astype(jnp.bfloat16)
    up_mid = jnp.einsum(
        "tip,ipq->iqt", normed, up_first, preferred_element_type=jnp.float32
    ).astype(jnp.bfloat16)
    gate_in, up_in = (
        lax.all_to_all(permuted(gate_mid), "chan", split_axis=0, concat_axis=0, tiled=True),
        lax.all_to_all(permuted(up_mid), "chan", split_axis=0, concat_axis=0, tiled=True),
    )
    gate_w = gate_second.reshape(local_blocks, BLOCKS, PIECE, HB)
    up_w = up_second.reshape(local_blocks, BLOCKS, PIECE, HB)
    gate = jnp.einsum("ijmt,jimh->tjh", gate_in, gate_w, preferred_element_type=jnp.float32)
    upper = jnp.einsum("ijmt,jimh->tjh", up_in, up_w, preferred_element_type=jnp.float32)
    act = (jax.nn.gelu(gate, approximate=True) * upper).astype(jnp.bfloat16)
    down_mid = jnp.einsum(
        "tjh,jhq->jqt", act, down_first, preferred_element_type=jnp.float32
    ).astype(jnp.bfloat16)
    down_in = lax.all_to_all(permuted(down_mid), "chan", split_axis=0, concat_axis=0, tiled=True)
    down_w = down_second.reshape(local_blocks, BLOCKS, PIECE, PB)
    result = jnp.einsum("jomt,ojmp->top", down_in, down_w, preferred_element_type=jnp.float32)
    return (stream_f + result.reshape(tok_dev, chan_dev)).astype(jnp.bfloat16)


def solution(mesh):
    in_specs = (
        P("seq", "chan"),
        P(None, "seq", None, "chan"),
        P("chan"),
        P("chan"),
        P("chan", None, None),
        P("chan", None, None),
        P("chan", None, None),
        P("chan", None, None),
        P("chan", None, None),
        P("chan", None, None),
    )
    out_specs = P("seq", "chan")
    return jax.shard_map(
        per_device, mesh=mesh, in_specs=in_specs, out_specs=out_specs, check_vma=False
    )
```

profile of v0, /device:TPU:32, one launch (start us, length us, event | category | flops | bytes accessed | tf_op | source)
XLA Modules:
  0.0 391.3 jit_solution(8543779385940512259)
XLA Ops:
  0.0 0.0 copy-start
  0.0 3.1 copy.42
  3.1 11.4 %all-to-all-start = ((bf16[4,512,256]{2,0,1:T(4,128)(2,1)}), bf16[4,512,256]{2,0,1:T(4,128)(2,1)S(1)}, u32[]{:S(2)}, u32[]{:S(2)}) async-start(bf16[4,512,256]{2,0,1:T(4,128)(2,1)} %copy.42), calls=%async_computation | async-start | bytes 2097152 | tf_op jit(solution)/shard_map/all_to_all | solution.py:97
  14.4 0.5 negate_convert_fusion.1
  15.0 0.2 fusion.80
  15.2 29.8 %all-to-all-done = bf16[4,512,256]{2,0,1:T(4,128)(2,1)S(1)} async-done(((bf16[4,512,256]{2,0,1:T(4,128)(2,1)}), bf16[4,512,256]{2,0,1:T(4,128)(2,1)S(1)}, u32[]{:S(2)}, u32[]{:S(2)}) %all-to-all-start) | async-done | bytes 1048608 | tf_op jit(solution)/shard_map/all_to_all | solution.py:97
  44.9 0.1 copy.43
  45.1 0.8 copy.44
  45.9 0.3 reshape.290
  46.2 1.2 fusion.57
  47.4 1.5 add_convert_fusion.2
  48.9 0.4 pad_maximum_fusion
  49.3 4.3 %copy.45 = bf16[2,256,16,256]{3,2,0,1:T(8,128)(2,1)} copy(bf16[2,256,16,256]{3,1,2,0:T(8,128)(2,1)S(1)} %pad_maximum_fusion) | data formatting | bytes 8388608 | tf_op jit(solution)/shard_map/stack | solution.py:53
  53.6 4.8 %all-to-all-start.1 = ((bf16[2,256,16,256]{3,2,0,1:T(8,128)(2,1)}), bf16[2,256,16,256]{3,2,0,1:T(8,128)(2,1)}, u32[]{:S(2)}, u32[]{:S(2)}) async-start(bf16[2,256,16,256]{3,2,0,1:T(8,128)(2,1)} %copy.45), calls=%async_computation.1 | async-start | bytes 8388608 | tf_op jit(solution)/shard_map/all_to_all | solution.py:99
  58.4 6.4 %convert_element_type.136 = f32[2,8,512,256]{3,2,1,0:T(8,128)} convert(bf16[2,8,512,256]{3,2,1,0:T(8,128)(2,1)} %param.11) | non-fusion elementwise | flops 2097152 | bytes 12582912 | tf_op jit(solution)/shard_map/convert_element_type | solution.py:60
  64.8 4.0 %fusion.51 = bf16[1,512,512]{1,2,0:T(8,128)(2,1)S(1)} fusion(), kind=kLoop, calls=%fused_computation.74 | loop fusion | flops 3932160 | bytes 524288 | tf_op jit(solution)/shard_map/convert.24
  68.8 4.3 %negate_convert_fusion = (bf16[1,512,512]{1,2,0:T(8,128)(2,1)S(1)}, bf16[1,512,512]{1,2,0:T(8,128)(2,1)S(1)}) fusion(), kind=kLoop, calls=%fused_computation.67 | loop fusion | flops 4456448 | bytes 1048576 | tf_op jit(solution)/shard_map/convert.20
  73.1 1.6 fusion.36
  74.8 0.2 fusion.78
  74.9 78.1 %all-to-all-done.1 = bf16[2,256,16,256]{3,2,0,1:T(8,128)(2,1)} async-done(((bf16[2,256,16,256]{3,2,0,1:T(8,128)(2,1)}), bf16[2,256,16,256]{3,2,0,1:T(8,128)(2,1)}, u32[]{:S(2)}, u32[]{:S(2)}) %all-to-all-start.1) | async-done | bytes 4194336 | tf_op jit(solution)/shard_map/all_to_all | solution.py:99
  153.0 0.0 copy-start.2
  153.0 0.0 copy-start.3
  153.0 0.0 slice-start
  153.0 2.8 copy.46
  155.8 0.0 copy-done.2
  155.8 0.0 copy-done.3
  155.8 0.0 slice-start.1
  155.8 4.5 %convolution_bitcast_fusion = f32[2,8,512,256]{3,2,1,0:T(8,128)S(1)} fusion(bf16[2,8,512,256,1]{3,2,0,1,4:T(8,128)(2,1)S(1)} %bitcast.158, bf16[1,2,512,512]{2,3,0,1:T(8,128)(2,1)S(1)} %copy-done.2, bf16[1,2,512,512]{2,3,0,1:T(8,128)(2,1)S(1)} %copy-done.3), kind=kOutput, calls=%fused_computation.27 | convolution fusion | flops 4299161600 | bytes 14680064 | tf_op jit(solution)/shard_map/kcbh,kjbd->jcdh/dot_general | solution.py:59
  160.3 0.0 slice-done
  160.3 0.0 slice-done.1
  160.4 1.7 subtract_convert_fusion.1
  162.1 4.5 %fusion.17 = f32[2,8,512,256]{3,2,1,0:T(8,128)S(1)} fusion(bf16[1,8,512,256]{3,2,1,0:T(8,128)(2,1)S(1)} %get-tuple-element.8, bf16[1,8,512,256]{3,2,1,0:T(8,128)(2,1)S(1)} %get-tuple-element.7, bf16[1,2,512,512]{2,3,1,0:T(8,128)(2,1)S(1)} %get-tuple-element.18, bf16[1,2,512,512]{2,3,1,0:T(8,128)(2,1)S(1)} %get-tuple-element.13), kind=kOutput, calls=%fused_computation.28 | convolution fusion | flops 4298113024 | bytes 14680064 | tf_op jit(solution)/shard_map/kcdh,kjdb->jcbh/dot_general | solution.py:64
  166.6 1.7 subtract_convert_fusion
  168.2 0.4 pad_maximum_fusion.2
  168.6 2.4 copy.49
  171.0 105.9 %all_to_all.78 = bf16[2,8,512,256]{3,1,0,2:T(8,128)(2,1)S(1)} all-to-all(bf16[2,8,512,256]{3,1,0,2:T(8,128)(2,1)S(1)} %copy.49), channel_id=1, replica_groups=mesh['seq'=32,'chan'=8] {'seq'}, dimensions={2} | all-to-all | bytes 8388608 | tf_op jit(solution)/shard_map/all_to_all | solution.py:103
  276.9 0.8 fusion.30
  277.7 0.0 copy-start.1
  277.7 0.0 copy-start.4
  277.7 0.6 copy.52
  278.3 33.8 %all_to_all.79 = bf16[128,16,256]{2,1,0:T(8,128)(2,1)S(1)} all-to-all(bf16[128,16,256]{2,1,0:T(8,128)(2,1)S(1)} %copy.52), channel_id=1, replica_groups=mesh['seq'=32,'chan'=8] {'seq'}, dimensions={0} | all-to-all | bytes 2097152 | tf_op jit(solution)/shard_map/all_to_all | solution.py:105
  312.0 0.3 copy.53
  312.3 0.0 copy-done.1
  312.3 0.0 copy-done.4
  312.3 0.0 copy-start.7
  312.4 0.4 fusion.24
  312.8 19.1 %psum.7 = f32[2048]{0:T(1024)S(1)} all-reduce(f32[2048]{0:T(1024)S(1)} %get-tuple-element.5), channel_id=1, replica_groups=mesh['seq'=32,'chan'=8] {'chan'}, use_global_device_ids=true, to_apply=%region_1.2 | all-reduce | flops 2048 | bytes 16384 | tf_op jit(solution)/shard_map/psum | solution.py:112
  331.9 0.0 copy-done.6
  331.9 0.0 copy-done.9
  331.9 1.6 convolution_convert_fusion.1
  333.5 3.6 all-to-all-start.4
  337.1 0.0 copy-done.7
  337.1 1.6 convolution_convert_fusion
  338.8 10.1 %all-to-all-done.4 = bf16[8,1,32,2048]{3,2,1,0:T(8,128)(2,1)S(1)} async-done(((bf16[8,1,32,2048]{3,2,1,0:T(8,128)(2,1)}), bf16[8,1,32,2048]{3,2,1,0:T(8,128)(2,1)S(1)}, u32[]{:S(2)}, u32[]{:S(2)}) %all-to-all-start.4) | async-done | bytes 1048608 | tf_op jit(solution)/shard_map/all_to_all | solution.py:129
  348.9 4.5 %all-to-all-start.5 = ((bf16[8,1,32,2048]{3,2,1,0:T(8,128)(2,1)}), bf16[8,1,32,2048]{3,2,1,0:T(8,128)(2,1)}, u32[]{:S(2)}, u32[]{:S(2)}) async-start(bf16[8,1,32,2048]{3,2,1,0:T(8,128)(2,1)} %bitcast.161), calls=%async_computation.5 | async-start | bytes 2097152 | tf_op jit(solution)/shard_map/all_to_all | solution.py:130
  353.4 0.0 copy-done
  353.4 0.0 copy-start.5
  353.4 4.6 %fusion.44 = f32[2048,1024,1]{1,0,2:T(8,128)} fusion(bf16[8,32,1024]{2,1,0:T(8,128)(2,1)S(1)} %bitcast.153, bf16[8,1,32,2048]{3,2,1,0:T(8,128)(2,1)S(1)} %all-to-all-done.4), kind=kOutput, calls=%fused_computation.65 | convolution fusion | flops 1073741824 | bytes 9961472 | tf_op jit(solution)/shard_map/ijmt,jimh->tjh/dot_general | solution.py:134
  357.9 7.2 %all-to-all-done.5 = bf16[8,1,32,2048]{3,2,1,0:T(8,128)(2,1)} async-done(((bf16[8,1,32,2048]{3,2,1,0:T(8,128)(2,1)}), bf16[8,1,32,2048]{3,2,1,0:T(8,128)(2,1)}, u32[]{:S(2)}, u32[]{:S(2)}) %all-to-all-start.5) | async-done | bytes 1048608 | tf_op jit(solution)/shard_map/all_to_all | solution.py:130
  365.2 0.0 copy-done.5
  365.2 7.7 %fusion.20 = bf16[2048,256]{0,1:T(8,128)(2,1)S(1)} fusion(f32[2048,1024,1]{1,0,2:T(8,128)} %fusion.44, bf16[8,32,1024]{2,1,0:T(8,128)(2,1)S(1)} %bitcast.164, bf16[8,1,32,2048]{3,2,1,0:T(8,128)(2,1)} %all-to-all-done.5, bf16[1,1024,256]{2,1,0:T(8,128)(2,1)} %param.18), kind=kOutput, calls=%fused_computation.33 | convolution fusion | flops 2168979456 | bytes 11534336 | tf_op jit(solution)/shard_map/tjh,jhq->jqt/dot_general | solution.py:137
  372.8 17.0 %all_to_all.80 = bf16[8,1,32,2048]{3,2,1,0:T(8,128)(2,1)S(1)} all-to-all(bf16[8,1,32,2048]{3,2,1,0:T(8,128)(2,1)S(1)} %bitcast.163), channel_id=1, replica_groups=mesh['seq'=32,'chan'=8] {'chan'}, dimensions={0} | all-to-all | bytes 2097152 | tf_op jit(solution)/shard_map/all_to_all | solution.py:140
  389.8 0.0 copy-done.8
  389.8 1.5 fusion.23
  (7 shorter events, 0.0 us)
Async XLA Ops:
  0.0 353.4 %copy-start = (bf16[1,256,1024]{2,1,0:T(8,128)(2,1)S(1)}, bf16[1,256,1024]{2,1,0:T(8,128)(2,1)}, u32[]{:S(2)}) copy-start(bf16[1,256,1024]{2,1,0:T(8,128)(2,1)} %param.16) | copy-start | bytes 1572868
  3.1 41.9 %all-to-all-start = ((bf16[4,512,256]{2,0,1:T(4,128)(2,1)}), bf16[4,512,256]{2,0,1:T(4,128)(2,1)S(1)}, u32[]{:S(2)}, u32[]{:S(2)}) async-start(bf16[4,512,256]{2,0,1:T(4,128)(2,1)} %copy.42), calls=%async_computation | async-start | bytes 2097152 | tf_op jit(solution)/shard_map/all_to_all | solution.py:97
  53.6 99.4 %all-to-all-start.1 = ((bf16[2,256,16,256]{3,2,0,1:T(8,128)(2,1)}), bf16[2,256,16,256]{3,2,0,1:T(8,128)(2,1)}, u32[]{:S(2)}, u32[]{:S(2)}) async-start(bf16[2,256,16,256]{3,2,0,1:T(8,128)(2,1)} %copy.45), calls=%async_computation.1 | async-start | bytes 8388608 | tf_op jit(solution)/shard_map/all_to_all | solution.py:99
  153.0 2.8 copy-start.2
  153.0 2.8 copy-start.3
  153.0 7.3 %slice-start = ((s8[8388608]{0:T(1024)(128)(4,1)}), s8[4194304]{0:T(1024)(128)(4,1)S(1)}, s32[]{:S(2)}) async-start(s8[8388608]{0:T(1024)(128)(4,1)} %bitcast.154), calls=%async_computation.7 | async-start | bytes 8388608
  155.8 4.5 %slice-start.1 = ((s8[8388608]{0:T(1024)(128)(4,1)}), s8[4194304]{0:T(1024)(128)(4,1)S(1)}, s32[]{:S(2)}) async-start(s8[8388608]{0:T(1024)(128)(4,1)} %bitcast.154), calls=%async_computation.8 | async-start | bytes 8388608
  277.7 34.7 %copy-start.1 = (bf16[2048,256]{1,0:T(8,128)(2,1)S(1)}, bf16[2048,256]{1,0:T(8,128)(2,1)}, u32[]{:S(2)}) copy-start(bf16[2048,256]{1,0:T(8,128)(2,1)} %param.10) | copy-start | bytes 3145732
  277.7 34.7 %copy-start.4 = (f32[256]{0:T(256)S(1)}, f32[256]{0:T(256)}, u32[]{:S(2)}) copy-start(f32[256]{0:T(256)} %param.12) | copy-start | bytes 3076
  312.0 19.9 %copy-start.6 = (bf16[1,256,256]{2,1,0:T(8,128)(2,1)S(1)}, bf16[1,256,256]{2,1,0:T(8,128)(2,1)}, u32[]{:S(2)}) copy-start(bf16[1,256,256]{2,1,0:T(8,128)(2,1)} %param.14) | copy-start | bytes 393220
  312.0 19.9 %copy-start.9 = (f32[256]{0:T(256)S(1)}, f32[256]{0:T(256)}, u32[]{:S(2)}) copy-start(f32[256]{0:T(256)} %param.13) | copy-start | bytes 3076
  312.3 24.8 %copy-start.7 = (bf16[1,256,256]{2,1,0:T(8,128)(2,1)S(1)}, bf16[1,256,256]{2,1,0:T(8,128)(2,1)}, u32[]{:S(2)}) copy-start(bf16[1,256,256]{2,1,0:T(8,128)(2,1)} %param.15) | copy-start | bytes 393220
  333.5 15.3 %all-to-all-start.4 = ((bf16[8,1,32,2048]{3,2,1,0:T(8,128)(2,1)}), bf16[8,1,32,2048]{3,2,1,0:T(8,128)(2,1)S(1)}, u32[]{:S(2)}, u32[]{:S(2)}) async-start(bf16[8,1,32,2048]{3,2,1,0:T(8,128)(2,1)} %bitcast.162), calls=%async_computation.4 | async-start | bytes 2097152 | tf_op jit(solution)/shard_map/all_to_all | solution.py:129
  348.9 16.3 %all-to-all-start.5 = ((bf16[8,1,32,2048]{3,2,1,0:T(8,128)(2,1)}), bf16[8,1,32,2048]{3,2,1,0:T(8,128)(2,1)}, u32[]{:S(2)}, u32[]{:S(2)}) async-start(bf16[8,1,32,2048]{3,2,1,0:T(8,128)(2,1)} %bitcast.161), calls=%async_computation.5 | async-start | bytes 2097152 | tf_op jit(solution)/shard_map/all_to_all | solution.py:130
  353.4 11.8 %copy-start.5 = (bf16[1,256,1024]{2,1,0:T(8,128)(2,1)S(1)}, bf16[1,256,1024]{2,1,0:T(8,128)(2,1)}, u32[]{:S(2)}) copy-start(bf16[1,256,1024]{2,1,0:T(8,128)(2,1)} %param.17) | copy-start | bytes 1572868
  365.2 24.7 %copy-start.8 = (bf16[1,256,256]{2,1,0:T(8,128)(2,1)S(1)}, bf16[1,256,256]{2,1,0:T(8,128)(2,1)}, u32[]{:S(2)}) copy-start(bf16[1,256,256]{2,1,0:T(8,128)(2,1)} %param.19) | copy-start | bytes 393220
where the time goes:
time: 392 us; the launch traced here: 391 us
  blocking collectives  176 us (45%)
  waiting for transfers between devices  125 us (32%)
  matrix products  27.9 us (7%)
  starting transfers between devices  24.2 us (6%)
  other arithmetic  23.2 us (6%)
  local copies, waits for them, and re-layouts  14.8 us (4%)
    all_to_all x1, blocking collectives, per_device(): lax.all_to_all(mixed, 'seq', split_axis=2, concat_axis=1, tiled=True)  106 us
    all_to_all x1, waiting for transfers between devices, per_device(): split = lax.all_to_all(freq, 'seq', split_axis=1, concat_axis=2, tiled=True)  78.1 us
    all_to_all x1, blocking collectives, per_device(): lax.all_to_all(conv_cols, 'seq', split_axis=0, concat_axis=1, tiled=True)  33.8 us
    all_to_all x1, waiting for transfers between devices, per_device(): lax.all_to_all(grid, 'seq', split_axis=1, concat_axis=0, tiled=True)  29.8 us
    psum x1, blocking collectives, per_device(): squares = lax.psum(jnp.sum(stream_f * stream_f, axis=1), 'chan')  19.1 us
    all_to_all x1, blocking collectives, per_device(): lax.all_to_all(permuted(down_mid), 'chan', split_axis=0, concat_axis=0, t...  17 us
    another operation x6, other arithmetic  13.6 us
    all_to_all x1, starting transfers between devices, per_device(): lax.all_to_all(grid, 'seq', split_axis=1, concat_axis=0, tiled=True)  11.4 us
  transfers between devices with their start and end apart: 4, of which 4 were waited for; matrix products, arithmetic and copies ran while one was open for 6% of the time, Pallas kernels for 0%

commit v1 on v0

v1 whole, which is shorter than its diff:
```python
import functools

import jax
import jax.numpy as jnp
import ml_dtypes
import numpy as np
from jax import lax
from jax.experimental import pallas as pl
from jax.experimental.pallas import tpu as pltpu
from jax.sharding import PartitionSpec as P

D = 2048
COLS = 512
AROWS = 256
SPAN = 131072
SEQ = 32
CHAN = 8
OWN = 8
WIDTH = 256
PB = 256
HB = 1024
PIECE = 32
ROWS_DEV = 4
S_ROWS = 128
X_ROWS = 32
F32 = jnp.float32
BF16 = jnp.bfloat16
VMEM_LIMIT = 56 * 1024 * 1024


def bf16(values):
    return np.asarray(values, np.float64).astype(np.float32).astype(ml_dtypes.bfloat16)


def angle(product, period):
    return 2.0 * np.pi / period * (product % period)


@functools.lru_cache(None)
def tables():
    cols = np.arange(COLS)
    perm_cols = (cols % 128) * 4 + cols // 128
    perm = np.zeros((COLS, COLS))
    perm[cols, perm_cols] = 1.0
    c = np.arange(AROWS)
    rows = angle(c[:, None] * np.arange(AROWS // 2)[None, :], AROWS)
    row_fwd = np.concatenate([np.cos(rows), -np.sin(rows)], 0)
    row_inv = row_fwd.T
    theta = angle(c[:, None] * perm_cols[None, :], SPAN)
    fwd, inv = [], []
    for q in range(4):
        ang = angle((4 * np.arange(128) + q)[:, None] * np.arange(128)[None, :], COLS)
        co, si = np.cos(ang), np.sin(ang)
        fwd.append(np.block([[co, -si], [si, co]]))
        inv.append(np.block([[co.T, si.T], [-si.T, co.T]]))
    return dict(
        perm=bf16(perm),
        eye=bf16(np.eye(WIDTH)),
        row_fwd=bf16(row_fwd),
        row_inv=bf16(row_inv),
        cos=np.cos(theta).astype(np.float32),
        sin=np.sin(theta).astype(np.float32),
        fwd=bf16(np.stack(fwd)),
        inv=bf16(np.stack(inv)),
    )


def dot(a, b):
    return jnp.dot(a, b, preferred_element_type=F32)


def dot_nt(a, b):
    return lax.dot_general(a, b, (((1,), (1,)), ((), ())), preferred_element_type=F32)


def params():
    return pltpu.CompilerParams(vmem_limit_bytes=VMEM_LIMIT)


def pack_kernel(tok_ref, spec_ref, eye_ref, perm_ref, msg_ref, xt_ref):
    step = pl.program_id(0)
    eye = eye_ref[...]

    def turned(tile):
        return dot_nt(eye, tile).reshape(SEQ, OWN, COLS)

    @pl.when(step < 8)
    def _():
        msg_ref[...] = jnp.concatenate([turned(spec_ref[0]), turned(spec_ref[1])], 1).astype(BF16)

    @pl.when(step >= 8)
    def _():
        perm = perm_ref[...]
        first = dot(perm, tok_ref[0]).astype(BF16)
        second = dot(perm, tok_ref[1]).astype(BF16)
        both = jnp.concatenate([turned(first), turned(second)], 1).astype(BF16)
        msg_ref[...] = both
        xt_ref[...] = both


def pack(tokens, spectrum, tb):
    tok = tokens.reshape(ROWS_DEV, COLS, WIDTH)
    spec = spectrum.reshape(16, COLS, WIDTH)
    return pl.pallas_call(
        pack_kernel,
        grid=(10,),
        in_specs=[
            pl.BlockSpec((2, COLS, WIDTH), lambda g: (jnp.maximum(g - 8, 0), 0, 0)),
            pl.BlockSpec((2, COLS, WIDTH), lambda g: (jnp.minimum(g, 7), 0, 0)),
            pl.BlockSpec((WIDTH, WIDTH), lambda g: (0, 0)),
            pl.BlockSpec((COLS, COLS), lambda g: (0, 0)),
        ],
        out_specs=[
            pl.BlockSpec((SEQ, 16, COLS), lambda g: (0, g, 0)),
            pl.BlockSpec((SEQ, 16, COLS), lambda g: (0, jnp.maximum(g - 8, 0), 0)),
        ],
        out_shape=[
            jax.ShapeDtypeStruct((SEQ, S_ROWS + X_ROWS, COLS), BF16),
            jax.ShapeDtypeStruct((SEQ, X_ROWS, COLS), BF16),
        ],
        compiler_params=params(),
        name="pack",
    )(tok, spec, tb["eye"], tb["perm"])


CH_C = 64
CH_S = 8
CH_M = CH_C * OWN


def conv_kernel(
    spec_ref, x_ref, row_fwd_ref, row_inv_ref, cos_ref, sin_ref, fwd_ref, inv_ref,
    out_ref, rows_f, y_s, x4_s, spec_f, p_s, v_s,
):
    step = pl.program_id(0)

    @pl.when(step == 0)
    def _():
        for q in range(4):
            x_q = x_ref[:, :, q * 128 : q * 128 + 128]
            rows_f[q] = x_q.reshape(AROWS // 2 * OWN, 128).astype(F32)

        @pl.loop(0, OWN)
        def _(h):
            every = pl.ds(h, AROWS // 2, stride=OWN)
            x_h = jnp.concatenate([rows_f[q, every, :] for q in range(4)], 1).astype(BF16)
            for half in range(2):
                c0 = half * 128
                f0 = dot(row_fwd_ref[pl.ds(c0, 128), :], x_h)
                f1 = dot(row_fwd_ref[pl.ds(AROWS + c0, 128), :], x_h)
                co, si = cos_ref[pl.ds(c0, 128), :], sin_ref[pl.ds(c0, 128), :]
                y0 = (f0 * co + f1 * si).astype(BF16)
                y1 = (f1 * co - f0 * si).astype(BF16)
                for q in range(4):
                    y_s[h, pl.ds(c0, 128), pl.ds(q * 256, 128)] = y0[:, q * 128 : q * 128 + 128]
                    y_s[h, pl.ds(c0, 128), pl.ds(q * 256 + 128, 128)] = y1[:, q * 128 : q * 128 + 128]

    c_start = pl.multiple_of(step * CH_C, CH_C)
    for k in range(2):
        for r in range(4):
            part = spec_ref[:, k * 64 : k * 64 + 64, r * 128 : r * 128 + 128]
            spec_f[k, r] = part.reshape(CH_M, 128).astype(F32)
    for q in range(4):
        part = y_s[:, pl.ds(c_start, CH_C), q * 256 : q * 256 + 256].reshape(CH_M, 256)
        x4_s[q] = dot(part, fwd_ref[q])

    @pl.loop(0, OWN)
    def _(h):
        for rb in range(CH_C // 16):
            r0 = pl.multiple_of(h * CH_C + rb * 16, 16)
            rows = pl.ds(r0, 16)
            srows = pl.ds(h + rb * 16 * OWN, 16, stride=OWN)
            re = [x4_s[q, rows, 0:128] for q in range(4)]
            im = [x4_s[q, rows, 128:256] for q in range(4)]
            t0r, t0i = re[0] + re[2], im[0] + im[2]
            t1r, t1i = re[0] - re[2], im[0] - im[2]
            t2r, t2i = re[1] + re[3], im[1] + im[3]
            t3r, t3i = re[1] - re[3], im[1] - im[3]
            zr = [t0r + t2r, t1r + t3i, t0r - t2r, t1r - t3i]
            zi = [t0i + t2i, t1i - t3r, t0i - t2i, t1i + t3r]
            pr, pi = [], []
            for r in range(4):
                sr = spec_f[0, r, srows, :]
                si = spec_f[1, r, srows, :]
                pr.append(zr[r] * sr - zi[r] * si)
                pi.append(zr[r] * si + zi[r] * sr)
            u0r, u0i = pr[0] + pr[2], pi[0] + pi[2]
            u1r, u1i = pr[0] - pr[2], pi[0] - pi[2]
            u2r, u2i = pr[1] + pr[3], pi[1] + pi[3]
            u3r, u3i = pr[1] - pr[3], pi[1] - pi[3]
            qr = [u0r + u2r, u1r - u3i, u0r - u2r, u1r + u3i]
            qi = [u0i + u2i, u1i + u3r, u0i - u2i, u1i - u3r]
            for q in range(4):
                p_s[rows, q * 256 : q * 256 + 128] = qr[q].astype(BF16)
                p_s[rows, q * 256 + 128 : q * 256 + 256] = qi[q].astype(BF16)

    for q in range(4):
        x4_s[q] = dot(p_s[:, q * 256 : q * 256 + 256], inv_ref[q])

    @pl.loop(0, OWN)
    def _(h):
        rows = pl.ds(pl.multiple_of(h * CH_C, CH_C), CH_C)
        crow = pl.ds(c_start, CH_C)
        for q in range(4):
            lanes = slice(q * 128, q * 128 + 128)
            co, si = cos_ref[crow, lanes], sin_ref[crow, lanes]
            q0, q1 = x4_s[q, rows, 0:128], x4_s[q, rows, 128:256]
            v_s[h, crow, lanes] = (q0 * co - q1 * si).astype(BF16)
            v_s[h, pl.ds(AROWS + c_start, CH_C), lanes] = (q1 * co + q0 * si).astype(BF16)

    @pl.when(step == pl.num_programs(0) - 1)
    def _():
        @pl.loop(0, OWN)
        def _(h):
            every = pl.ds(h, AROWS // 2, stride=OWN)
            rows = dot(row_inv_ref[...], v_s[h]) * (1.0 / SPAN)
            for q in range(4):
                rows_f[q, every, :] = rows[:, q * 128 : q * 128 + 128]

        for q in range(4):
            part = rows_f[q].astype(BF16).reshape(SEQ, X_ROWS, 128)
            out_ref[:, :, q * 128 : q * 128 + 128] = part


def convolve(msg, tb):
    whole = lambda *shape: pl.BlockSpec(shape, lambda g: (0,) * len(shape))
    return pl.pallas_call(
        conv_kernel,
        grid=(AROWS // CH_C,),
        in_specs=[
            pl.BlockSpec((CH_S, S_ROWS, COLS), lambda g: (g, 0, 0)),
            pl.BlockSpec((SEQ, X_ROWS, COLS), lambda g: (0, S_ROWS // X_ROWS, 0)),
            whole(2 * AROWS, AROWS // 2),
            whole(AROWS // 2, 2 * AROWS),
            whole(AROWS, COLS),
            whole(AROWS, COLS),
            whole(4, 256, 256),
            whole(4, 256, 256),
        ],
        out_specs=whole(SEQ, X_ROWS, COLS),
        out_shape=jax.ShapeDtypeStruct((SEQ, X_ROWS, COLS), BF16),
        scratch_shapes=[
            pltpu.VMEM((4, AROWS // 2 * OWN, 128), F32),
            pltpu.VMEM((OWN, AROWS, 2 * COLS), BF16),
            pltpu.VMEM((4, CH_M, 256), F32),
            pltpu.VMEM((2, 4, CH_M, 128), F32),
            pltpu.VMEM((CH_M, 2 * COLS), BF16),
            pltpu.VMEM((OWN, 2 * AROWS, COLS), BF16),
        ],
        compiler_params=params(),
        name="convolve",
    )(msg, msg, tb["row_fwd"], tb["row_inv"], tb["cos"], tb["sin"], tb["fwd"], tb["inv"])


G_ROWS = 4 * 2 * PIECE + 16


def first_kernel(conv_ref, xt_ref, skip_ref, gain_ref, w_ref, out_ref, stream_ref):
    skip, gain = skip_ref[...], gain_ref[...]
    w = w_ref[...]
    sums = []
    for pair in range(2):
        rows = slice(pair * 16, pair * 16 + 16)
        conv = conv_ref[:, rows, :].astype(F32)
        xt = xt_ref[:, rows, :].astype(F32)
        kept = []
        for sub in range(2):
            tc = pair * 2 + sub
            part = slice(sub * 8, sub * 8 + 8)
            stream = (conv[:, part, :] + skip * xt[:, part, :]).astype(BF16).astype(F32)
            kept.append(stream)
            sums.append(jnp.sum(jnp.sum(stream * stream, axis=0), axis=0, keepdims=True))
            scaled = (stream * gain).reshape(WIDTH, COLS).astype(BF16)
            mid = dot(w, scaled).astype(BF16)
            for j in range(CHAN):
                r0 = tc * 2 * PIECE
                out_ref[j, r0 : r0 + PIECE, :] = mid[j * PIECE : (j + 1) * PIECE]
                out_ref[j, r0 + PIECE : r0 + 2 * PIECE, :] = mid[PB + j * PIECE : PB + (j + 1) * PIECE]
        stream_ref[:, rows, :] = jnp.concatenate(kept, 1).astype(BF16)
    total = jnp.concatenate(sums, 0)
    high = total.astype(BF16).astype(F32)
    tail = jnp.concatenate([high, total - high, jnp.zeros((8, COLS), F32)], 0).astype(BF16)
    for j in range(CHAN):
        out_ref[j, 4 * 2 * PIECE :, :] = tail


def first(conv, xt, skip, gain, w):
    return pl.pallas_call(
        first_kernel,
        out_shape=[
            jax.ShapeDtypeStruct((CHAN, G_ROWS, COLS), BF16),
            jax.ShapeDtypeStruct((SEQ, X_ROWS, COLS), BF16),
        ],
        compiler_params=params(),
        name="first",
    )(conv, xt, skip, gain, w)


def second_kernel(mid_ref, sum_ref, gate_ref, up_ref, down_ref, out_ref):
    step = pl.program_id(0)
    total = jnp.sum(sum_ref[...].astype(F32), axis=0)
    pick = lax.broadcasted_iota(jnp.int32, (16, 1), 0)
    mine = jnp.logical_or(pick == step, pick == step + 4)
    total = jnp.sum(jnp.where(mine, total, 0.0), axis=0, keepdims=True)
    scale = lax.rsqrt(total * (1.0 / D) + 1e-05)
    gate_in = mid_ref[:, 0:PIECE, :].reshape(PB, COLS)
    up_in = mid_ref[:, PIECE : 2 * PIECE, :].reshape(PB, COLS)
    acc = jnp.zeros((PB, COLS), F32)
    for e in range(4):
        rows = slice(e * 256, e * 256 + 256)
        gate = dot(gate_ref[rows, :], gate_in) * scale
        upper = dot(up_ref[rows, :], up_in) * scale
        act = (jax.nn.gelu(gate, approximate=True) * upper).astype(BF16)
        acc = acc + dot(down_ref[:, rows], act)
    out_ref[...] = acc.astype(BF16).reshape(CHAN, PIECE, COLS)


def second(mid, gate_w, up_w, down_w):
    whole = lambda *shape: pl.BlockSpec(shape, lambda g: (0,) * len(shape))
    return pl.pallas_call(
        second_kernel,
        grid=(ROWS_DEV,),
        in_specs=[
            pl.BlockSpec((CHAN, 2 * PIECE, COLS), lambda g: (0, g, 0)),
            pl.BlockSpec((CHAN, 16, COLS), lambda g: (0, 4 * 2 * PIECE // 16, 0)),
            whole(HB, PB),
            whole(HB, PB),
            whole(PB, HB),
        ],
        out_specs=pl.BlockSpec((CHAN, PIECE, COLS), lambda g: (0, g, 0)),
        out_shape=jax.ShapeDtypeStruct((CHAN, ROWS_DEV * PIECE, COLS), BF16),
        compiler_params=params(),
        name="second",
    )(mid, mid, gate_w, up_w, down_w)


def last_kernel(down_ref, stream_ref, w_ref, perm_ref, out_ref):
    w, perm = w_ref[...], perm_ref[...]
    stream = stream_ref[...].astype(F32)
    for sub in range(2):
        down = down_ref[:, sub * PIECE : (sub + 1) * PIECE, :].reshape(PB, COLS)
        kept = stream[:, sub * 8 : sub * 8 + 8, :].reshape(WIDTH, COLS)
        res = (kept + dot(w, down)).astype(BF16)
        out_ref[sub * COLS : (sub + 1) * COLS, :] = dot_nt(perm, res).astype(BF16)


def last(down, stream, w, tb):
    whole = lambda *shape: pl.BlockSpec(shape, lambda g: (0,) * len(shape))
    return pl.pallas_call(
        last_kernel,
        grid=(2,),
        in_specs=[
            pl.BlockSpec((CHAN, 2 * PIECE, COLS), lambda g: (0, g, 0)),
            pl.BlockSpec((SEQ, 16, COLS), lambda g: (0, g, 0)),
            whole(PB, PB),
            whole(COLS, COLS),
        ],
        out_specs=pl.BlockSpec((2 * COLS, WIDTH), lambda g: (g, 0)),
        out_shape=jax.ShapeDtypeStruct((ROWS_DEV * COLS, WIDTH), BF16),
        compiler_params=params(),
        name="last",
    )(down, stream, w, np.ascontiguousarray(tb["perm"].T))


def exchange(value, axis):
    return lax.all_to_all(value, axis, split_axis=0, concat_axis=0, tiled=True)


def per_device(
    tokens, spectrum, skip_gain, norm_gain,
    gate_first, up_first, gate_second, up_second, down_first, down_second,
):
    tb = tables()
    msg, xt = pack(tokens, spectrum, tb)
    conv = convolve(exchange(msg, "seq"), tb)
    conv = exchange(conv, "seq")
    first_w = jnp.concatenate([gate_first[0].T, up_first[0].T], 0)
    skip = skip_gain.reshape(SEQ, OWN, 1)
    gain = norm_gain.reshape(SEQ, OWN, 1)
    mid, stream = first(conv, xt, skip, gain, first_w)
    down = second(exchange(mid, "chan"), gate_second[0].T, up_second[0].T, down_first[0].T)
    return last(exchange(down, "chan"), stream, down_second[0].T, tb)


def solution(mesh):
    in_specs = (
        P("seq", "chan"),
        P(None, "seq", None, "chan"),
        P("chan"),
        P("chan"),
        P("chan", None, None),
        P("chan", None, None),
        P("chan", None, None),
        P("chan", None, None),
        P("chan", None, None),
        P("chan", None, None),
    )
    return jax.shard_map(
        per_device, mesh=mesh, in_specs=in_specs, out_specs=P("seq", "chan"), check_vma=False
    )
```

time: 392 us -> 268 us (0.68)
  waiting for transfers between devices: 125 us -> 65.9 us
  Pallas kernels: 0 us -> 45.1 us
  blocking collectives: 176 us -> 132 us
  matrix products: 27.9 us -> 0 us
  other arithmetic: 23.2 us -> 0.74 us
  starting transfers between devices: 24.2 us -> 11.8 us
  local copies, waits for them, and re-layouts: 14.8 us -> 10.1 us
    all_to_all x4 -> x3, waiting for transfers between devices: 125 us -> 65.9 us  [exchange(): return lax.all_to_all(value, axis, split_axis=0, concat_axis=0, tiled=True)]
    pallas_call x0 -> x5, Pallas kernels: none -> 45.1 us  [the longest x1 17.9 us: convolve(): pl.pallas_call(conv_kernel, grid=(AROWS // CH_C,), in_specs=[pl.BlockSpec...]
    dot_general x9 -> x0, matrix products: 27.9 us -> none  [the longest x1 7.66 us: per_device(): jnp.einsum('tjh,jhq->jqt', act, down_first, preferred_element_type=jnp.fl...]
    all_to_all x3 -> x1, blocking collectives: 157 us -> 132 us  [exchange(): return lax.all_to_all(value, axis, split_axis=0, concat_axis=0, tiled=True)]
    psum x1 -> x0, blocking collectives: 19.1 us -> none  [per_device(): squares = lax.psum(jnp.sum(stream_f * stream_f, axis=1), 'chan')]
    another operation x9 -> x0, other arithmetic: 16 us -> none
    all_to_all x4 -> x3, starting transfers between devices: 24.2 us -> 11.8 us  [exchange(): return lax.all_to_all(value, axis, split_axis=0, concat_axis=0, tiled=True)]
    unnamed x24 -> x26, local copies, waits for them, and re-layouts: 0.06 us -> 8.34 us
  transfers between devices with their start and end apart: 4 -> 3, of which waited for: 4 -> 3; matrix products, arithmetic and copies ran while one was open for 6% -> 3% of each run, Pallas kernels for 0% -> 0%
where the time goes in v1:
time: 268 us; the launch traced here: 266 us
  blocking collectives  132 us (49%)
  waiting for transfers between devices  65.9 us (25%)
  Pallas kernels  45.1 us (17%)
  starting transfers between devices  11.8 us (4%)
  local copies, waits for them, and re-layouts  10.1 us (4%)
    all_to_all x1, blocking collectives, exchange(): return lax.all_to_all(value, axis, split_axis=0, concat_axis=0, tiled=True)  132 us
    all_to_all x3, waiting for transfers between devices, exchange(): return lax.all_to_all(value, axis, split_axis=0, concat_axis=0, tiled=True)  65.9 us
    pallas_call x1, Pallas kernels, convolve(): pl.pallas_call(conv_kernel, grid=(AROWS // CH_C,), in_specs=[pl.BlockSpec...  17.9 us
    all_to_all x3, starting transfers between devices, exchange(): return lax.all_to_all(value, axis, split_axis=0, concat_axis=0, tiled=True)  11.8 us
    pallas_call x1, Pallas kernels, pack(): pl.pallas_call(pack_kernel, grid=(10,), in_specs=[pl.BlockSpec((2, COLS,...  10.2 us
    pallas_call x1, Pallas kernels, second(): pl.pallas_call(second_kernel, grid=(ROWS_DEV,), in_specs=[pl.BlockSpec((C...  9.29 us
    unnamed x26, local copies, waits for them, and re-layouts  8.34 us
  transfers between devices with their start and end apart: 3, of which 3 were waited for; matrix products, arithmetic and copies ran while one was open for 3% of the time, Pallas kernels for 0%

profile of v1, /device:TPU:32, one launch (start us, length us, event | category | flops | bytes accessed | tf_op | source)
XLA Modules:
  0.0 265.6 jit_solution(9995574767538693471)
XLA Ops:
  0.0 10.2 %pack.1 = (bf16[32,160,512]{2,1,0:T(8,128)(2,1)}, bf16[32,32,512]{2,1,0:T(8,128)(2,1)}) custom-call(bf16[4,512,256]{2,1,0:T(8,128)(2,1)} %bitcast.24, bf16[16,512,256]{2,1,0:T(8,128)(2,1)} %bitcast.20, bf16[256,256]{1,0:T(8,128)(2,1)} %constant.18.clone.eye_ref, bf16[512,512]{1,0:T(8,128)(2,1)} %constant.19.clone.perm_ref), custom_call_target="tpu_custom_call" | custom-call | tf_op jit(solution)/shard_map/pack/pallas_call | solution.py:104
  10.2 131.8 %all_to_all.20.spec_ref.x_ref = bf16[32,160,512]{2,1,0:T(8,128)(2,1)} all-to-all(bf16[32,160,512]{2,1,0:T(8,128)(2,1)} %get-tuple-element.9), channel_id=1, replica_groups=mesh['seq'=32,'chan'=8] {'seq'}, dimensions={0} | all-to-all | bytes 10485760 | tf_op jit(solution)/shard_map/all_to_all | solution.py:366
  142.0 0.0 copy-start.5
  142.0 0.0 copy-start.6
  142.0 0.0 copy-start.8
  142.0 0.0 copy-start.9
  142.0 17.9 %convolve.1 = bf16[32,32,512]{2,1,0:T(8,128)(2,1)} custom-call(bf16[32,160,512]{2,1,0:T(8,128)(2,1)} %all_to_all.20.spec_ref.x_ref, bf16[32,160,512]{2,1,0:T(8,128)(2,1)} %all_to_all.20.spec_ref.x_ref, bf16[512,128]{1,0:T(8,128)(2,1)} %constant.20.clone.row_fwd_ref, bf16[128,512]{1,0:T(8,128)(2,1)} %constant.21.clone.row_inv_ref, ...), custom_call_target="tpu_custom_call" | custom-call | tf_op jit(solution)/shard_map/convolve/pallas_call | solution.py:227
  160.0 3.7 %all-to-all-start.1 = ((bf16[32,32,512]{2,1,0:T(8,128)(2,1)}), bf16[32,32,512]{2,1,0:T(8,128)(2,1)S(1)}, u32[]{:S(2)}, u32[]{:S(2)}) async-start(bf16[32,32,512]{2,1,0:T(8,128)(2,1)} %convolve.1), calls=%async_computation.1 | async-start | bytes 2097152 | tf_op jit(solution)/shard_map/all_to_all | solution.py:366
  163.7 0.0 copy-done.5
  163.7 0.0 copy-start.3
  163.7 0.1 copy.26
  163.8 0.0 copy-done.6
  163.8 0.1 copy.27
  163.9 0.0 copy-done.8
  163.9 0.9 reshape.16.skip_ref
  164.8 0.0 copy-done.9
  164.8 0.9 reshape.17.gain_ref
  165.7 0.7 pad_maximum_fusion.w_ref
  166.4 0.0 copy-start.4
  166.4 27.5 %all-to-all-done.1.conv_ref = bf16[32,32,512]{2,1,0:T(8,128)(2,1)S(1)} async-done(((bf16[32,32,512]{2,1,0:T(8,128)(2,1)}), bf16[32,32,512]{2,1,0:T(8,128)(2,1)S(1)}, u32[]{:S(2)}, u32[]{:S(2)}) %all-to-all-start.1) | async-done | bytes 1048608 | tf_op jit(solution)/shard_map/all_to_all | solution.py:366
  193.9 0.0 copy-start.1
  193.9 1.0 copy-done.1
  194.9 4.2 %first.1 = (bf16[8,272,512]{2,1,0:T(8,128)(2,1)}, bf16[32,32,512]{2,1,0:T(8,128)(2,1)}) custom-call(bf16[32,32,512]{2,1,0:T(8,128)(2,1)} %copy-done.1, bf16[32,32,512]{2,1,0:T(8,128)(2,1)} %get-tuple-element.10.xt_ref, f32[32,8,1]{2,1,0:T(8,128)} %reshape.16.skip_ref, f32[32,8,1]{2,1,0:T(8,128)} %reshape.17.gain_ref, bf16[512,256]{1,0:T(8,128)(2,1)} %pad_maximum_fusion.w_ref), custom_call_target="tpu_custom_call" | custom-call | tf_op jit(solution)/shard_map/first/pallas_call | solution.py:288
  199.1 4.4 %all-to-all-start.2 = ((bf16[8,272,512]{2,1,0:T(8,128)(2,1)}), bf16[8,272,512]{2,1,0:T(8,128)(2,1)S(1)}, u32[]{:S(2)}, u32[]{:S(2)}) async-start(bf16[8,272,512]{2,1,0:T(8,128)(2,1)} %get-tuple-element.11), calls=%async_computation.2 | async-start | bytes 4456448 | tf_op jit(solution)/shard_map/all_to_all | solution.py:366
  203.5 0.0 copy-done.3
  203.5 1.0 copy.32
  204.5 0.0 copy-done.4
  204.5 1.0 copy.30
  205.5 2.0 copy.31
  207.5 23.6 %all-to-all-done.2.mid_ref.sum_ref = bf16[8,272,512]{2,1,0:T(8,128)(2,1)S(1)} async-done(((bf16[8,272,512]{2,1,0:T(8,128)(2,1)}), bf16[8,272,512]{2,1,0:T(8,128)(2,1)S(1)}, u32[]{:S(2)}, u32[]{:S(2)}) %all-to-all-start.2) | async-done | bytes 2228256 | tf_op jit(solution)/shard_map/all_to_all | solution.py:366
  231.1 0.0 copy-start
  231.1 1.4 copy-done
  232.5 0.0 copy-start.7
  232.5 9.3 %second.1 = bf16[8,128,512]{2,1,0:T(8,128)(2,1)} custom-call(bf16[8,272,512]{2,1,0:T(8,128)(2,1)} %copy-done, bf16[8,272,512]{2,1,0:T(8,128)(2,1)} %copy-done, bf16[1024,256]{1,0:T(8,128)(2,1)} %bitcast.22, bf16[1024,256]{1,0:T(8,128)(2,1)} %bitcast.23, bf16[256,1024]{1,0:T(8,128)(2,1)} %bitcast.21), custom_call_target="tpu_custom_call" | custom-call | tf_op jit(solution)/shard_map/second/pallas_call | solution.py:320
  241.8 3.7 %all-to-all-start.3 = ((bf16[8,128,512]{2,1,0:T(8,128)(2,1)}), bf16[8,128,512]{2,1,0:T(8,128)(2,1)S(1)}, u32[]{:S(2)}, u32[]{:S(2)}) async-start(bf16[8,128,512]{2,1,0:T(8,128)(2,1)} %second.1), calls=%async_computation.3 | async-start | bytes 2097152 | tf_op jit(solution)/shard_map/all_to_all | solution.py:366
  245.5 0.0 copy-done.7
  245.5 0.8 copy.33
  246.2 14.9 %all-to-all-done.3.down_ref = bf16[8,128,512]{2,1,0:T(8,128)(2,1)S(1)} async-done(((bf16[8,128,512]{2,1,0:T(8,128)(2,1)}), bf16[8,128,512]{2,1,0:T(8,128)(2,1)S(1)}, u32[]{:S(2)}, u32[]{:S(2)}) %all-to-all-start.3) | async-done | bytes 1048608 | tf_op jit(solution)/shard_map/all_to_all | solution.py:366
  261.1 0.0 copy-start.2
  261.1 1.0 copy-done.2
  262.1 3.5 %last.1 = bf16[2048,256]{1,0:T(8,128)(2,1)} custom-call(bf16[8,128,512]{2,1,0:T(8,128)(2,1)} %copy-done.2, bf16[32,32,512]{2,1,0:T(8,128)(2,1)} %get-tuple-element.12.stream_ref, bf16[256,256]{1,0:T(8,128)(2,1)} %bitcast.27, bf16[512,512]{1,0:T(8,128)(2,1)} %constant.26.clone.perm_ref), custom_call_target="tpu_custom_call" | custom-call | tf_op jit(solution)/shard_map/last/pallas_call | solution.py:349
Async XLA Ops:
  142.0 21.7 %copy-start.5 = (bf16[1,256,256]{2,1,0:T(8,128)(2,1)S(1)}, bf16[1,256,256]{2,1,0:T(8,128)(2,1)}, u32[]{:S(2)}) copy-start(bf16[1,256,256]{2,1,0:T(8,128)(2,1)} %param.23) | copy-start | bytes 393220
  142.0 21.8 %copy-start.6 = (bf16[1,256,256]{2,1,0:T(8,128)(2,1)S(1)}, bf16[1,256,256]{2,1,0:T(8,128)(2,1)}, u32[]{:S(2)}) copy-start(bf16[1,256,256]{2,1,0:T(8,128)(2,1)} %param.24) | copy-start | bytes 393220
  142.0 21.9 %copy-start.8 = (f32[256]{0:T(256)S(1)}, f32[256]{0:T(256)}, u32[]{:S(2)}) copy-start(f32[256]{0:T(256)} %param.21) | copy-start | bytes 3076
  142.0 22.8 %copy-start.9 = (f32[256]{0:T(256)S(1)}, f32[256]{0:T(256)}, u32[]{:S(2)}) copy-start(f32[256]{0:T(256)} %param.22) | copy-start | bytes 3076
  160.0 34.0 %all-to-all-start.1 = ((bf16[32,32,512]{2,1,0:T(8,128)(2,1)}), bf16[32,32,512]{2,1,0:T(8,128)(2,1)S(1)}, u32[]{:S(2)}, u32[]{:S(2)}) async-start(bf16[32,32,512]{2,1,0:T(8,128)(2,1)} %convolve.1), calls=%async_computation.1 | async-start | bytes 2097152 | tf_op jit(solution)/shard_map/all_to_all | solution.py:366
  163.7 39.8 %copy-start.3 = (bf16[1,1024,256]{2,1,0:T(8,128)(2,1)S(1)}, bf16[1,1024,256]{2,1,0:T(8,128)(2,1)}, u32[]{:S(2)}) copy-start(bf16[1,1024,256]{2,1,0:T(8,128)(2,1)} %param.27) | copy-start | bytes 1572868
  166.4 38.1 %copy-start.4 = (bf16[1,256,1024]{2,1,0:T(8,128)(2,1)S(1)}, bf16[1,256,1024]{2,1,0:T(8,128)(2,1)}, u32[]{:S(2)}) copy-start(bf16[1,256,1024]{2,1,0:T(8,128)(2,1)} %param.25) | copy-start | bytes 1572868
  193.9 1.0 copy-start.1
  199.1 32.0 %all-to-all-start.2 = ((bf16[8,272,512]{2,1,0:T(8,128)(2,1)}), bf16[8,272,512]{2,1,0:T(8,128)(2,1)S(1)}, u32[]{:S(2)}, u32[]{:S(2)}) async-start(bf16[8,272,512]{2,1,0:T(8,128)(2,1)} %get-tuple-element.11), calls=%async_computation.2 | async-start | bytes 4456448 | tf_op jit(solution)/shard_map/all_to_all | solution.py:366
  231.1 1.4 copy-start
  232.5 13.0 %copy-start.7 = (bf16[1,256,256]{2,1,0:T(8,128)(2,1)S(1)}, bf16[1,256,256]{2,1,0:T(8,128)(2,1)}, u32[]{:S(2)}) copy-start(bf16[1,256,256]{2,1,0:T(8,128)(2,1)} %param.28) | copy-start | bytes 393220
  241.8 19.3 %all-to-all-start.3 = ((bf16[8,128,512]{2,1,0:T(8,128)(2,1)}), bf16[8,128,512]{2,1,0:T(8,128)(2,1)S(1)}, u32[]{:S(2)}, u32[]{:S(2)}) async-start(bf16[8,128,512]{2,1,0:T(8,128)(2,1)} %second.1), calls=%async_computation.3 | async-start | bytes 2097152 | tf_op jit(solution)/shard_map/all_to_all | solution.py:366
  261.1 1.0 copy-start.2

commit v2 on v0

v2 whole, which is shorter than its diff:
```python
import functools

import jax
import jax.numpy as jnp
import ml_dtypes
import numpy as np
from jax import lax
from jax.experimental import pallas as pl
from jax.experimental.pallas import tpu as pltpu
from jax.sharding import PartitionSpec as P

D = 2048
COLS = 512
AROWS = 256
SPAN = 131072
SEQ = 32
CHAN = 8
OWN = 8
WIDTH = 256
PB = 256
HB = 1024
PIECE = 32
ROWS_DEV = 4
TOK = 256
S_ROWS = 128
X_ROWS = 32
F32 = jnp.float32
BF16 = jnp.bfloat16
VMEM_LIMIT = 56 * 1024 * 1024


def bf16(values):
    return np.asarray(values, np.float64).astype(np.float32).astype(ml_dtypes.bfloat16)


def angle(product, period):
    return 2.0 * np.pi / period * (product % period)


@functools.lru_cache(None)
def tables():
    cols = np.arange(COLS)
    perm_cols = (cols % 128) * 4 + cols // 128
    perm = np.zeros((COLS, COLS))
    perm[cols, perm_cols] = 1.0
    place = np.arange(TOK)
    token = 4 * (place % 64) + 2 * (place // 128) + place // 64 % 2
    unperm = np.zeros((TOK, TOK))
    unperm[token, place] = 1.0
    c = np.arange(AROWS)
    rows = angle(c[:, None] * np.arange(AROWS // 2)[None, :], AROWS)
    row_fwd = np.concatenate([np.cos(rows), -np.sin(rows)], 0)
    row_inv = row_fwd.T
    theta = angle(c[:, None] * perm_cols[None, :], SPAN)
    fwd, inv = [], []
    for q in range(4):
        ang = angle((4 * np.arange(128) + q)[:, None] * np.arange(128)[None, :], COLS)
        co, si = np.cos(ang), np.sin(ang)
        fwd.append(np.block([[co, -si], [si, co]]))
        inv.append(np.block([[co.T, si.T], [-si.T, co.T]]))
    return dict(
        perm=bf16(perm),
        unperm=bf16(unperm),
        row_fwd=bf16(row_fwd),
        row_inv=bf16(row_inv),
        cos=np.cos(theta).astype(np.float32),
        sin=np.sin(theta).astype(np.float32),
        fwd=bf16(np.stack(fwd)),
        inv=bf16(np.stack(inv)),
    )


def dot(a, b):
    return jnp.dot(a, b, preferred_element_type=F32)


def dot_nt(a, b):
    return lax.dot_general(a, b, (((1,), (1,)), ((), ())), preferred_element_type=F32)


def params():
    return pltpu.CompilerParams(vmem_limit_bytes=VMEM_LIMIT)


W_ROWS = 1936
PIECES = 4


def turn_weights(g1_ref, u1_ref, g2_ref, u2_ref, d1_ref, d2_ref, gain_ref, out_ref):
    tiles = [g2_ref[0, :, 0:256], g2_ref[0, :, 256:512], u2_ref[0, :, 0:256], u2_ref[0, :, 256:512]]
    tiles += [d1_ref[0, 0:256, :], d1_ref[0, 256:512, :]]
    for n, tile in enumerate(tiles):
        out_ref[n * 256 : n * 256 + 256, :] = tile.T
    for n, ref in enumerate((g1_ref, u1_ref, d2_ref)):
        r0 = 1536 + n * 128
        out_ref[r0 : r0 + 128, :] = ref[0].T
    gain = gain_ref[...]
    high = gain.astype(BF16).astype(F32)
    mid = (gain - high).astype(BF16).astype(F32)
    low = gain - high - mid
    out_ref[1920:, :] = jnp.concatenate([high, mid, low, jnp.zeros((13, PB), F32)], 0).astype(BF16)


def pack_kernel(core_ref, tok_ref, spec_ref, perm_ref, *refs):
    weight_refs, (msg_ref, w_ref, msg_s, w_s, msg_sem, w_sem) = refs[:7], refs[7:]
    step = pl.program_id(0)

    def turned(tiles):
        tiles = [tile.T.astype(F32).reshape(SEQ, OWN, COLS) for tile in tiles]
        return jnp.concatenate(tiles, 1).astype(BF16)

    def copies(at):
        rows = pl.ds(pl.multiple_of(at * 32, 32), 32)
        for n in range(PIECES):
            part = pl.ds(n * (SEQ // PIECES), SEQ // PIECES)
            yield pltpu.make_async_copy(
                msg_s.at[part, rows, :], msg_ref.at[part, rows, :], msg_sem.at[at, n]
            )

    w_copy = pltpu.make_async_copy(w_s, w_ref, w_sem)

    @pl.when(step < 4)
    def _():
        for n in range(2):
            rows = pl.ds(pl.multiple_of(step * 32 + n * 16, 16), 16)
            msg_s[:, rows, :] = turned([spec_ref[2 * n], spec_ref[2 * n + 1]])

    @pl.when(step == 4)
    def _():
        perm = perm_ref[...]
        for n in range(2):
            tiles = [dot(perm, tok_ref[2 * n + m]).astype(BF16) for m in range(2)]
            msg_s[:, S_ROWS + n * 16 : S_ROWS + n * 16 + 16, :] = turned(tiles)

    for copy in copies(step):
        copy.start()

    @pl.when(step == 1)
    def _():
        turn_weights(*weight_refs, w_s)
        w_copy.start()

    @pl.when(step == 4)
    def _():
        for at in range(5):
            for copy in copies(at):
                copy.wait()
        w_copy.wait()


def pack(tokens, spectrum, core, weights, gain, tb):
    tok = tokens.reshape(ROWS_DEV, COLS, WIDTH)
    spec = spectrum.reshape(16, COLS, WIDTH)
    whole = lambda *shape: pl.BlockSpec(shape, lambda g, core: (0,) * len(shape))
    cols = lambda n: pl.BlockSpec((1, PB, n), lambda g, core: (0, 0, core[0]))
    hbm = pl.BlockSpec(memory_space=pltpu.HBM)
    return pl.pallas_call(
        pack_kernel,
        grid_spec=pltpu.PrefetchScalarGridSpec(
            num_scalar_prefetch=1,
            grid=(5,),
            in_specs=[
                whole(ROWS_DEV, COLS, WIDTH),
                pl.BlockSpec((4, COLS, WIDTH), lambda g, core: (jnp.minimum(g, 3), 0, 0)),
                whole(COLS, COLS),
                cols(128),
                cols(128),
                cols(512),
                cols(512),
                pl.BlockSpec((1, 512, PB), lambda g, core: (0, core[0], 0)),
                cols(128),
                whole(1, WIDTH),
            ],
            out_specs=[hbm, hbm],
            scratch_shapes=[
                pltpu.VMEM((SEQ, S_ROWS + X_ROWS, COLS), BF16),
                pltpu.VMEM((W_ROWS, PB), BF16),
                pltpu.SemaphoreType.DMA((5, PIECES)),
                pltpu.SemaphoreType.DMA,
            ],
        ),
        out_shape=[
            jax.ShapeDtypeStruct((SEQ, S_ROWS + X_ROWS, COLS), BF16),
            jax.ShapeDtypeStruct((W_ROWS, PB), BF16),
        ],
        compiler_params=params(),
        name="pack",
    )(core, tok, spec, tb["perm"], *weights, gain)


def conv_kernel(
    msg_hbm, skip_ref, row_fwd_ref, row_inv_ref, cos_ref, sin_ref, fwd_ref, inv_ref,
    out_ref, msg_ref, x_f, spec_f, conv_f, sem,
):
    def spec_copy(part):
        devs, rows = pl.ds(part * 4, 4), pl.ds(0, S_ROWS)
        return pltpu.make_async_copy(msg_hbm.at[devs, rows, :], msg_ref.at[devs, rows, :], sem.at[part])

    rows = pl.ds(S_ROWS, X_ROWS)
    x_copy = pltpu.make_async_copy(msg_hbm.at[:, rows, :], msg_ref.at[:, rows, :], sem.at[8])
    x_copy.start()
    for part in range(SEQ // 4):
        spec_copy(part).start()
    x_copy.wait()
    for q in range(4):
        x_q = msg_ref[:, S_ROWS:, q * 128 : q * 128 + 128]
        x_f[q] = x_q.reshape(AROWS // 2 * OWN, 128).astype(F32)

    @pl.loop(0, SEQ // 4)
    def _(part):
        rows = pl.ds(pl.multiple_of(part * 256, 256), 256)
        spec_copy(part).wait()
        for k in range(2):
            for r in range(4):
                lanes = slice(r * 128, r * 128 + 128)
                block = msg_ref[pl.ds(part * 4, 4), k * 64 : k * 64 + 64, lanes]
                spec_f[k, r, rows, :] = block.reshape(256, 128).astype(F32)

    @pl.loop(0, OWN, unroll=4)
    def _(h):
        every = pl.ds(h, AROWS // 2, stride=OWN)
        x_h = jnp.concatenate([x_f[q, every, :] for q in range(4)], 1).astype(BF16)
        f = dot(row_fwd_ref[...], x_h)
        blocks = [(n * 16, n * 16 + 16) for n in range(AROWS // 16)]
        sides = []
        for q in range(4):
            lanes = slice(q * 128, q * 128 + 128)
            parts = []
            for lo, hi in blocks:
                co, si = cos_ref[lo:hi, lanes], sin_ref[lo:hi, lanes]
                f0, f1 = f[lo:hi, lanes], f[AROWS + lo : AROWS + hi, lanes]
                y0, y1 = f0 * co + f1 * si, f1 * co - f0 * si
                parts.append(jnp.concatenate([y0, y1], 1).astype(BF16))
            sides.append(dot(jnp.concatenate(parts, 0), fwd_ref[q]))

        parts = [[] for _ in range(4)]
        for lo, hi in blocks:
            re = [sides[q][lo:hi, 0:128] for q in range(4)]
            im = [sides[q][lo:hi, 128:256] for q in range(4)]
            t0r, t0i = re[0] + re[2], im[0] + im[2]
            t1r, t1i = re[0] - re[2], im[0] - im[2]
            t2r, t2i = re[1] + re[3], im[1] + im[3]
            t3r, t3i = re[1] - re[3], im[1] - im[3]
            zr = [t0r + t2r, t1r + t3i, t0r - t2r, t1r - t3i]
            zi = [t0i + t2i, t1i - t3r, t0i - t2i, t1i + t3r]
            pr, pi = [], []
            srows = pl.ds(h + lo * OWN, 16, stride=OWN)
            for r in range(4):
                sr, si = spec_f[0, r, srows, :], spec_f[1, r, srows, :]
                pr.append(zr[r] * sr - zi[r] * si)
                pi.append(zr[r] * si + zi[r] * sr)
            u0r, u0i = pr[0] + pr[2], pi[0] + pi[2]
            u1r, u1i = pr[0] - pr[2], pi[0] - pi[2]
            u2r, u2i = pr[1] + pr[3], pi[1] + pi[3]
            u3r, u3i = pr[1] - pr[3], pi[1] - pi[3]
            qr = [u0r + u2r, u1r - u3i, u0r - u2r, u1r + u3i]
            qi = [u0i + u2i, u1i + u3r, u0i - u2i, u1i - u3r]
            for q in range(4):
                parts[q].append(jnp.concatenate([qr[q], qi[q]], 1).astype(BF16))

        columns = []
        for q in range(4):
            lanes = slice(q * 128, q * 128 + 128)
            back = dot(jnp.concatenate(parts[q], 0), inv_ref[q])
            v0, v1 = [], []
            for lo, hi in blocks:
                co, si = cos_ref[lo:hi, lanes], sin_ref[lo:hi, lanes]
                b0, b1 = back[lo:hi, 0:128], back[lo:hi, 128:256]
                v0.append((b0 * co - b1 * si).astype(BF16))
                v1.append((b1 * co + b0 * si).astype(BF16))
            columns.append(jnp.concatenate(v0 + v1, 0))
        conv = dot(row_inv_ref[...], jnp.concatenate(columns, 1)) * (1.0 / SPAN)
        for q in range(4):
            conv_f[q, every, :] = conv[:, q * 128 : q * 128 + 128]

    skip = skip_ref[...].reshape(1, OWN, 1)

    @pl.loop(0, 8)
    def _(part):
        a0 = pl.multiple_of(part * 16, 16)
        kept = []
        for q in range(4):
            conv = conv_f[q, pl.ds(a0 * OWN, 16 * OWN), :].astype(BF16).astype(F32)
            x_q = msg_ref[pl.ds(part * 4, 4), S_ROWS:, q * 128 : q * 128 + 128].astype(F32)
            kept.append(conv.reshape(16, OWN, 128) + skip * x_q.reshape(16, OWN, 128))
        for half in range(2):
            lanes = slice(half * 64, half * 64 + 64)
            pairs = [
                jnp.concatenate([kept[2 * n][:, :, lanes], kept[2 * n + 1][:, :, lanes]], 2)
                for n in range(2)
            ]
            out_ref[pl.ds(a0, 16), half] = jnp.concatenate(pairs, 1).astype(BF16)


def in_vmem(value):
    return pltpu.with_memory_space_constraint(value, pltpu.VMEM)


def convolve(msg, skip, tb):
    vmem = pl.BlockSpec(memory_space=pltpu.VMEM)
    return pl.pallas_call(
        conv_kernel,
        in_specs=[pl.BlockSpec(memory_space=pltpu.HBM)] + [vmem] * 7,
        out_specs=vmem,
        out_shape=jax.ShapeDtypeStruct((AROWS // 2, 2, 16, 128), BF16),
        scratch_shapes=[
            pltpu.VMEM((SEQ, S_ROWS + X_ROWS, COLS), BF16),
            pltpu.VMEM((4, AROWS // 2 * OWN, 128), F32),
            pltpu.VMEM((2, 4, AROWS * OWN, 128), F32),
            pltpu.VMEM((4, AROWS // 2 * OWN, 128), F32),
            pltpu.SemaphoreType.DMA((9,)),
        ],
        compiler_params=pltpu.CompilerParams(vmem_limit_bytes=30 * 1024 * 1024),
        name="convolve",
    )(msg, in_vmem(skip), *(in_vmem(jnp.asarray(tb[n])) for n in ("row_fwd", "row_inv", "cos", "sin", "fwd", "inv")))


def mlp_kernel(
    x_ref, w_hbm, unperm_ref, out_ref, w_ref, stream_s, gate_s, up_s, down_s, gain_s, sem,
):
    def second_copy(j):
        part = pl.ds(0, 1536)
        return pltpu.make_async_copy(w_hbm.at[j, :, part, :], w_ref.at[j, :, part, :], sem.at[j])

    part = pl.ds(1536, W_ROWS - 1536)
    first_copy = pltpu.make_async_copy(w_hbm.at[:, :, part, :], w_ref.at[:, :, part, :], sem.at[8])
    first_copy.start()
    for j in range(8):
        second_copy(j).start()

    total = jnp.zeros((1, TOK), F32)
    for i in range(8):
        rows = x_ref[:, i].astype(F32)
        rows = jnp.concatenate([rows[:, 0:8, :], rows[:, 8:16, :]], 2).reshape(WIDTH, TOK)
        stream_s[i] = rows
        total = total + jnp.sum(rows * rows, axis=0, keepdims=True)
    scale = lax.rsqrt(total * (1.0 / D) + 1e-05)
    first_copy.wait()
    parts = jnp.concatenate([w_ref[i, 0, 1920:1936, :] for i in range(8)], 1)
    gain_s[...] = lax.dot_general(
        parts, jnp.ones((16, 128), BF16), (((0,), (0,)), ((), ())), preferred_element_type=F32
    )

    @pl.loop(0, 8, unroll=8)
    def _(i):
        gain = gain_s[pl.ds(pl.multiple_of(i * WIDTH, WIDTH), WIDTH), :]
        normed = (stream_s[i] * scale * jnp.concatenate([gain, gain], 1)).astype(BF16)
        rows = pl.ds(pl.multiple_of(i * PIECE, PIECE), PIECE)
        for half in range(2):
            mid = dot(w_ref[i, half, 1536:1792, :], normed).astype(BF16)
            for n in range(4):
                gate_s[half * 4 + n, rows, :] = mid[n * PIECE : n * PIECE + PIECE]
                n1 = 128 + n * PIECE
                up_s[half * 4 + n, rows, :] = mid[n1 : n1 + PIECE]

    def block(j):
        gate_in, up_in = gate_s[j], up_s[j]
        acts, lefts = [], []
        for half in range(2):
            for n in range(2):
                r0 = n * 256
                gate = dot(w_ref[j, half, r0 : r0 + 256, :], gate_in)
                upper = dot(w_ref[j, half, 512 + r0 : 768 + r0, :], up_in)
                acts.append((jax.nn.gelu(gate, approximate=True) * upper).astype(BF16))
                lefts.append(w_ref[j, half, 1024 + r0 : 1280 + r0, :])
        mid = dot(jnp.concatenate(lefts, 1), jnp.concatenate(acts, 0)).astype(BF16)
        rows = pl.ds(pl.multiple_of(j * PIECE, PIECE), PIECE)
        for o in range(8):
            down_s[o, rows, :] = mid[o * PIECE : o * PIECE + PIECE]

    @pl.loop(0, 2)
    def _(group):
        for n in range(4):
            second_copy(group * 4 + n).wait()
        for n in range(4):
            block(group * 4 + n)

    unperm = unperm_ref[...]

    @pl.loop(0, 8, unroll=8)
    def _(o):
        down = down_s[o]
        res = jnp.concatenate([dot(w_ref[o, half, 1792:1920, :], down) for half in range(2)], 0)
        res = (stream_s[o] + res).astype(BF16)
        out_ref[o] = dot_nt(unperm, res).astype(BF16)


def in_vmem(value):
    return pltpu.with_memory_space_constraint(value, pltpu.VMEM)


def mlp(x, weights, tb):
    vmem = pl.BlockSpec(memory_space=pltpu.VMEM)
    return pl.pallas_call(
        mlp_kernel,
        in_specs=[vmem, pl.BlockSpec(memory_space=pltpu.HBM), vmem],
        out_specs=vmem,
        out_shape=jax.ShapeDtypeStruct((8, TOK, WIDTH), BF16),
        scratch_shapes=[
            pltpu.VMEM((8, 2, W_ROWS, PB), BF16),
            pltpu.VMEM((8, WIDTH, TOK), F32),
            pltpu.VMEM((8, PB, TOK), BF16),
            pltpu.VMEM((8, PB, TOK), BF16),
            pltpu.VMEM((8, PB, TOK), BF16),
            pltpu.VMEM((D, 128), F32),
            pltpu.SemaphoreType.DMA((9,)),
        ],
        compiler_params=pltpu.CompilerParams(vmem_limit_bytes=40 * 1024 * 1024),
        name="mlp",
    )(in_vmem(x), weights, in_vmem(jnp.asarray(tb["unperm"])))


def exchange(value, axis):
    return lax.all_to_all(value, axis, split_axis=0, concat_axis=0, tiled=True)


SEQ_AXES = ("chip", "core")


def per_device(
    tokens, spectrum, skip_gain, norm_gain,
    gate_first, up_first, gate_second, up_second, down_first, down_second,
):
    tb = tables()
    core = lax.axis_index("core").astype(jnp.int32).reshape(1)
    raw = (gate_first, up_first, gate_second, up_second, down_first, down_second)
    msg, weights = pack(tokens, spectrum, core, raw, norm_gain.reshape(1, WIDTH), tb)
    weights = lax.all_gather(weights, ("chan", "core"), axis=0, tiled=False)
    weights = weights.reshape(8, 2, W_ROWS, PB)
    skip = lax.dynamic_slice(skip_gain, (lax.axis_index(SEQ_AXES) * OWN,), (OWN,)).reshape(OWN, 1)
    stream = convolve(exchange(msg, SEQ_AXES), skip, tb).reshape(SEQ * CHAN, 16, 128)
    stream = exchange(stream, SEQ_AXES + ("chan",)).reshape(SEQ, CHAN, 16, 128)
    out = mlp(stream, weights, tb)
    return exchange(out, "chan").reshape(ROWS_DEV * COLS, WIDTH)


def solution(mesh):
    split = jax.sharding.Mesh(mesh.devices.reshape(SEQ // 2, 2, CHAN), ("chip", "core", "chan"))
    in_specs = (
        P(SEQ_AXES, "chan"),
        P(None, SEQ_AXES, None, "chan"),
        P("chan"),
        P("chan"),
        P("chan", None, None),
        P("chan", None, None),
        P("chan", None, None),
        P("chan", None, None),
        P("chan", None, None),
        P("chan", None, None),
    )
    return jax.shard_map(
        per_device, mesh=split, in_specs=in_specs, out_specs=P(SEQ_AXES, "chan"), check_vma=False
    )
```

time: 392 us -> 237 us (0.60)
  blocking collectives: 176 us -> 61.5 us
  Pallas kernels: 0 us -> 30 us
  matrix products: 27.9 us -> 0 us
  other arithmetic: 23.2 us -> 0 us
  local copies, waits for them, and re-layouts: 14.8 us -> 1.18 us
  between operations: 0.33 us -> 13.5 us
  starting transfers between devices: 24.2 us -> 11.6 us
  waiting for transfers between devices: 125 us -> 117 us
    all_to_all x3 -> x2, blocking collectives: 157 us -> 61.5 us  [exchange(): return lax.all_to_all(value, axis, split_axis=0, concat_axis=0, tiled=True)]
    pallas_call x0 -> x3, Pallas kernels: none -> 30 us  [the longest x1 13.6 us: convolve(): pl.pallas_call(conv_kernel, in_specs=[pl.BlockSpec(memory_space=pltpu.HBM...]
    dot_general x9 -> x0, matrix products: 27.9 us -> none  [the longest x1 7.66 us: per_device(): jnp.einsum('tjh,jhq->jqt', act, down_first, preferred_element_type=jnp.fl...]
    psum x1 -> x0, blocking collectives: 19.1 us -> none  [per_device(): squares = lax.psum(jnp.sum(stream_f * stream_f, axis=1), 'chan')]
    another operation x9 -> x0, other arithmetic: 16 us -> none
    all_to_all x4 -> x1, starting transfers between devices: 24.2 us -> 11.5 us  [exchange(): return lax.all_to_all(value, axis, split_axis=0, concat_axis=0, tiled=True)]
    all_to_all x4 -> x1, waiting for transfers between devices: 125 us -> 117 us  [exchange(): return lax.all_to_all(value, axis, split_axis=0, concat_axis=0, tiled=True)]
    another operation x2 -> x0, local copies, waits for them, and re-layouts: 6.74 us -> none  [the longest x1 4.32 us: forward_rows(): return jnp.stack([real_part, imag_part]).astype(jnp.bfloat16)]
  transfers between devices with their start and end apart: 4 -> 2, of which waited for: 4 -> 1; matrix products, arithmetic and copies ran while one was open for 6% -> 0% of each run, Pallas kernels for 0% -> 6%
where the time goes in v2:
time: 237 us; the launch traced here: 235 us
  waiting for transfers between devices  117 us (49%)
  blocking collectives  61.5 us (26%)
  Pallas kernels  30 us (13%)
  between operations  13.5 us (6%)
  starting transfers between devices  11.6 us (5%)
    all_to_all x1, waiting for transfers between devices, exchange(): return lax.all_to_all(value, axis, split_axis=0, concat_axis=0, tiled=True)  117 us
    all_to_all x2, blocking collectives, exchange(): return lax.all_to_all(value, axis, split_axis=0, concat_axis=0, tiled=True)  61.5 us
    pallas_call x1, Pallas kernels, convolve(): pl.pallas_call(conv_kernel, in_specs=[pl.BlockSpec(memory_space=pltpu.HBM...  13.6 us
    all_to_all x1, starting transfers between devices, exchange(): return lax.all_to_all(value, axis, split_axis=0, concat_axis=0, tiled=True)  11.5 us
    pallas_call x1, Pallas kernels, mlp(): pl.pallas_call(mlp_kernel, in_specs=[vmem, pl.BlockSpec(memory_space=pltp...  9.08 us
    pallas_call x1, Pallas kernels, pack(): pl.pallas_call(pack_kernel, grid_spec=pltpu.PrefetchScalarGridSpec(num_sc...  7.39 us
  transfers between devices with their start and end apart: 2, of which 1 were waited for; matrix products, arithmetic and copies ran while one was open for 0% of the time, Pallas kernels for 6%

profile of v2, /device:TPU:32, one launch (start us, length us, event | category | flops | bytes accessed | tf_op | source)
XLA Modules:
  0.0 235.3 jit_solution(16617924890843767840)
XLA Ops:
  6.5 0.0 copy-start
  6.5 0.0 all-gather.3.cloned.1.call-start
  6.5 7.4 %pack.1 = (bf16[32,160,512]{2,1,0:T(8,128)(2,1)}, bf16[1936,256]{1,0:T(8,128)(2,1)}) custom-call(s32[1]{0:T(128)} %bitcast.core_ref, bf16[4,512,256]{2,1,0:T(8,128)(2,1)} %bitcast.15, bf16[16,512,256]{2,1,0:T(8,128)(2,1)} %bitcast.13, bf16[512,512]{1,0:T(8,128)(2,1)} %constant.35.clone.perm_ref, bf16[1,256,256]{2,1,0:T(8,128)(2,1)} %refs_0_.1, ...), custom_call_target="tpu_custom_call" | custom-call | tf_op jit(solution)/shard_map/pack/pallas_call | solution.py:157
  13.9 0.0 all-gather.3.cloned.1.call-update
  14.0 0.0 copy-start.1
  14.0 0.0 copy-start.2
  14.0 0.0 copy-start.3
  14.0 0.0 copy-start.4
  14.0 0.0 copy-start.6
  14.0 0.0 copy-start.7
  14.0 11.5 %all-to-all-start = ((bf16[32,160,512]{2,1,0:T(8,128)(2,1)}), bf16[32,160,512]{2,1,0:T(8,128)(2,1)}, u32[]{:S(2)}, u32[]{:S(2)}) async-start(bf16[32,160,512]{2,1,0:T(8,128)(2,1)} %get-tuple-element.7), calls=%async_computation | async-start | bytes 10485760 | tf_op jit(solution)/shard_map/all_to_all | solution.py:414
  25.6 0.0 copy-done
  25.6 0.1 dynamic-slice_bitcast_fusion
  25.7 0.1 copy.19.skip_ref
  25.8 0.0 copy-start.5
  25.8 117.5 %all-to-all-done.msg_hbm = bf16[32,160,512]{2,1,0:T(8,128)(2,1)} async-done(((bf16[32,160,512]{2,1,0:T(8,128)(2,1)}), bf16[32,160,512]{2,1,0:T(8,128)(2,1)}, u32[]{:S(2)}, u32[]{:S(2)}) %all-to-all-start) | async-done | bytes 5242912 | tf_op jit(solution)/shard_map/all_to_all | solution.py:414
  143.2 0.0 copy-done.1
  143.3 0.0 copy-done.2
  143.3 0.0 copy-done.3
  143.3 0.0 copy-done.4
  143.3 0.0 copy-done.6
  143.3 0.0 copy-done.7
  143.3 13.6 %convolve.1 = bf16[128,2,16,128]{3,2,1,0:T(8,128)(2,1)S(1)} custom-call(bf16[32,160,512]{2,1,0:T(8,128)(2,1)} %all-to-all-done.msg_hbm, f32[8,1]{1,0:T(8,128)S(1)} %copy.19.skip_ref, bf16[512,128]{1,0:T(8,128)(2,1)S(1)} %copy-done.6, bf16[128,512]{1,0:T(8,128)(2,1)S(1)} %copy-done.7, f32[256,512]{1,0:T(8,128)S(1)} %copy-done.1, f32[256,512]{1,0:T(8,128)S(1)} %copy-done.2, ...), custom_call_target="tpu_custom_call" | custom-call | tf_op jit(solution)/shard_map/convolve/pallas_call | solution.py:301
  156.9 42.7 %all_to_all.15 = bf16[256,16,128]{2,1,0:T(8,128)(2,1)S(1)} all-to-all(bf16[256,16,128]{2,1,0:T(8,128)(2,1)S(1)} %bitcast.11), channel_id=1, replica_groups=mesh['chip'=16,'core'=2,'chan'=8] {'chip','core','chan'}, dimensions={0} | all-to-all | bytes 2097152 | tf_op jit(solution)/shard_map/all_to_all | solution.py:414
  199.5 0.0 all-gather.3.cloned.1.call-done
  199.5 0.0 copy-done.5
  199.5 9.1 %mlp.1 = bf16[8,256,256]{2,1,0:T(8,128)(2,1)S(1)} custom-call(bf16[32,8,16,128]{3,2,1,0:T(8,128)(2,1)S(1)} %bitcast.10, bf16[8,2,1936,256]{3,2,1,0:T(8,128)(2,1)} %bitcast.12, bf16[256,256]{1,0:T(8,128)(2,1)S(1)} %copy-done.5), custom_call_target="tpu_custom_call" | custom-call | tf_op jit(solution)/shard_map/mlp/pallas_call | solution.py:394
  208.6 18.8 %all_to_all.16 = bf16[8,256,256]{2,1,0:T(8,128)(2,1)S(1)} all-to-all(bf16[8,256,256]{2,1,0:T(8,128)(2,1)S(1)} %mlp.1), channel_id=1, replica_groups=mesh['chip'=16,'core'=2,'chan'=8] {'chan'}, dimensions={0} | all-to-all | bytes 2097152 | tf_op jit(solution)/shard_map/all_to_all | solution.py:414
  227.4 1.0 copy.21
Async XLA Ops:
  6.5 19.1 %copy-start = (f32[256]{0:T(256)S(1)}, f32[256]{0:T(256)}, u32[]{:S(2)}) copy-start(f32[256]{0:T(256)} %param.20) | copy-start | bytes 3076
  6.5 193.0 %all-gather.3.cloned.1.call-start = ((), (), s32[]{:S(2)}) async-start(), calls=%async_computation.3 | async-start | bytes 16850944 | tf_op jit(solution)/shard_map/all_gather | solution.py:428
  14.0 129.3 %copy-start.1 = (f32[256,512]{1,0:T(8,128)S(1)}, f32[256,512]{1,0:T(8,128)}, u32[]{:S(2)}) copy-start(f32[256,512]{1,0:T(8,128)} %constant.38.clone.cos_ref) | copy-start | bytes 1572868
  14.0 129.3 %copy-start.2 = (f32[256,512]{1,0:T(8,128)S(1)}, f32[256,512]{1,0:T(8,128)}, u32[]{:S(2)}) copy-start(f32[256,512]{1,0:T(8,128)} %constant.39.clone.sin_ref) | copy-start | bytes 1572868
  14.0 129.3 %copy-start.3 = (bf16[4,256,256]{2,1,0:T(8,128)(2,1)S(1)}, bf16[4,256,256]{2,1,0:T(8,128)(2,1)}, u32[]{:S(2)}) copy-start(bf16[4,256,256]{2,1,0:T(8,128)(2,1)} %constant.40.clone.fwd_ref) | copy-start | bytes 1572868
  14.0 129.3 %copy-start.4 = (bf16[4,256,256]{2,1,0:T(8,128)(2,1)S(1)}, bf16[4,256,256]{2,1,0:T(8,128)(2,1)}, u32[]{:S(2)}) copy-start(bf16[4,256,256]{2,1,0:T(8,128)(2,1)} %constant.41.clone.inv_ref) | copy-start | bytes 1572868
  14.0 129.3 %copy-start.6 = (bf16[512,128]{1,0:T(8,128)(2,1)S(1)}, bf16[512,128]{1,0:T(8,128)(2,1)}, u32[]{:S(2)}) copy-start(bf16[512,128]{1,0:T(8,128)(2,1)} %constant.36.clone.row_fwd_ref) | copy-start | bytes 393220
  14.0 129.3 %copy-start.7 = (bf16[128,512]{1,0:T(8,128)(2,1)S(1)}, bf16[128,512]{1,0:T(8,128)(2,1)}, u32[]{:S(2)}) copy-start(bf16[128,512]{1,0:T(8,128)(2,1)} %constant.37.clone.row_inv_ref) | copy-start | bytes 393220
  14.0 129.2 %all-to-all-start = ((bf16[32,160,512]{2,1,0:T(8,128)(2,1)}), bf16[32,160,512]{2,1,0:T(8,128)(2,1)}, u32[]{:S(2)}, u32[]{:S(2)}) async-start(bf16[32,160,512]{2,1,0:T(8,128)(2,1)} %get-tuple-element.7), calls=%async_computation | async-start | bytes 10485760 | tf_op jit(solution)/shard_map/all_to_all | solution.py:414
  25.8 173.8 %copy-start.5 = (bf16[256,256]{1,0:T(8,128)(2,1)S(1)}, bf16[256,256]{1,0:T(8,128)(2,1)}, u32[]{:S(2)}) copy-start(bf16[256,256]{1,0:T(8,128)(2,1)} %constant.42.clone.unperm_ref) | copy-start | bytes 393220
Sparse Core Ops, SparseCore 0:
  14.1 145.6 all-gather.2

commit v3 on v2

--- a/solution.py
+++ b/solution.py
@@ -315,18 +315,28 @@
     )(msg, in_vmem(skip), *(in_vmem(jnp.asarray(tb[n])) for n in ("row_fwd", "row_inv", "cos", "sin", "fwd", "inv")))
 
 
-def mlp_kernel(
-    x_ref, w_hbm, unperm_ref, out_ref, w_ref, stream_s, gate_s, up_s, down_s, gain_s, sem,
-):
-    def second_copy(j):
-        part = pl.ds(0, 1536)
-        return pltpu.make_async_copy(w_hbm.at[j, :, part, :], w_ref.at[j, :, part, :], sem.at[j])
-
-    part = pl.ds(1536, W_ROWS - 1536)
-    first_copy = pltpu.make_async_copy(w_hbm.at[:, :, part, :], w_ref.at[:, :, part, :], sem.at[8])
-    first_copy.start()
-    for j in range(8):
-        second_copy(j).start()
+def mlp_kernel(place_ref, x_ref, unperm_ref, *refs):
+    held = refs[0:4], refs[4:8]
+    out_ref, w_ref, stream_s, gate_s, up_s, down_s, gain_s, sem = refs[8:]
+    y, x, core = place_ref[0], place_ref[1], place_ref[2]
+
+    def block_of(n):
+        return lax.rem(y + lax.rem(n, 2), 2) * 4 + lax.rem(x - n // 2 + 4, 4)
+
+    def copies(part, k):
+        rows = (pl.ds(1536, W_ROWS - 1536), pl.ds(0, 1536))[part]
+        for twin in range(2):
+            half = lax.rem(core + twin, 2)
+            yield pltpu.make_async_copy(
+                held[twin][k].at[:, rows, :],
+                w_ref.at[pl.ds(2 * k, 2), half, rows, :],
+                sem.at[part, k, twin],
+            )
+
+    for part in range(2):
+        for k in range(4):
+            for copy in copies(part, k):
+                copy.start()
 
     total = jnp.zeros((1, TOK), F32)
     for i in range(8):
@@ -335,65 +345,64 @@
         stream_s[i] = rows
         total = total + jnp.sum(rows * rows, axis=0, keepdims=True)
     scale = lax.rsqrt(total * (1.0 / D) + 1e-05)
-    first_copy.wait()
-    parts = jnp.concatenate([w_ref[i, 0, 1920:1936, :] for i in range(8)], 1)
+    for k in range(4):
+        for copy in copies(0, k):
+            copy.wait()
+    parts = jnp.concatenate([w_ref[n, 0, 1920:1936, :] for n in range(8)], 1)
     gain_s[...] = lax.dot_general(
         parts, jnp.ones((16, 128), BF16), (((0,), (0,)), ((), ())), preferred_element_type=F32
     )
 
-    @pl.loop(0, 8, unroll=8)
-    def _(i):
-        gain = gain_s[pl.ds(pl.multiple_of(i * WIDTH, WIDTH), WIDTH), :]
+    for n in range(8):
+        i = block_of(n)
+        gain = gain_s[n * WIDTH : n * WIDTH + WIDTH, :]
         normed = (stream_s[i] * scale * jnp.concatenate([gain, gain], 1)).astype(BF16)
         rows = pl.ds(pl.multiple_of(i * PIECE, PIECE), PIECE)
         for half in range(2):
-            mid = dot(w_ref[i, half, 1536:1792, :], normed).astype(BF16)
-            for n in range(4):
-                gate_s[half * 4 + n, rows, :] = mid[n * PIECE : n * PIECE + PIECE]
-                n1 = 128 + n * PIECE
-                up_s[half * 4 + n, rows, :] = mid[n1 : n1 + PIECE]
-
-    def block(j):
+            mid = dot(w_ref[n, half, 1536:1792, :], normed).astype(BF16)
+            for m in range(4):
+                gate_s[half * 4 + m, rows, :] = mid[m * PIECE : m * PIECE + PIECE]
+                m1 = 128 + m * PIECE
+                up_s[half * 4 + m, rows, :] = mid[m1 : m1 + PIECE]
+
+    def block(n):
+        j = block_of(n)
         gate_in, up_in = gate_s[j], up_s[j]
         acts, lefts = [], []
         for half in range(2):
-            for n in range(2):
-                r0 = n * 256
-                gate = dot(w_ref[j, half, r0 : r0 + 256, :], gate_in)
-                upper = dot(w_ref[j, half, 512 + r0 : 768 + r0, :], up_in)
+            for m in range(2):
+                r0 = m * 256
+                gate = dot(w_ref[n, half, r0 : r0 + 256, :], gate_in)
+                upper = dot(w_ref[n, half, 512 + r0 : 768 + r0, :], up_in)
                 acts.append((jax.nn.gelu(gate, approximate=True) * upper).astype(BF16))
-                lefts.append(w_ref[j, half, 1024 + r0 : 1280 + r0, :])
+                lefts.append(w_ref[n, half, 1024 + r0 : 1280 + r0, :])
         mid = dot(jnp.concatenate(lefts, 1), jnp.concatenate(acts, 0)).astype(BF16)
         rows = pl.ds(pl.multiple_of(j * PIECE, PIECE), PIECE)
         for o in range(8):
             down_s[o, rows, :] = mid[o * PIECE : o * PIECE + PIECE]
 
-    @pl.loop(0, 2)
-    def _(group):
-        for n in range(4):
-            second_copy(group * 4 + n).wait()
+    for group in range(2):
+        for k in range(2):
+            for copy in copies(1, group * 2 + k):
+                copy.wait()
         for n in range(4):
             block(group * 4 + n)
 
     unperm = unperm_ref[...]
-
-    @pl.loop(0, 8, unroll=8)
-    def _(o):
+    for n in range(8):
+        o = block_of(n)
         down = down_s[o]
-        res = jnp.concatenate([dot(w_ref[o, half, 1792:1920, :], down) for half in range(2)], 0)
+        res = jnp.concatenate([dot(w_ref[n, half, 1792:1920, :], down) for half in range(2)], 0)
         res = (stream_s[o] + res).astype(BF16)
         out_ref[o] = dot_nt(unperm, res).astype(BF16)
 
 
-def in_vmem(value):
-    return pltpu.with_memory_space_constraint(value, pltpu.VMEM)
-
-
-def mlp(x, weights, tb):
+def mlp(place, x, held, twins, tb):
     vmem = pl.BlockSpec(memory_space=pltpu.VMEM)
+    hbm = pl.BlockSpec(memory_space=pltpu.HBM)
     return pl.pallas_call(
         mlp_kernel,
-        in_specs=[vmem, pl.BlockSpec(memory_space=pltpu.HBM), vmem],
+        in_specs=[pl.BlockSpec(memory_space=pltpu.SMEM), vmem, vmem] + [hbm] * 8,
         out_specs=vmem,
         out_shape=jax.ShapeDtypeStruct((8, TOK, WIDTH), BF16),
         scratch_shapes=[
@@ -403,11 +412,11 @@
             pltpu.VMEM((8, PB, TOK), BF16),
             pltpu.VMEM((8, PB, TOK), BF16),
             pltpu.VMEM((D, 128), F32),
-            pltpu.SemaphoreType.DMA((9,)),
+            pltpu.SemaphoreType.DMA((2, 4, 2)),
         ],
         compiler_params=pltpu.CompilerParams(vmem_limit_bytes=40 * 1024 * 1024),
         name="mlp",
-    )(in_vmem(x), weights, in_vmem(jnp.asarray(tb["unperm"])))
+    )(place, in_vmem(x), in_vmem(jnp.asarray(tb["unperm"])), *held, *twins)
 
 
 def exchange(value, axis):
@@ -425,12 +434,18 @@
     core = lax.axis_index("core").astype(jnp.int32).reshape(1)
     raw = (gate_first, up_first, gate_second, up_second, down_first, down_second)
     msg, weights = pack(tokens, spectrum, core, raw, norm_gain.reshape(1, WIDTH), tb)
-    weights = lax.all_gather(weights, ("chan", "core"), axis=0, tiled=False)
-    weights = weights.reshape(8, 2, W_ROWS, PB)
+    other = lax.ppermute(weights, "chan", [(n, n ^ 4) for n in range(CHAN)])
+    pair = jnp.stack([weights, other])
+    held = [pair]
+    for k in range(1, 4):
+        held.append(lax.ppermute(pair, "chan", [(n, n // 4 * 4 + (n + k) % 4) for n in range(CHAN)]))
+    twins = [lax.ppermute(part, "core", [(0, 1), (1, 0)]) for part in held]
     skip = lax.dynamic_slice(skip_gain, (lax.axis_index(SEQ_AXES) * OWN,), (OWN,)).reshape(OWN, 1)
     stream = convolve(exchange(msg, SEQ_AXES), skip, tb).reshape(SEQ * CHAN, 16, 128)
     stream = exchange(stream, SEQ_AXES + ("chan",)).reshape(SEQ, CHAN, 16, 128)
-    out = mlp(stream, weights, tb)
+    chan = lax.axis_index("chan")
+    place = jnp.stack([chan // 4, chan % 4, lax.axis_index("core")]).astype(jnp.int32)
+    out = mlp(place, stream, held, twins, tb)
     return exchange(out, "chan").reshape(ROWS_DEV * COLS, WIDTH)
 
 

time: 237 us -> 228 us (0.962)
  blocking collectives: 61.5 us -> 18.8 us
  waiting for transfers between devices: 117 us -> 140 us
  starting transfers between devices: 11.6 us -> 30 us
  between operations: 13.5 us -> 0.11 us
    ppermute x0 -> x8, waiting for transfers between devices: none -> 65.6 us  [the longest x1 53.9 us: per_device(): other = lax.ppermute(weights, 'chan', [(n, n ^ 4) for n in range(CHAN)])]
    all_to_all x1 -> x2, waiting for transfers between devices: 117 us -> 74.7 us  [exchange(): return lax.all_to_all(value, axis, split_axis=0, concat_axis=0, tiled=True)]
    all_to_all x2 -> x1, blocking collectives: 61.5 us -> 18.8 us  [exchange(): return lax.all_to_all(value, axis, split_axis=0, concat_axis=0, tiled=True)]
    all_to_all x1 -> x2, starting transfers between devices: 11.5 us -> 23.6 us  [exchange(): return lax.all_to_all(value, axis, split_axis=0, concat_axis=0, tiled=True)]
    ppermute x0 -> x8, starting transfers between devices: none -> 6.4 us  [the longest x3 4.52 us: per_device(): lax.ppermute(pair, 'chan', [(n, n // 4 * 4 + (n + k) % 4) for n in range(...]
  transfers between devices with their start and end apart: 2 -> 10, of which waited for: 1 -> 7; matrix products, arithmetic and copies ran while one was open for 0% -> 1% of each run, Pallas kernels for 6% -> 6%
where the time goes in v3:
time: 228 us; the launch traced here: 225 us
  waiting for transfers between devices  140 us (61%)
  Pallas kernels  31.4 us (14%)
  starting transfers between devices  30 us (13%)
  blocking collectives  18.8 us (8%)
  local copies, waits for them, and re-layouts  3.24 us (1%)
    all_to_all x2, waiting for transfers between devices, exchange(): return lax.all_to_all(value, axis, split_axis=0, concat_axis=0, tiled=True)  74.7 us
    ppermute x1, waiting for transfers between devices, per_device(): other = lax.ppermute(weights, 'chan', [(n, n ^ 4) for n in range(CHAN)])  53.9 us
    all_to_all x2, starting transfers between devices, exchange(): return lax.all_to_all(value, axis, split_axis=0, concat_axis=0, tiled=True)  23.6 us
    all_to_all x1, blocking collectives, exchange(): return lax.all_to_all(value, axis, split_axis=0, concat_axis=0, tiled=True)  18.8 us
    pallas_call x1, Pallas kernels, convolve(): pl.pallas_call(conv_kernel, in_specs=[pl.BlockSpec(memory_space=pltpu.HBM...  14.5 us
    ppermute x4, waiting for transfers between devices, per_device(): twins = [lax.ppermute(part, 'core', [(0, 1), (1, 0)]) for part in held]  11.7 us
    pallas_call x1, Pallas kernels, mlp(): pl.pallas_call(mlp_kernel, in_specs=[pl.BlockSpec(memory_space=pltpu.SMEM...  9.46 us
    pallas_call x1, Pallas kernels, pack(): pl.pallas_call(pack_kernel, grid_spec=pltpu.PrefetchScalarGridSpec(num_sc...  7.44 us
  transfers between devices with their start and end apart: 10, of which 7 were waited for; matrix products, arithmetic and copies ran while one was open for 1% of the time, Pallas kernels for 6%

profile of v3, /device:TPU:32, one launch (start us, length us, event | category | flops | bytes accessed | tf_op | source)
XLA Modules:
  0.0 225.4 jit_solution(7660809801762145347)
XLA Ops:
  0.0 0.0 copy-start
  0.0 7.4 %pack.1 = (bf16[32,160,512]{2,1,0:T(8,128)(2,1)}, bf16[1936,256]{1,0:T(8,128)(2,1)}) custom-call(s32[1]{0:T(128)} %bitcast.2.core_ref, bf16[4,512,256]{2,1,0:T(8,128)(2,1)} %bitcast.16, bf16[16,512,256]{2,1,0:T(8,128)(2,1)} %bitcast.14, bf16[512,512]{1,0:T(8,128)(2,1)} %constant.62.clone.perm_ref, bf16[1,256,256]{2,1,0:T(8,128)(2,1)} %refs_0_.1, ...), custom_call_target="tpu_custom_call" | custom-call | tf_op jit(solution)/shard_map/pack/pallas_call | solution.py:157
  7.4 0.0 copy-start.8
  7.5 11.6 %all-to-all-start = ((bf16[32,160,512]{2,1,0:T(8,128)(2,1)}), bf16[32,160,512]{2,1,0:T(8,128)(2,1)}, u32[]{:S(2)}, u32[]{:S(2)}) async-start(bf16[32,160,512]{2,1,0:T(8,128)(2,1)} %get-tuple-element.7), calls=%async_computation | async-start | bytes 10485760 | tf_op jit(solution)/shard_map/all_to_all | solution.py:423
  19.0 0.0 copy-done.8
  19.0 0.8 collective-permute-start
  19.8 53.9 %collective-permute-done = bf16[1936,256]{1,0:T(8,128)(2,1)S(1)} collective-permute-done((bf16[1936,256]{1,0:T(8,128)(2,1)S(1)}, bf16[1936,256]{1,0:T(8,128)(2,1)S(1)}, u32[]{:S(2)}, u32[]{:S(2)}) %collective-permute-start) | collective-permute-done | bytes 991264 | tf_op jit(solution)/shard_map/ppermute | solution.py:437
  73.7 0.0 copy-start.1
  73.7 0.0 copy-start.2
  73.7 0.0 copy-start.6
  73.7 0.0 copy-start.7
  73.7 1.5 pad_maximum_fusion.refs_0_
  75.2 2.8 %collective-permute-start.3 = (bf16[2,1936,256]{2,1,0:T(8,128)(2,1)S(1)}, bf16[2,1936,256]{2,1,0:T(8,128)(2,1)}, u32[]{:S(2)}, u32[]{:S(2)}) collective-permute-start(bf16[2,1936,256]{2,1,0:T(8,128)(2,1)S(1)} %pad_maximum_fusion.refs_0_), channel_id=1, source_target_pairs={{0,3},{1,0},{2,1},{3,2},{4,7},{5,4},{6,5},{7,6},{8,11},{9,8},{10,9... | collective-permute-start | bytes 5947400 | tf_op jit(solution)/shard_map/ppermute | solution.py:441
  78.0 0.8 collective-permute-start.2
  78.8 0.9 collective-permute-start.1
  79.7 0.0 copy-done
  79.7 0.1 dynamic-slice_bitcast_fusion
  79.8 0.1 copy.19.skip_ref
  79.9 56.8 %all-to-all-done.msg_hbm = bf16[32,160,512]{2,1,0:T(8,128)(2,1)} async-done(((bf16[32,160,512]{2,1,0:T(8,128)(2,1)}), bf16[32,160,512]{2,1,0:T(8,128)(2,1)}, u32[]{:S(2)}, u32[]{:S(2)}) %all-to-all-start) | async-done | bytes 5242912 | tf_op jit(solution)/shard_map/all_to_all | solution.py:423
  136.7 0.0 copy-done.1
  136.7 0.0 copy-done.2
  136.7 0.0 copy-done.6
  136.7 0.0 copy-done.7
  136.7 0.0 copy-start.3
  136.7 1.0 copy-done.3
  137.7 0.0 copy-start.4
  137.7 1.0 copy-done.4
  138.8 14.5 %convolve.1 = bf16[128,2,16,128]{3,2,1,0:T(8,128)(2,1)} custom-call(bf16[32,160,512]{2,1,0:T(8,128)(2,1)} %all-to-all-done.msg_hbm, f32[8,1]{1,0:T(8,128)S(1)} %copy.19.skip_ref, bf16[512,128]{1,0:T(8,128)(2,1)S(1)} %copy-done.7, bf16[128,512]{1,0:T(8,128)(2,1)S(1)} %copy-done.6, f32[256,512]{1,0:T(8,128)S(1)} %copy-done.4, f32[256,512]{1,0:T(8,128)S(1)} %copy-done.3, ...), custom_call_target="tpu_custom_call" | custom-call | tf_op jit(solution)/shard_map/convolve/pallas_call | solution.py:301
  153.3 0.0 copy-start.5
  153.3 12.0 %all-to-all-start.1 = ((bf16[256,16,128]{2,1,0:T(8,128)(2,1)}), bf16[256,16,128]{2,1,0:T(8,128)(2,1)S(1)}, u32[]{:S(2)}, u32[]{:S(2)}) async-start(bf16[256,16,128]{2,1,0:T(8,128)(2,1)} %bitcast.7), calls=%async_computation.1 | async-start | bytes 2097152 | tf_op jit(solution)/shard_map/all_to_all | solution.py:423
  165.3 0.2 collective-permute-start.4
  165.6 0.0 collective-permute-done.3.refs_3_
  165.6 0.4 collective-permute-start.7
  165.9 0.0 collective-permute-done.2.refs_2_
  165.9 0.3 collective-permute-start.6
  166.2 0.0 collective-permute-done.1.refs_1_
  166.2 0.2 collective-permute-start.5
  166.4 0.1 pad_add_fusion.place_ref
  166.5 4.3 %collective-permute-done.4.refs_4_ = bf16[2,1936,256]{2,1,0:T(8,128)(2,1)} collective-permute-done((bf16[2,1936,256]{2,1,0:T(8,128)(2,1)S(1)}, bf16[2,1936,256]{2,1,0:T(8,128)(2,1)}, u32[]{:S(2)}, u32[]{:S(2)}) %collective-permute-start.4) | collective-permute-done | bytes 1982496 | tf_op jit(solution)/shard_map/ppermute | solution.py:442
  170.8 1.7 collective-permute-done.7.refs_7_
  172.6 2.8 %collective-permute-done.6.refs_6_ = bf16[2,1936,256]{2,1,0:T(8,128)(2,1)} collective-permute-done((bf16[2,1936,256]{2,1,0:T(8,128)(2,1)}, bf16[2,1936,256]{2,1,0:T(8,128)(2,1)}, u32[]{:S(2)}, u32[]{:S(2)}) %collective-permute-start.6) | collective-permute-done | bytes 1982496 | tf_op jit(solution)/shard_map/ppermute | solution.py:442
  175.4 2.8 %collective-permute-done.5.refs_5_ = bf16[2,1936,256]{2,1,0:T(8,128)(2,1)} collective-permute-done((bf16[2,1936,256]{2,1,0:T(8,128)(2,1)}, bf16[2,1936,256]{2,1,0:T(8,128)(2,1)}, u32[]{:S(2)}, u32[]{:S(2)}) %collective-permute-start.5) | collective-permute-done | bytes 1982496 | tf_op jit(solution)/shard_map/ppermute | solution.py:442
  178.3 17.9 %all-to-all-done.1 = bf16[256,16,128]{2,1,0:T(8,128)(2,1)S(1)} async-done(((bf16[256,16,128]{2,1,0:T(8,128)(2,1)}), bf16[256,16,128]{2,1,0:T(8,128)(2,1)S(1)}, u32[]{:S(2)}, u32[]{:S(2)}) %all-to-all-start.1) | async-done | bytes 1048608 | tf_op jit(solution)/shard_map/all_to_all | solution.py:423
  196.2 0.0 copy-done.5
  196.2 9.5 %mlp.1 = bf16[8,256,256]{2,1,0:T(8,128)(2,1)S(1)} custom-call(s32[3]{0:T(128)S(1)} %pad_add_fusion.place_ref, bf16[32,8,16,128]{3,2,1,0:T(8,128)(2,1)S(1)} %bitcast.13, bf16[256,256]{1,0:T(8,128)(2,1)S(1)} %copy-done.5, bf16[2,1936,256]{2,1,0:T(8,128)(2,1)S(1)} %pad_maximum_fusion.refs_0_, bf16[2,1936,256]{2,1,0:T(8,128)(2,1)} %collective-permute-done.1.refs_1_, ...), custom_call_target="tpu_custom_call" | custom-call | tf_op jit(solution)/shard_map/mlp/pallas_call | solution.py:403
  205.6 18.8 %all_to_all.15 = bf16[8,256,256]{2,1,0:T(8,128)(2,1)S(1)} all-to-all(bf16[8,256,256]{2,1,0:T(8,128)(2,1)S(1)} %mlp.1), channel_id=1, replica_groups=mesh['chip'=16,'core'=2,'chan'=8] {'chan'}, dimensions={0} | all-to-all | bytes 2097152 | tf_op jit(solution)/shard_map/all_to_all | solution.py:423
  224.4 1.0 copy.21
Async XLA Ops:
  0.0 79.7 %copy-start = (f32[256]{0:T(256)S(1)}, f32[256]{0:T(256)}, u32[]{:S(2)}) copy-start(f32[256]{0:T(256)} %param.20) | copy-start | bytes 3076
  7.4 11.6 %copy-start.8 = (bf16[1936,256]{1,0:T(8,128)(2,1)S(1)}, bf16[1936,256]{1,0:T(8,128)(2,1)}, u32[]{:S(2)}) copy-start(bf16[1936,256]{1,0:T(8,128)(2,1)} %get-tuple-element.8) | copy-start | bytes 2973700
  7.5 129.2 %all-to-all-start = ((bf16[32,160,512]{2,1,0:T(8,128)(2,1)}), bf16[32,160,512]{2,1,0:T(8,128)(2,1)}, u32[]{:S(2)}, u32[]{:S(2)}) async-start(bf16[32,160,512]{2,1,0:T(8,128)(2,1)} %get-tuple-element.7), calls=%async_computation | async-start | bytes 10485760 | tf_op jit(solution)/shard_map/all_to_all | solution.py:423
  19.0 54.7 %collective-permute-start = (bf16[1936,256]{1,0:T(8,128)(2,1)S(1)}, bf16[1936,256]{1,0:T(8,128)(2,1)S(1)}, u32[]{:S(2)}, u32[]{:S(2)}) collective-permute-start(bf16[1936,256]{1,0:T(8,128)(2,1)S(1)} %copy-done.8), channel_id=1, source_target_pairs={{0,4},{1,5},{2,6},{3,7},{4,0},{5,1},{6,2},{7,3},{8,12},{9,13},{10,... | collective-permute-start | bytes 2973704 | tf_op jit(solution)/shard_map/ppermute | solution.py:437
  73.7 63.0 %copy-start.1 = (bf16[4,256,256]{2,1,0:T(8,128)(2,1)S(1)}, bf16[4,256,256]{2,1,0:T(8,128)(2,1)}, u32[]{:S(2)}) copy-start(bf16[4,256,256]{2,1,0:T(8,128)(2,1)} %constant.68.clone.inv_ref) | copy-start | bytes 1572868
  73.7 63.0 %copy-start.2 = (bf16[4,256,256]{2,1,0:T(8,128)(2,1)S(1)}, bf16[4,256,256]{2,1,0:T(8,128)(2,1)}, u32[]{:S(2)}) copy-start(bf16[4,256,256]{2,1,0:T(8,128)(2,1)} %constant.67.clone.fwd_ref) | copy-start | bytes 1572868
  73.7 63.0 %copy-start.6 = (bf16[128,512]{1,0:T(8,128)(2,1)S(1)}, bf16[128,512]{1,0:T(8,128)(2,1)}, u32[]{:S(2)}) copy-start(bf16[128,512]{1,0:T(8,128)(2,1)} %constant.64.clone.row_inv_ref) | copy-start | bytes 393220
  73.7 63.0 %copy-start.7 = (bf16[512,128]{1,0:T(8,128)(2,1)S(1)}, bf16[512,128]{1,0:T(8,128)(2,1)}, u32[]{:S(2)}) copy-start(bf16[512,128]{1,0:T(8,128)(2,1)} %constant.63.clone.row_fwd_ref) | copy-start | bytes 393220
  75.2 90.4 %collective-permute-start.3 = (bf16[2,1936,256]{2,1,0:T(8,128)(2,1)S(1)}, bf16[2,1936,256]{2,1,0:T(8,128)(2,1)}, u32[]{:S(2)}, u32[]{:S(2)}) collective-permute-start(bf16[2,1936,256]{2,1,0:T(8,128)(2,1)S(1)} %pad_maximum_fusion.refs_0_), channel_id=1, source_target_pairs={{0,3},{1,0},{2,1},{3,2},{4,7},{5,4},{6,5},{7,6},{8,11},{9,8},{10,9... | collective-permute-start | bytes 5947400 | tf_op jit(solution)/shard_map/ppermute | solution.py:441
  78.0 87.9 %collective-permute-start.2 = (bf16[2,1936,256]{2,1,0:T(8,128)(2,1)S(1)}, bf16[2,1936,256]{2,1,0:T(8,128)(2,1)}, u32[]{:S(2)}, u32[]{:S(2)}) collective-permute-start(bf16[2,1936,256]{2,1,0:T(8,128)(2,1)S(1)} %pad_maximum_fusion.refs_0_), channel_id=1, source_target_pairs={{0,2},{1,3},{2,0},{3,1},{4,6},{5,7},{6,4},{7,5},{8,10},{9,11},{10,... | collective-permute-start | bytes 5947400 | tf_op jit(solution)/shard_map/ppermute | solution.py:441
  78.8 87.4 %collective-permute-start.1 = (bf16[2,1936,256]{2,1,0:T(8,128)(2,1)S(1)}, bf16[2,1936,256]{2,1,0:T(8,128)(2,1)}, u32[]{:S(2)}, u32[]{:S(2)}) collective-permute-start(bf16[2,1936,256]{2,1,0:T(8,128)(2,1)S(1)} %pad_maximum_fusion.refs_0_), channel_id=1, source_target_pairs={{0,1},{1,2},{2,3},{3,0},{4,5},{5,6},{6,7},{7,4},{8,9},{9,10},{10,1... | collective-permute-start | bytes 5947400 | tf_op jit(solution)/shard_map/ppermute | solution.py:441
  136.7 1.0 copy-start.3
  137.7 1.0 copy-start.4
  153.3 42.9 %copy-start.5 = (bf16[256,256]{1,0:T(8,128)(2,1)S(1)}, bf16[256,256]{1,0:T(8,128)(2,1)}, u32[]{:S(2)}) copy-start(bf16[256,256]{1,0:T(8,128)(2,1)} %constant.69.clone.unperm_ref) | copy-start | bytes 393220
  153.3 42.9 %all-to-all-start.1 = ((bf16[256,16,128]{2,1,0:T(8,128)(2,1)}), bf16[256,16,128]{2,1,0:T(8,128)(2,1)S(1)}, u32[]{:S(2)}, u32[]{:S(2)}) async-start(bf16[256,16,128]{2,1,0:T(8,128)(2,1)} %bitcast.7), calls=%async_computation.1 | async-start | bytes 2097152 | tf_op jit(solution)/shard_map/all_to_all | solution.py:423
  165.3 5.5 %collective-permute-start.4 = (bf16[2,1936,256]{2,1,0:T(8,128)(2,1)S(1)}, bf16[2,1936,256]{2,1,0:T(8,128)(2,1)}, u32[]{:S(2)}, u32[]{:S(2)}) collective-permute-start(bf16[2,1936,256]{2,1,0:T(8,128)(2,1)S(1)} %pad_maximum_fusion.refs_0_), channel_id=1, source_target_pairs={{0,8},{8,0},{1,9},{9,1},{2,10},{10,2},{3,11},{11,3},{4,12},{12,4},... | collective-permute-start | bytes 5947400 | tf_op jit(solution)/shard_map/ppermute | solution.py:442
  165.6 7.0 %collective-permute-start.7 = (bf16[2,1936,256]{2,1,0:T(8,128)(2,1)}, bf16[2,1936,256]{2,1,0:T(8,128)(2,1)}, u32[]{:S(2)}, u32[]{:S(2)}) collective-permute-start(bf16[2,1936,256]{2,1,0:T(8,128)(2,1)} %collective-permute-done.3.refs_3_), channel_id=1, source_target_pairs={{0,8},{8,0},{1,9},{9,1},{2,10},{10,2},{3,11},{11,3},{4,12},{12,4},... | collective-permute-start | bytes 5947400 | tf_op jit(solution)/shard_map/ppermute | solution.py:442
  165.9 9.5 %collective-permute-start.6 = (bf16[2,1936,256]{2,1,0:T(8,128)(2,1)}, bf16[2,1936,256]{2,1,0:T(8,128)(2,1)}, u32[]{:S(2)}, u32[]{:S(2)}) collective-permute-start(bf16[2,1936,256]{2,1,0:T(8,128)(2,1)} %collective-permute-done.2.refs_2_), channel_id=1, source_target_pairs={{0,8},{8,0},{1,9},{9,1},{2,10},{10,2},{3,11},{11,3},{4,12},{12,4},... | collective-permute-start | bytes 5947400 | tf_op jit(solution)/shard_map/ppermute | solution.py:442
  166.2 12.1 %collective-permute-start.5 = (bf16[2,1936,256]{2,1,0:T(8,128)(2,1)}, bf16[2,1936,256]{2,1,0:T(8,128)(2,1)}, u32[]{:S(2)}, u32[]{:S(2)}) collective-permute-start(bf16[2,1936,256]{2,1,0:T(8,128)(2,1)} %collective-permute-done.1.refs_1_), channel_id=1, source_target_pairs={{0,8},{8,0},{1,9},{9,1},{2,10},{10,2},{3,11},{11,3},{4,12},{12,4},... | collective-permute-start | bytes 5947400 | tf_op jit(solution)/shard_map/ppermute | solution.py:442

commit v4 on v3

--- a/solution.py
+++ b/solution.py
@@ -47,10 +47,12 @@
     token = 4 * (place % 64) + 2 * (place // 128) + place // 64 % 2
     unperm = np.zeros((TOK, TOK))
     unperm[token, place] = 1.0
-    c = np.arange(AROWS)
-    rows = angle(c[:, None] * np.arange(AROWS // 2)[None, :], AROWS)
-    row_fwd = np.concatenate([np.cos(rows), -np.sin(rows)], 0)
-    row_inv = row_fwd.T
+    half = AROWS // 2
+    c = np.arange(half + 16)
+    rows = angle(c[:, None] * np.arange(half)[None, :], AROWS)
+    cos_a, sin_a = np.cos(rows) * (c <= half)[:, None], -np.sin(rows) * (c <= half)[:, None]
+    row_fwd = np.concatenate([cos_a, sin_a], 0)
+    row_inv = np.concatenate([cos_a[:half], cos_a[half : half + 1], sin_a[1:half]], 0).T
     theta = angle(c[:, None] * perm_cols[None, :], SPAN)
     fwd, inv = [], []
     for q in range(4):
@@ -65,6 +67,7 @@
         row_inv=bf16(row_inv),
         cos=np.cos(theta).astype(np.float32),
         sin=np.sin(theta).astype(np.float32),
+        flip=bf16(np.eye(256)[::-1]),
         fwd=bf16(np.stack(fwd)),
         inv=bf16(np.stack(inv)),
     )
@@ -86,149 +89,199 @@
 PIECES = 4
 
 
-def turn_weights(g1_ref, u1_ref, g2_ref, u2_ref, d1_ref, d2_ref, gain_ref, out_ref):
-    tiles = [g2_ref[0, :, 0:256], g2_ref[0, :, 256:512], u2_ref[0, :, 0:256], u2_ref[0, :, 256:512]]
-    tiles += [d1_ref[0, 0:256, :], d1_ref[0, 256:512, :]]
+def pack_kernel(core_ref, tok_hbm, spec_hbm, perm_hbm, *refs):
+    weights_hbm, (msg_ref, w_ref), refs = refs[:7], refs[7:9], refs[9:]
+    tok_s, spec_s, perm_s, g1_s, u1_s, g2_s, u2_s, d1_s, d2_s, gain_s, msg_s, w_s = refs[:12]
+    in_sem, w_sem, out_sem = refs[12:]
+    core = core_ref[0]
+
+    def columns(n):
+        return pl.ds(pl.multiple_of(core * n, n), n)
+
+    def fetch(source, target, sem):
+        return pltpu.make_async_copy(source, target, sem)
+
+    def spec_fetch(n):
+        return fetch(spec_hbm.at[pl.ds(4 * n, 4)], spec_s.at[pl.ds(4 * n, 4)], in_sem.at[n])
+
+    raw = [
+        fetch(ref.at[0, :, columns(target.shape[1])], target, w_sem.at[n])
+        for n, (ref, target) in enumerate(zip(weights_hbm[:4], (g1_s, u1_s, g2_s, u2_s)))
+    ]
+    raw.append(fetch(weights_hbm[4].at[0, columns(512), :], d1_s, w_sem.at[4]))
+    raw.append(fetch(weights_hbm[5].at[0, :, columns(128)], d2_s, w_sem.at[5]))
+    raw.append(fetch(weights_hbm[6], gain_s, w_sem.at[6]))
+    tokens = [fetch(tok_hbm, tok_s, in_sem.at[4]), fetch(perm_hbm, perm_s, in_sem.at[5])]
+    for n in range(4):
+        spec_fetch(n).start()
+    for copy in raw + tokens:
+        copy.start()
+
+    def turned(tiles):
+        tiles = [tile.T.astype(F32).reshape(SEQ, OWN, COLS) for tile in tiles]
+        return jnp.concatenate(tiles, 1).astype(BF16)
+
+    sent = []
+
+    def send(rows, at):
+        for n in range(PIECES):
+            part = pl.ds(n * (SEQ // PIECES), SEQ // PIECES)
+            copy = pltpu.make_async_copy(
+                msg_s.at[part, rows, :], msg_ref.at[part, rows, :], out_sem.at[at, n]
+            )
+            copy.start()
+            sent.append(copy)
+
+    for n in range(4):
+        spec_fetch(n).wait()
+        for m in range(2):
+            pair = turned([spec_s[4 * n + 2 * m], spec_s[4 * n + 2 * m + 1]])
+            msg_s[:, n * 32 + m * 16 : n * 32 + m * 16 + 16, :] = pair
+        send(pl.ds(n * 32, 32), n)
+
+    for copy in raw:
+        copy.wait()
+    tiles = [g2_s[:, 0:256], g2_s[:, 256:512], u2_s[:, 0:256], u2_s[:, 256:512]]
+    tiles += [d1_s[0:256, :], d1_s[256:512, :]]
     for n, tile in enumerate(tiles):
-        out_ref[n * 256 : n * 256 + 256, :] = tile.T
-    for n, ref in enumerate((g1_ref, u1_ref, d2_ref)):
+        w_s[n * 256 : n * 256 + 256, :] = tile.T
+    for n, ref in enumerate((g1_s, u1_s, d2_s)):
         r0 = 1536 + n * 128
-        out_ref[r0 : r0 + 128, :] = ref[0].T
-    gain = gain_ref[...]
+        w_s[r0 : r0 + 128, :] = ref[...].T
+    gain = gain_s[...]
     high = gain.astype(BF16).astype(F32)
     mid = (gain - high).astype(BF16).astype(F32)
     low = gain - high - mid
-    out_ref[1920:, :] = jnp.concatenate([high, mid, low, jnp.zeros((13, PB), F32)], 0).astype(BF16)
-
-
-def pack_kernel(core_ref, tok_ref, spec_ref, perm_ref, *refs):
-    weight_refs, (msg_ref, w_ref, msg_s, w_s, msg_sem, w_sem) = refs[:7], refs[7:]
-    step = pl.program_id(0)
-
-    def turned(tiles):
-        tiles = [tile.T.astype(F32).reshape(SEQ, OWN, COLS) for tile in tiles]
-        return jnp.concatenate(tiles, 1).astype(BF16)
-
-    def copies(at):
-        rows = pl.ds(pl.multiple_of(at * 32, 32), 32)
-        for n in range(PIECES):
-            part = pl.ds(n * (SEQ // PIECES), SEQ // PIECES)
-            yield pltpu.make_async_copy(
-                msg_s.at[part, rows, :], msg_ref.at[part, rows, :], msg_sem.at[at, n]
-            )
-
-    w_copy = pltpu.make_async_copy(w_s, w_ref, w_sem)
-
-    @pl.when(step < 4)
-    def _():
-        for n in range(2):
-            rows = pl.ds(pl.multiple_of(step * 32 + n * 16, 16), 16)
-            msg_s[:, rows, :] = turned([spec_ref[2 * n], spec_ref[2 * n + 1]])
-
-    @pl.when(step == 4)
-    def _():
-        perm = perm_ref[...]
-        for n in range(2):
-            tiles = [dot(perm, tok_ref[2 * n + m]).astype(BF16) for m in range(2)]
-            msg_s[:, S_ROWS + n * 16 : S_ROWS + n * 16 + 16, :] = turned(tiles)
-
-    for copy in copies(step):
-        copy.start()
-
-    @pl.when(step == 1)
-    def _():
-        turn_weights(*weight_refs, w_s)
-        w_copy.start()
-
-    @pl.when(step == 4)
-    def _():
-        for at in range(5):
-            for copy in copies(at):
-                copy.wait()
-        w_copy.wait()
+    w_s[1920:, :] = jnp.concatenate([high, mid, low, jnp.zeros((13, PB), F32)], 0).astype(BF16)
+    w_copy = pltpu.make_async_copy(w_s, w_ref, w_sem.at[7])
+    w_copy.start()
+    sent.append(w_copy)
+
+    for copy in tokens:
+        copy.wait()
+    perm = perm_s[...]
+    for m in range(2):
+        pair = [dot(perm, tok_s[2 * m + n]).astype(BF16) for n in range(2)]
+        msg_s[:, S_ROWS + m * 16 : S_ROWS + m * 16 + 16, :] = turned(pair)
+    send(pl.ds(S_ROWS, X_ROWS), 4)
+    for copy in sent:
+        copy.wait()
 
 
 def pack(tokens, spectrum, core, weights, gain, tb):
     tok = tokens.reshape(ROWS_DEV, COLS, WIDTH)
     spec = spectrum.reshape(16, COLS, WIDTH)
-    whole = lambda *shape: pl.BlockSpec(shape, lambda g, core: (0,) * len(shape))
-    cols = lambda n: pl.BlockSpec((1, PB, n), lambda g, core: (0, 0, core[0]))
     hbm = pl.BlockSpec(memory_space=pltpu.HBM)
+    shapes = [tok.shape, spec.shape, (COLS, COLS), (PB, 128), (PB, 128), (PB, 512), (PB, 512)]
+    shapes += [(512, PB), (PB, 128)]
     return pl.pallas_call(
         pack_kernel,
-        grid_spec=pltpu.PrefetchScalarGridSpec(
-            num_scalar_prefetch=1,
-            grid=(5,),
-            in_specs=[
-                whole(ROWS_DEV, COLS, WIDTH),
-                pl.BlockSpec((4, COLS, WIDTH), lambda g, core: (jnp.minimum(g, 3), 0, 0)),
-                whole(COLS, COLS),
-                cols(128),
-                cols(128),
-                cols(512),
-                cols(512),
-                pl.BlockSpec((1, 512, PB), lambda g, core: (0, core[0], 0)),
-                cols(128),
-                whole(1, WIDTH),
-            ],
-            out_specs=[hbm, hbm],
-            scratch_shapes=[
-                pltpu.VMEM((SEQ, S_ROWS + X_ROWS, COLS), BF16),
-                pltpu.VMEM((W_ROWS, PB), BF16),
-                pltpu.SemaphoreType.DMA((5, PIECES)),
-                pltpu.SemaphoreType.DMA,
-            ],
-        ),
+        in_specs=[pl.BlockSpec(memory_space=pltpu.SMEM)] + [hbm] * 10,
+        out_specs=[hbm, hbm],
         out_shape=[
             jax.ShapeDtypeStruct((SEQ, S_ROWS + X_ROWS, COLS), BF16),
             jax.ShapeDtypeStruct((W_ROWS, PB), BF16),
         ],
+        scratch_shapes=[
+            *(pltpu.VMEM(shape, BF16) for shape in shapes),
+            pltpu.VMEM((1, WIDTH), F32),
+            pltpu.VMEM((SEQ, S_ROWS + X_ROWS, COLS), BF16),
+            pltpu.VMEM((W_ROWS, PB), BF16),
+            pltpu.SemaphoreType.DMA((6,)),
+            pltpu.SemaphoreType.DMA((8,)),
+            pltpu.SemaphoreType.DMA((5, PIECES)),
+        ],
         compiler_params=params(),
         name="pack",
-    )(core, tok, spec, tb["perm"], *weights, gain)
-
-
-def conv_kernel(
-    msg_hbm, skip_ref, row_fwd_ref, row_inv_ref, cos_ref, sin_ref, fwd_ref, inv_ref,
-    out_ref, msg_ref, x_f, spec_f, conv_f, sem,
-):
+    )(core, tok, spec, jnp.asarray(tb["perm"]), *weights, gain)
+
+
+HALF = AROWS // 2
+C_ROWS = HALF + 16
+MIRROR = SEQ // 2
+TABLES = ("row_fwd", "row_inv", "cos", "sin", "fwd", "inv", "flip")
+
+
+def conv_kernel(msg_hbm, skip_ref, *refs):
+    tables_hbm, out_ref, msg_ref = refs[:7], refs[7], refs[8]
+    table_refs, (x_f, flip_f, spec_f, conv_f, sem, table_sem) = refs[9:16], refs[16:]
+    row_fwd_ref, row_inv_ref, cos_ref, sin_ref, fwd_ref, inv_ref, flip_ref = table_refs
+
     def spec_copy(part):
         devs, rows = pl.ds(part * 4, 4), pl.ds(0, S_ROWS)
         return pltpu.make_async_copy(msg_hbm.at[devs, rows, :], msg_ref.at[devs, rows, :], sem.at[part])
 
+    def table_copy(n):
+        return pltpu.make_async_copy(tables_hbm[n], table_refs[n], table_sem.at[n])
+
     rows = pl.ds(S_ROWS, X_ROWS)
     x_copy = pltpu.make_async_copy(msg_hbm.at[:, rows, :], msg_ref.at[:, rows, :], sem.at[8])
+    table_copy(6).start()
+    for part in range(4, 8):
+        spec_copy(part).start()
+    for part in range(4):
+        spec_copy(part).start()
     x_copy.start()
-    for part in range(SEQ // 4):
-        spec_copy(part).start()
+    for n in range(6):
+        table_copy(n).start()
+
+    flip_f[:, :, HALF * OWN :, :] = jnp.zeros((2, 4, OWN, 128), F32)
+    spec_f[:, :, HALF * OWN :, :] = jnp.zeros((2, 4, 16 * OWN, 128), F32)
+    table_copy(6).wait()
+    flip = flip_ref[...]
+    for part in range(4):
+        spec_copy(part + 4).wait()
+        for k in range(2):
+            for pair in range(2):
+                lanes = slice(pair * 256, pair * 256 + 256)
+                block = msg_ref[MIRROR + part * 4 : MIRROR + part * 4 + 4, k * 64 : k * 64 + 64, lanes]
+                turned = dot(block.reshape(256, 256), flip)
+                rows = slice(part * 256, part * 256 + 256)
+                flip_f[k, 2 - 2 * pair, rows, :] = turned[:, 0:128]
+                flip_f[k, 3 - 2 * pair, rows, :] = turned[:, 128:256]
+
+    for part in range(4):
+        spec_copy(part).wait()
+
+    @pl.loop(0, MIRROR, unroll=4)
+    def _(dev):
+        for k in range(2):
+            for r in range(4):
+                own = msg_ref[dev, k * 64 : k * 64 + 64, r * 128 : r * 128 + 128].astype(F32)
+                mirror = [
+                    flip_f[k, r, pl.ds(pl.multiple_of((HALF - j) * OWN - dev * 64, OWN), OWN), :]
+                    for j in range(8)
+                ]
+                mirror = jnp.concatenate(mirror, 0)
+                rows = pl.ds(pl.multiple_of(dev * 64, 64), 64)
+                spec_f[k, r, rows, :] = own + mirror if k == 0 else own - mirror
+
+    for k in range(2):
+        for r in range(4):
+            first = msg_ref[MIRROR, k * 64 : k * 64 + 16, r * 128 : r * 128 + 128].astype(F32)
+            spec_f[k, r, HALF * OWN : HALF * OWN + OWN, :] = first[0:OWN]
+
     x_copy.wait()
     for q in range(4):
         x_q = msg_ref[:, S_ROWS:, q * 128 : q * 128 + 128]
-        x_f[q] = x_q.reshape(AROWS // 2 * OWN, 128).astype(F32)
-
-    @pl.loop(0, SEQ // 4)
-    def _(part):
-        rows = pl.ds(pl.multiple_of(part * 256, 256), 256)
-        spec_copy(part).wait()
-        for k in range(2):
-            for r in range(4):
-                lanes = slice(r * 128, r * 128 + 128)
-                block = msg_ref[pl.ds(part * 4, 4), k * 64 : k * 64 + 64, lanes]
-                spec_f[k, r, rows, :] = block.reshape(256, 128).astype(F32)
-
-    @pl.loop(0, OWN, unroll=4)
+        x_f[q] = x_q.reshape(HALF * OWN, 128).astype(F32)
+    for n in range(6):
+        table_copy(n).wait()
+    top = lax.broadcasted_iota(jnp.int32, (16, 128), 0) == 0
+
+    @pl.loop(0, OWN, unroll=8)
     def _(h):
-        every = pl.ds(h, AROWS // 2, stride=OWN)
+        every = pl.ds(h, HALF, stride=OWN)
         x_h = jnp.concatenate([x_f[q, every, :] for q in range(4)], 1).astype(BF16)
         f = dot(row_fwd_ref[...], x_h)
-        blocks = [(n * 16, n * 16 + 16) for n in range(AROWS // 16)]
+        blocks = [(lo, lo + 16) for lo in range(0, C_ROWS, 16)]
         sides = []
         for q in range(4):
             lanes = slice(q * 128, q * 128 + 128)
             parts = []
             for lo, hi in blocks:
                 co, si = cos_ref[lo:hi, lanes], sin_ref[lo:hi, lanes]
-                f0, f1 = f[lo:hi, lanes], f[AROWS + lo : AROWS + hi, lanes]
+                f0, f1 = f[lo:hi, lanes], f[C_ROWS + lo : C_ROWS + hi, lanes]
                 y0, y1 = f0 * co + f1 * si, f1 * co - f0 * si
                 parts.append(jnp.concatenate([y0, y1], 1).astype(BF16))
             sides.append(dot(jnp.concatenate(parts, 0), fwd_ref[q]))
@@ -266,30 +319,32 @@
             for lo, hi in blocks:
                 co, si = cos_ref[lo:hi, lanes], sin_ref[lo:hi, lanes]
                 b0, b1 = back[lo:hi, 0:128], back[lo:hi, 128:256]
-                v0.append((b0 * co - b1 * si).astype(BF16))
-                v1.append((b1 * co + b0 * si).astype(BF16))
-            columns.append(jnp.concatenate(v0 + v1, 0))
+                v0.append(b0 * co - b1 * si)
+                v1.append(b1 * co + b0 * si)
+            v1[0] = jnp.where(top, v0[8], v1[0])
+            columns.append(jnp.concatenate([v.astype(BF16) for v in v0[:8] + v1[:8]], 0))
         conv = dot(row_inv_ref[...], jnp.concatenate(columns, 1)) * (1.0 / SPAN)
         for q in range(4):
             conv_f[q, every, :] = conv[:, q * 128 : q * 128 + 128]
 
     skip = skip_ref[...].reshape(1, OWN, 1)
-
-    @pl.loop(0, 8)
+    left = lax.broadcasted_iota(jnp.int32, (16, OWN, 128), 2) < 64
+
+    @pl.loop(0, 8, unroll=8)
     def _(part):
         a0 = pl.multiple_of(part * 16, 16)
         kept = []
         for q in range(4):
             conv = conv_f[q, pl.ds(a0 * OWN, 16 * OWN), :].astype(BF16).astype(F32)
-            x_q = msg_ref[pl.ds(part * 4, 4), S_ROWS:, q * 128 : q * 128 + 128].astype(F32)
+            x_q = x_f[q, pl.ds(a0 * OWN, 16 * OWN), :]
             kept.append(conv.reshape(16, OWN, 128) + skip * x_q.reshape(16, OWN, 128))
-        for half in range(2):
-            lanes = slice(half * 64, half * 64 + 64)
-            pairs = [
-                jnp.concatenate([kept[2 * n][:, :, lanes], kept[2 * n + 1][:, :, lanes]], 2)
-                for n in range(2)
-            ]
-            out_ref[pl.ds(a0, 16), half] = jnp.concatenate(pairs, 1).astype(BF16)
+        low, high = [], []
+        for n in range(2):
+            even, odd = kept[2 * n], kept[2 * n + 1]
+            low.append(jnp.where(left, even, pltpu.roll(odd, 64, 2)))
+            high.append(jnp.where(left, pltpu.roll(even, 64, 2), odd))
+        out_ref[pl.ds(a0, 16), 0] = jnp.concatenate(low, 1).astype(BF16)
+        out_ref[pl.ds(a0, 16), 1] = jnp.concatenate(high, 1).astype(BF16)
 
 
 def in_vmem(value):
@@ -298,21 +353,26 @@
 
 def convolve(msg, skip, tb):
     vmem = pl.BlockSpec(memory_space=pltpu.VMEM)
+    hbm = pl.BlockSpec(memory_space=pltpu.HBM)
+    tabs = [jnp.asarray(tb[n]) for n in TABLES]
     return pl.pallas_call(
         conv_kernel,
-        in_specs=[pl.BlockSpec(memory_space=pltpu.HBM)] + [vmem] * 7,
+        in_specs=[hbm, vmem] + [hbm] * len(tabs),
         out_specs=vmem,
-        out_shape=jax.ShapeDtypeStruct((AROWS // 2, 2, 16, 128), BF16),
+        out_shape=jax.ShapeDtypeStruct((HALF, 2, 16, 128), BF16),
         scratch_shapes=[
             pltpu.VMEM((SEQ, S_ROWS + X_ROWS, COLS), BF16),
-            pltpu.VMEM((4, AROWS // 2 * OWN, 128), F32),
-            pltpu.VMEM((2, 4, AROWS * OWN, 128), F32),
-            pltpu.VMEM((4, AROWS // 2 * OWN, 128), F32),
+            *(pltpu.VMEM(t.shape, t.dtype) for t in tabs),
+            pltpu.VMEM((4, HALF * OWN, 128), F32),
+            pltpu.VMEM((2, 4, HALF * OWN + OWN, 128), F32),
+            pltpu.VMEM((2, 4, C_ROWS * OWN, 128), F32),
+            pltpu.VMEM((4, HALF * OWN, 128), F32),
             pltpu.SemaphoreType.DMA((9,)),
+            pltpu.SemaphoreType.DMA((7,)),
         ],
-        compiler_params=pltpu.CompilerParams(vmem_limit_bytes=30 * 1024 * 1024),
+        compiler_params=pltpu.CompilerParams(vmem_limit_bytes=40 * 1024 * 1024),
         name="convolve",
-    )(msg, in_vmem(skip), *(in_vmem(jnp.asarray(tb[n])) for n in ("row_fwd", "row_inv", "cos", "sin", "fwd", "inv")))
+    )(msg, in_vmem(skip), *tabs)
 
 
 def mlp_kernel(place_ref, x_ref, unperm_ref, *refs):

time: 228 us -> 222 us (0.974)
  Pallas kernels: 31.4 us -> 26.3 us
    pallas_call x2, Pallas kernels: 21.9 us -> 16.9 us  [the longest x1 10.9 us: convolve(): pl.pallas_call(conv_kernel, in_specs=[hbm, vmem] + [hbm] * len(tabs), out...]
  transfers between devices with their start and end apart: 10 -> 10, of which waited for: 7 -> 8; matrix products, arithmetic and copies ran while one was open for 1% -> 1% of each run, Pallas kernels for 6% -> 5%
where the time goes in v4:
time: 222 us; the launch traced here: 220 us
  waiting for transfers between devices  141 us (64%)
  starting transfers between devices  29.6 us (13%)
  Pallas kernels  26.3 us (12%)
  blocking collectives  18.8 us (8%)
  local copies, waits for them, and re-layouts  2.96 us (1%)
    all_to_all x2, waiting for transfers between devices, exchange(): return lax.all_to_all(value, axis, split_axis=0, concat_axis=0, tiled=True)  74.7 us
    ppermute x1, waiting for transfers between devices, per_device(): other = lax.ppermute(weights, 'chan', [(n, n ^ 4) for n in range(CHAN)])  53.9 us
    all_to_all x2, starting transfers between devices, exchange(): return lax.all_to_all(value, axis, split_axis=0, concat_axis=0, tiled=True)  23.6 us
    all_to_all x1, blocking collectives, exchange(): return lax.all_to_all(value, axis, split_axis=0, concat_axis=0, tiled=True)  18.8 us
    ppermute x4, waiting for transfers between devices, per_device(): twins = [lax.ppermute(part, 'core', [(0, 1), (1, 0)]) for part in held]  11.4 us
    pallas_call x1, Pallas kernels, convolve(): pl.pallas_call(conv_kernel, in_specs=[hbm, vmem] + [hbm] * len(tabs), out...  10.9 us
    pallas_call x1, Pallas kernels, mlp(): pl.pallas_call(mlp_kernel, in_specs=[pl.BlockSpec(memory_space=pltpu.SMEM...  9.46 us
    pallas_call x1, Pallas kernels, pack(): pl.pallas_call(pack_kernel, in_specs=[pl.BlockSpec(memory_space=pltpu.SME...  6.02 us
  transfers between devices with their start and end apart: 10, of which 8 were waited for; matrix products, arithmetic and copies ran while one was open for 1% of the time, Pallas kernels for 5%

profile of v4, /device:TPU:32, one launch (start us, length us, event | category | flops | bytes accessed | tf_op | source)
XLA Modules:
  0.0 220.1 jit_solution(15406226862150204101)
XLA Ops:
  0.0 0.0 copy-start
  0.0 6.0 %pack.1 = (bf16[32,160,512]{2,1,0:T(8,128)(2,1)}, bf16[1936,256]{1,0:T(8,128)(2,1)}) custom-call(s32[1]{0:T(128)} %bitcast.2.core_ref, bf16[4,512,256]{2,1,0:T(8,128)(2,1)} %bitcast.16, bf16[16,512,256]{2,1,0:T(8,128)(2,1)} %bitcast.14, bf16[512,512]{1,0:T(8,128)(2,1)} %constant.64.clone.perm_hbm, bf16[1,256,256]{2,1,0:T(8,128)(2,1)} %refs_0_.2, ...), custom_call_target="tpu_custom_call" | custom-call | tf_op jit(solution)/shard_map/pack/pallas_call | solution.py:177
  6.0 0.0 copy-start.9
  6.0 11.6 %all-to-all-start = ((bf16[32,160,512]{2,1,0:T(8,128)(2,1)}), bf16[32,160,512]{2,1,0:T(8,128)(2,1)}, u32[]{:S(2)}, u32[]{:S(2)}) async-start(bf16[32,160,512]{2,1,0:T(8,128)(2,1)} %get-tuple-element.7), calls=%async_computation | async-start | bytes 10485760 | tf_op jit(solution)/shard_map/all_to_all | solution.py:483
  17.6 0.0 copy-done.9
  17.6 0.8 collective-permute-start
  18.4 53.9 %collective-permute-done = bf16[1936,256]{1,0:T(8,128)(2,1)S(1)} collective-permute-done((bf16[1936,256]{1,0:T(8,128)(2,1)S(1)}, bf16[1936,256]{1,0:T(8,128)(2,1)S(1)}, u32[]{:S(2)}, u32[]{:S(2)}) %collective-permute-start) | collective-permute-done | bytes 991264 | tf_op jit(solution)/shard_map/ppermute | solution.py:497
  72.3 0.0 copy-start.1
  72.3 0.0 copy-start.2
  72.3 0.0 copy-start.3
  72.3 0.0 copy-start.6
  72.3 0.0 copy-start.7
  72.3 1.5 pad_maximum_fusion.refs_0_
  73.8 2.8 %collective-permute-start.3 = (bf16[2,1936,256]{2,1,0:T(8,128)(2,1)S(1)}, bf16[2,1936,256]{2,1,0:T(8,128)(2,1)}, u32[]{:S(2)}, u32[]{:S(2)}) collective-permute-start(bf16[2,1936,256]{2,1,0:T(8,128)(2,1)S(1)} %pad_maximum_fusion.refs_0_), channel_id=1, source_target_pairs={{0,3},{1,0},{2,1},{3,2},{4,7},{5,4},{6,5},{7,6},{8,11},{9,8},{10,9... | collective-permute-start | bytes 5947400 | tf_op jit(solution)/shard_map/ppermute | solution.py:501
  76.6 0.8 collective-permute-start.2
  77.4 0.9 collective-permute-start.1
  78.3 0.0 copy-done
  78.3 0.1 dynamic-slice_bitcast_fusion
  78.4 0.1 copy.20.skip_ref
  78.5 56.8 %all-to-all-done.msg_hbm = bf16[32,160,512]{2,1,0:T(8,128)(2,1)} async-done(((bf16[32,160,512]{2,1,0:T(8,128)(2,1)}), bf16[32,160,512]{2,1,0:T(8,128)(2,1)}, u32[]{:S(2)}, u32[]{:S(2)}) %all-to-all-start) | async-done | bytes 5242912 | tf_op jit(solution)/shard_map/all_to_all | solution.py:483
  135.2 0.0 copy-done.1
  135.2 0.0 copy-done.2
  135.3 0.0 copy-done.3
  135.3 0.0 copy-done.6
  135.3 0.0 copy-done.7
  135.3 0.0 copy-start.4
  135.3 1.0 copy-done.4
  136.2 0.0 copy-start.8
  136.2 0.8 copy-done.8
  137.1 10.9 %convolve.1 = bf16[128,2,16,128]{3,2,1,0:T(8,128)(2,1)} custom-call(bf16[32,160,512]{2,1,0:T(8,128)(2,1)} %all-to-all-done.msg_hbm, f32[8,1]{1,0:T(8,128)S(1)} %copy.20.skip_ref, bf16[288,128]{1,0:T(8,128)(2,1)S(1)} %copy-done.7, bf16[128,256]{1,0:T(8,128)(2,1)S(1)} %copy-done.8, f32[144,512]{1,0:T(8,128)S(1)} %copy-done.4, f32[144,512]{1,0:T(8,128)S(1)} %copy-done.3, ...), custom_call_target="tpu_custom_call" | custom-call | tf_op jit(solution)/shard_map/convolve/pallas_call | solution.py:358
  148.0 0.0 copy-start.5
  148.0 12.0 %all-to-all-start.1 = ((bf16[256,16,128]{2,1,0:T(8,128)(2,1)}), bf16[256,16,128]{2,1,0:T(8,128)(2,1)S(1)}, u32[]{:S(2)}, u32[]{:S(2)}) async-start(bf16[256,16,128]{2,1,0:T(8,128)(2,1)} %bitcast.7), calls=%async_computation.1 | async-start | bytes 2097152 | tf_op jit(solution)/shard_map/all_to_all | solution.py:483
  160.0 0.2 collective-permute-start.4
  160.2 0.0 collective-permute-done.3.refs_3_
  160.2 0.4 collective-permute-start.7
  160.6 0.0 collective-permute-done.2.refs_2_
  160.6 0.1 collective-permute-start.6
  160.8 0.7 collective-permute-done.1.refs_1_
  161.4 0.0 collective-permute-start.5
  161.4 0.1 pad_add_fusion.place_ref
  161.5 4.0 %collective-permute-done.4.refs_4_ = bf16[2,1936,256]{2,1,0:T(8,128)(2,1)} collective-permute-done((bf16[2,1936,256]{2,1,0:T(8,128)(2,1)S(1)}, bf16[2,1936,256]{2,1,0:T(8,128)(2,1)}, u32[]{:S(2)}, u32[]{:S(2)}) %collective-permute-start.4) | collective-permute-done | bytes 1982496 | tf_op jit(solution)/shard_map/ppermute | solution.py:502
  165.5 1.7 collective-permute-done.7.refs_7_
  167.3 2.8 %collective-permute-done.6.refs_6_ = bf16[2,1936,256]{2,1,0:T(8,128)(2,1)} collective-permute-done((bf16[2,1936,256]{2,1,0:T(8,128)(2,1)}, bf16[2,1936,256]{2,1,0:T(8,128)(2,1)}, u32[]{:S(2)}, u32[]{:S(2)}) %collective-permute-start.6) | collective-permute-done | bytes 1982496 | tf_op jit(solution)/shard_map/ppermute | solution.py:502
  170.1 2.8 %collective-permute-done.5.refs_5_ = bf16[2,1936,256]{2,1,0:T(8,128)(2,1)} collective-permute-done((bf16[2,1936,256]{2,1,0:T(8,128)(2,1)}, bf16[2,1936,256]{2,1,0:T(8,128)(2,1)}, u32[]{:S(2)}, u32[]{:S(2)}) %collective-permute-start.5) | collective-permute-done | bytes 1982496 | tf_op jit(solution)/shard_map/ppermute | solution.py:502
  172.9 17.9 %all-to-all-done.1 = bf16[256,16,128]{2,1,0:T(8,128)(2,1)S(1)} async-done(((bf16[256,16,128]{2,1,0:T(8,128)(2,1)}), bf16[256,16,128]{2,1,0:T(8,128)(2,1)S(1)}, u32[]{:S(2)}, u32[]{:S(2)}) %all-to-all-start.1) | async-done | bytes 1048608 | tf_op jit(solution)/shard_map/all_to_all | solution.py:483
  190.8 0.0 copy-done.5
  190.8 9.5 %mlp.1 = bf16[8,256,256]{2,1,0:T(8,128)(2,1)S(1)} custom-call(s32[3]{0:T(128)S(1)} %pad_add_fusion.place_ref, bf16[32,8,16,128]{3,2,1,0:T(8,128)(2,1)S(1)} %bitcast.13, bf16[256,256]{1,0:T(8,128)(2,1)S(1)} %copy-done.5, bf16[2,1936,256]{2,1,0:T(8,128)(2,1)S(1)} %pad_maximum_fusion.refs_0_, bf16[2,1936,256]{2,1,0:T(8,128)(2,1)} %collective-permute-done.1.refs_1_, ...), custom_call_target="tpu_custom_call" | custom-call | tf_op jit(solution)/shard_map/mlp/pallas_call | solution.py:463
  200.3 18.8 %all_to_all.15 = bf16[8,256,256]{2,1,0:T(8,128)(2,1)S(1)} all-to-all(bf16[8,256,256]{2,1,0:T(8,128)(2,1)S(1)} %mlp.1), channel_id=1, replica_groups=mesh['chip'=16,'core'=2,'chan'=8] {'chan'}, dimensions={0} | all-to-all | bytes 2097152 | tf_op jit(solution)/shard_map/all_to_all | solution.py:483
  219.1 1.0 copy.22
Async XLA Ops:
  0.0 78.3 %copy-start = (f32[256]{0:T(256)S(1)}, f32[256]{0:T(256)}, u32[]{:S(2)}) copy-start(f32[256]{0:T(256)} %param.21) | copy-start | bytes 3076
  6.0 11.6 %copy-start.9 = (bf16[1936,256]{1,0:T(8,128)(2,1)S(1)}, bf16[1936,256]{1,0:T(8,128)(2,1)}, u32[]{:S(2)}) copy-start(bf16[1936,256]{1,0:T(8,128)(2,1)} %get-tuple-element.8) | copy-start | bytes 2973700
  6.0 129.2 %all-to-all-start = ((bf16[32,160,512]{2,1,0:T(8,128)(2,1)}), bf16[32,160,512]{2,1,0:T(8,128)(2,1)}, u32[]{:S(2)}, u32[]{:S(2)}) async-start(bf16[32,160,512]{2,1,0:T(8,128)(2,1)} %get-tuple-element.7), calls=%async_computation | async-start | bytes 10485760 | tf_op jit(solution)/shard_map/all_to_all | solution.py:483
  17.6 54.7 %collective-permute-start = (bf16[1936,256]{1,0:T(8,128)(2,1)S(1)}, bf16[1936,256]{1,0:T(8,128)(2,1)S(1)}, u32[]{:S(2)}, u32[]{:S(2)}) collective-permute-start(bf16[1936,256]{1,0:T(8,128)(2,1)S(1)} %copy-done.9), channel_id=1, source_target_pairs={{0,4},{1,5},{2,6},{3,7},{4,0},{5,1},{6,2},{7,3},{8,12},{9,13},{10,... | collective-permute-start | bytes 2973704 | tf_op jit(solution)/shard_map/ppermute | solution.py:497
  72.3 63.0 %copy-start.1 = (bf16[4,256,256]{2,1,0:T(8,128)(2,1)S(1)}, bf16[4,256,256]{2,1,0:T(8,128)(2,1)}, u32[]{:S(2)}) copy-start(bf16[4,256,256]{2,1,0:T(8,128)(2,1)} %constant.70.clone.refs_5_) | copy-start | bytes 1572868
  72.3 63.0 %copy-start.2 = (bf16[4,256,256]{2,1,0:T(8,128)(2,1)S(1)}, bf16[4,256,256]{2,1,0:T(8,128)(2,1)}, u32[]{:S(2)}) copy-start(bf16[4,256,256]{2,1,0:T(8,128)(2,1)} %constant.69.clone.refs_4_) | copy-start | bytes 1572868
  72.3 63.0 %copy-start.3 = (f32[144,512]{1,0:T(8,128)S(1)}, f32[144,512]{1,0:T(8,128)}, u32[]{:S(2)}) copy-start(f32[144,512]{1,0:T(8,128)} %constant.68.clone.refs_3_) | copy-start | bytes 884740
  72.3 63.0 %copy-start.6 = (bf16[256,256]{1,0:T(8,128)(2,1)S(1)}, bf16[256,256]{1,0:T(8,128)(2,1)}, u32[]{:S(2)}) copy-start(bf16[256,256]{1,0:T(8,128)(2,1)} %constant.71.clone.refs_6_) | copy-start | bytes 393220
  72.3 63.0 %copy-start.7 = (bf16[288,128]{1,0:T(8,128)(2,1)S(1)}, bf16[288,128]{1,0:T(8,128)(2,1)}, u32[]{:S(2)}) copy-start(bf16[288,128]{1,0:T(8,128)(2,1)} %constant.65.clone.refs_0_) | copy-start | bytes 221188
  73.8 86.4 %collective-permute-start.3 = (bf16[2,1936,256]{2,1,0:T(8,128)(2,1)S(1)}, bf16[2,1936,256]{2,1,0:T(8,128)(2,1)}, u32[]{:S(2)}, u32[]{:S(2)}) collective-permute-start(bf16[2,1936,256]{2,1,0:T(8,128)(2,1)S(1)} %pad_maximum_fusion.refs_0_), channel_id=1, source_target_pairs={{0,3},{1,0},{2,1},{3,2},{4,7},{5,4},{6,5},{7,6},{8,11},{9,8},{10,9... | collective-permute-start | bytes 5947400 | tf_op jit(solution)/shard_map/ppermute | solution.py:501
  76.6 84.0 %collective-permute-start.2 = (bf16[2,1936,256]{2,1,0:T(8,128)(2,1)S(1)}, bf16[2,1936,256]{2,1,0:T(8,128)(2,1)}, u32[]{:S(2)}, u32[]{:S(2)}) collective-permute-start(bf16[2,1936,256]{2,1,0:T(8,128)(2,1)S(1)} %pad_maximum_fusion.refs_0_), channel_id=1, source_target_pairs={{0,2},{1,3},{2,0},{3,1},{4,6},{5,7},{6,4},{7,5},{8,10},{9,11},{10,... | collective-permute-start | bytes 5947400 | tf_op jit(solution)/shard_map/ppermute | solution.py:501
  77.4 84.0 %collective-permute-start.1 = (bf16[2,1936,256]{2,1,0:T(8,128)(2,1)S(1)}, bf16[2,1936,256]{2,1,0:T(8,128)(2,1)}, u32[]{:S(2)}, u32[]{:S(2)}) collective-permute-start(bf16[2,1936,256]{2,1,0:T(8,128)(2,1)S(1)} %pad_maximum_fusion.refs_0_), channel_id=1, source_target_pairs={{0,1},{1,2},{2,3},{3,0},{4,5},{5,6},{6,7},{7,4},{8,9},{9,10},{10,1... | collective-permute-start | bytes 5947400 | tf_op jit(solution)/shard_map/ppermute | solution.py:501
  135.3 1.0 copy-start.4
  136.2 0.8 copy-start.8
  148.0 42.9 %copy-start.5 = (bf16[256,256]{1,0:T(8,128)(2,1)S(1)}, bf16[256,256]{1,0:T(8,128)(2,1)}, u32[]{:S(2)}) copy-start(bf16[256,256]{1,0:T(8,128)(2,1)} %constant.72.clone.unperm_ref) | copy-start | bytes 393220
  148.0 42.9 %all-to-all-start.1 = ((bf16[256,16,128]{2,1,0:T(8,128)(2,1)}), bf16[256,16,128]{2,1,0:T(8,128)(2,1)S(1)}, u32[]{:S(2)}, u32[]{:S(2)}) async-start(bf16[256,16,128]{2,1,0:T(8,128)(2,1)} %bitcast.7), calls=%async_computation.1 | async-start | bytes 2097152 | tf_op jit(solution)/shard_map/all_to_all | solution.py:483
  160.0 5.5 %collective-permute-start.4 = (bf16[2,1936,256]{2,1,0:T(8,128)(2,1)S(1)}, bf16[2,1936,256]{2,1,0:T(8,128)(2,1)}, u32[]{:S(2)}, u32[]{:S(2)}) collective-permute-start(bf16[2,1936,256]{2,1,0:T(8,128)(2,1)S(1)} %pad_maximum_fusion.refs_0_), channel_id=1, source_target_pairs={{0,8},{8,0},{1,9},{9,1},{2,10},{10,2},{3,11},{11,3},{4,12},{12,4},... | collective-permute-start | bytes 5947400 | tf_op jit(solution)/shard_map/ppermute | solution.py:502
  160.2 7.0 %collective-permute-start.7 = (bf16[2,1936,256]{2,1,0:T(8,128)(2,1)}, bf16[2,1936,256]{2,1,0:T(8,128)(2,1)}, u32[]{:S(2)}, u32[]{:S(2)}) collective-permute-start(bf16[2,1936,256]{2,1,0:T(8,128)(2,1)} %collective-permute-done.3.refs_3_), channel_id=1, source_target_pairs={{0,8},{8,0},{1,9},{9,1},{2,10},{10,2},{3,11},{11,3},{4,12},{12,4},... | collective-permute-start | bytes 5947400 | tf_op jit(solution)/shard_map/ppermute | solution.py:502
  160.6 9.5 %collective-permute-start.6 = (bf16[2,1936,256]{2,1,0:T(8,128)(2,1)}, bf16[2,1936,256]{2,1,0:T(8,128)(2,1)}, u32[]{:S(2)}, u32[]{:S(2)}) collective-permute-start(bf16[2,1936,256]{2,1,0:T(8,128)(2,1)} %collective-permute-done.2.refs_2_), channel_id=1, source_target_pairs={{0,8},{8,0},{1,9},{9,1},{2,10},{10,2},{3,11},{11,3},{4,12},{12,4},... | collective-permute-start | bytes 5947400 | tf_op jit(solution)/shard_map/ppermute | solution.py:502
  161.4 11.5 %collective-permute-start.5 = (bf16[2,1936,256]{2,1,0:T(8,128)(2,1)}, bf16[2,1936,256]{2,1,0:T(8,128)(2,1)}, u32[]{:S(2)}, u32[]{:S(2)}) collective-permute-start(bf16[2,1936,256]{2,1,0:T(8,128)(2,1)} %collective-permute-done.1.refs_1_), channel_id=1, source_target_pairs={{0,8},{8,0},{1,9},{9,1},{2,10},{10,2},{3,11},{11,3},{4,12},{12,4},... | collective-permute-start | bytes 5947400 | tf_op jit(solution)/shard_map/ppermute | solution.py:502

commit v5 on v4

--- a/solution.py
+++ b/solution.py
@@ -269,12 +269,12 @@
         table_copy(n).wait()
     top = lax.broadcasted_iota(jnp.int32, (16, 128), 0) == 0
 
-    @pl.loop(0, OWN, unroll=8)
-    def _(h):
+    blocks = [(lo, lo + 16) for lo in range(0, C_ROWS, 16)]
+
+    def forward(h):
         every = pl.ds(h, HALF, stride=OWN)
         x_h = jnp.concatenate([x_f[q, every, :] for q in range(4)], 1).astype(BF16)
         f = dot(row_fwd_ref[...], x_h)
-        blocks = [(lo, lo + 16) for lo in range(0, C_ROWS, 16)]
         sides = []
         for q in range(4):
             lanes = slice(q * 128, q * 128 + 128)
@@ -285,7 +285,9 @@
                 y0, y1 = f0 * co + f1 * si, f1 * co - f0 * si
                 parts.append(jnp.concatenate([y0, y1], 1).astype(BF16))
             sides.append(dot(jnp.concatenate(parts, 0), fwd_ref[q]))
-
+        return sides
+
+    def middle(h, sides):
         parts = [[] for _ in range(4)]
         for lo, hi in blocks:
             re = [sides[q][lo:hi, 0:128] for q in range(4)]
@@ -311,10 +313,13 @@
             for q in range(4):
                 parts[q].append(jnp.concatenate([qr[q], qi[q]], 1).astype(BF16))
 
+        return [dot(jnp.concatenate(parts[q], 0), inv_ref[q]) for q in range(4)]
+
+    def backward(h, backs):
         columns = []
         for q in range(4):
             lanes = slice(q * 128, q * 128 + 128)
-            back = dot(jnp.concatenate(parts[q], 0), inv_ref[q])
+            back = backs[q]
             v0, v1 = [], []
             for lo, hi in blocks:
                 co, si = cos_ref[lo:hi, lanes], sin_ref[lo:hi, lanes]
@@ -325,7 +330,16 @@
             columns.append(jnp.concatenate([v.astype(BF16) for v in v0[:8] + v1[:8]], 0))
         conv = dot(row_inv_ref[...], jnp.concatenate(columns, 1)) * (1.0 / SPAN)
         for q in range(4):
-            conv_f[q, every, :] = conv[:, q * 128 : q * 128 + 128]
+            conv_f[q, pl.ds(h, HALF, stride=OWN), :] = conv[:, q * 128 : q * 128 + 128]
+
+    sides, backs = {}, {}
+    for step in range(OWN + 2):
+        if step < OWN:
+            sides[step] = forward(step)
+        if 0 <= step - 1 < OWN:
+            backs[step - 1] = middle(step - 1, sides.pop(step - 1))
+        if step >= 2:
+            backward(step - 2, backs.pop(step - 2))
 
     skip = skip_ref[...].reshape(1, OWN, 1)
     left = lax.broadcasted_iota(jnp.int32, (16, OWN, 128), 2) < 64
@@ -345,6 +359,10 @@
             high.append(jnp.where(left, pltpu.roll(even, 64, 2), odd))
         out_ref[pl.ds(a0, 16), 0] = jnp.concatenate(low, 1).astype(BF16)
         out_ref[pl.ds(a0, 16), 1] = jnp.concatenate(high, 1).astype(BF16)
+
+
+def in_hbm(value):
+    return pltpu.with_memory_space_constraint(value, pltpu.HBM)
 
 
 def in_vmem(value):
@@ -372,7 +390,7 @@
         ],
         compiler_params=pltpu.CompilerParams(vmem_limit_bytes=40 * 1024 * 1024),
         name="convolve",
-    )(msg, in_vmem(skip), *tabs)
+    )(msg, in_vmem(skip), *(in_hbm(t) for t in tabs))
 
 
 def mlp_kernel(place_ref, x_ref, unperm_ref, *refs):
@@ -425,17 +443,22 @@
                 m1 = 128 + m * PIECE
                 up_s[half * 4 + m, rows, :] = mid[m1 : m1 + PIECE]
 
-    def block(n):
+    def widen(n):
         j = block_of(n)
         gate_in, up_in = gate_s[j], up_s[j]
+        halves = []
+        for half in range(2):
+            gate = dot(w_ref[n, half, 0:512, :], gate_in)
+            halves.append((gate, dot(w_ref[n, half, 512:1024, :], up_in)))
+        return halves
+
+    def narrow(n, halves):
+        j = block_of(n)
         acts, lefts = [], []
-        for half in range(2):
+        for half, (gate, upper) in enumerate(halves):
+            acts.append((jax.nn.gelu(gate, approximate=True) * upper).astype(BF16))
             for m in range(2):
-                r0 = m * 256
-                gate = dot(w_ref[n, half, r0 : r0 + 256, :], gate_in)
-                upper = dot(w_ref[n, half, 512 + r0 : 768 + r0, :], up_in)
-                acts.append((jax.nn.gelu(gate, approximate=True) * upper).astype(BF16))
-                lefts.append(w_ref[n, half, 1024 + r0 : 1280 + r0, :])
+                lefts.append(w_ref[n, half, 1024 + m * 256 : 1280 + m * 256, :])
         mid = dot(jnp.concatenate(lefts, 1), jnp.concatenate(acts, 0)).astype(BF16)
         rows = pl.ds(pl.multiple_of(j * PIECE, PIECE), PIECE)
         for o in range(8):
@@ -445,8 +468,12 @@
         for k in range(2):
             for copy in copies(1, group * 2 + k):
                 copy.wait()
-        for n in range(4):
-            block(group * 4 + n)
+        wide = None
+        for n in range(5):
+            later = widen(group * 4 + n) if n < 4 else None
+            if n > 0:
+                narrow(group * 4 + n - 1, wide)
+            wide = later
 
     unperm = unperm_ref[...]
     for n in range(8):

time: 222 us -> 220 us (level)
  transfers between devices with their start and end apart: 10 -> 10, of which waited for: 8 -> 8; matrix products, arithmetic and copies ran while one was open for 1% -> 0% of each run, Pallas kernels for 5% -> 5%
where the time goes in v5:
time: 220 us; the launch traced here: 218 us
  waiting for transfers between devices  142 us (65%)
  starting transfers between devices  29.6 us (13%)
  Pallas kernels  25.7 us (12%)
  blocking collectives  18.8 us (9%)
    all_to_all x2, waiting for transfers between devices, exchange(): return lax.all_to_all(value, axis, split_axis=0, concat_axis=0, tiled=True)  76 us
    ppermute x1, waiting for transfers between devices, per_device(): other = lax.ppermute(weights, 'chan', [(n, n ^ 4) for n in range(CHAN)])  53.9 us
    all_to_all x2, starting transfers between devices, exchange(): return lax.all_to_all(value, axis, split_axis=0, concat_axis=0, tiled=True)  23.6 us
    all_to_all x1, blocking collectives, exchange(): return lax.all_to_all(value, axis, split_axis=0, concat_axis=0, tiled=True)  18.8 us
    ppermute x4, waiting for transfers between devices, per_device(): twins = [lax.ppermute(part, 'core', [(0, 1), (1, 0)]) for part in held]  10.6 us
    pallas_call x1, Pallas kernels, convolve(): pl.pallas_call(conv_kernel, in_specs=[hbm, vmem] + [hbm] * len(tabs), out...  10.5 us
    pallas_call x1, Pallas kernels, mlp(): pl.pallas_call(mlp_kernel, in_specs=[pl.BlockSpec(memory_space=pltpu.SMEM...  9.09 us
    pallas_call x1, Pallas kernels, pack(): pl.pallas_call(pack_kernel, in_specs=[pl.BlockSpec(memory_space=pltpu.SME...  6.08 us
  transfers between devices with their start and end apart: 10, of which 8 were waited for; matrix products, arithmetic and copies ran while one was open for 0% of the time, Pallas kernels for 5%

profile of v5, /device:TPU:32, one launch (start us, length us, event | category | flops | bytes accessed | tf_op | source)
XLA Modules:
  0.0 217.6 jit_solution(1323274210801985273)
XLA Ops:
  0.0 0.0 copy-start
  0.0 6.1 %pack.1 = (bf16[32,160,512]{2,1,0:T(8,128)(2,1)}, bf16[1936,256]{1,0:T(8,128)(2,1)}) custom-call(s32[1]{0:T(128)} %bitcast.2.core_ref, bf16[4,512,256]{2,1,0:T(8,128)(2,1)} %bitcast.16, bf16[16,512,256]{2,1,0:T(8,128)(2,1)} %bitcast.14, bf16[512,512]{1,0:T(8,128)(2,1)} %constant.64.clone.perm_hbm, bf16[1,256,256]{2,1,0:T(8,128)(2,1)} %refs_0_.2, ...), custom_call_target="tpu_custom_call" | custom-call | tf_op jit(solution)/shard_map/pack/pallas_call | solution.py:177
  6.1 0.0 copy-start.2
  6.1 11.6 %all-to-all-start = ((bf16[32,160,512]{2,1,0:T(8,128)(2,1)}), bf16[32,160,512]{2,1,0:T(8,128)(2,1)}, u32[]{:S(2)}, u32[]{:S(2)}) async-start(bf16[32,160,512]{2,1,0:T(8,128)(2,1)} %get-tuple-element.7), calls=%async_computation | async-start | bytes 10485760 | tf_op jit(solution)/shard_map/all_to_all | solution.py:510
  17.7 0.0 copy-done.2
  17.7 0.8 collective-permute-start
  18.4 53.9 %collective-permute-done = bf16[1936,256]{1,0:T(8,128)(2,1)S(1)} collective-permute-done((bf16[1936,256]{1,0:T(8,128)(2,1)S(1)}, bf16[1936,256]{1,0:T(8,128)(2,1)S(1)}, u32[]{:S(2)}, u32[]{:S(2)}) %collective-permute-start) | collective-permute-done | bytes 991264 | tf_op jit(solution)/shard_map/ppermute | solution.py:524
  72.3 0.2 pad_maximum_fusion.refs_0_
  72.5 2.8 %collective-permute-start.3 = (bf16[2,1936,256]{2,1,0:T(8,128)(2,1)S(1)}, bf16[2,1936,256]{2,1,0:T(8,128)(2,1)}, u32[]{:S(2)}, u32[]{:S(2)}) collective-permute-start(bf16[2,1936,256]{2,1,0:T(8,128)(2,1)S(1)} %pad_maximum_fusion.refs_0_), channel_id=1, source_target_pairs={{0,3},{1,0},{2,1},{3,2},{4,7},{5,4},{6,5},{7,6},{8,11},{9,8},{10,9... | collective-permute-start | bytes 5947400 | tf_op jit(solution)/shard_map/ppermute | solution.py:528
  75.4 0.8 collective-permute-start.2
  76.2 0.9 collective-permute-start.1
  77.0 0.0 copy-done
  77.0 0.1 dynamic-slice_bitcast_fusion
  77.1 0.1 copy.20.skip_ref
  77.2 58.1 %all-to-all-done.msg_hbm = bf16[32,160,512]{2,1,0:T(8,128)(2,1)} async-done(((bf16[32,160,512]{2,1,0:T(8,128)(2,1)}), bf16[32,160,512]{2,1,0:T(8,128)(2,1)}, u32[]{:S(2)}, u32[]{:S(2)}) %all-to-all-start) | async-done | bytes 5242912 | tf_op jit(solution)/shard_map/all_to_all | solution.py:510
  135.3 10.5 %convolve.1 = bf16[128,2,16,128]{3,2,1,0:T(8,128)(2,1)} custom-call(bf16[32,160,512]{2,1,0:T(8,128)(2,1)} %all-to-all-done.msg_hbm, f32[8,1]{1,0:T(8,128)S(1)} %copy.20.skip_ref, bf16[288,128]{1,0:T(8,128)(2,1)} %constant.65.clone.refs_0_, bf16[128,256]{1,0:T(8,128)(2,1)} %constant.66.clone.refs_1_, f32[144,512]{1,0:T(8,128)} %constant.67.clone.refs_2_, ...), custom_call_target="tpu_custom_call" | custom-call | tf_op jit(solution)/shard_map/convolve/pallas_call | solution.py:376
  145.8 0.0 copy-start.1
  145.8 12.0 %all-to-all-start.1 = ((bf16[256,16,128]{2,1,0:T(8,128)(2,1)}), bf16[256,16,128]{2,1,0:T(8,128)(2,1)S(1)}, u32[]{:S(2)}, u32[]{:S(2)}) async-start(bf16[256,16,128]{2,1,0:T(8,128)(2,1)} %bitcast.7), calls=%async_computation.1 | async-start | bytes 2097152 | tf_op jit(solution)/shard_map/all_to_all | solution.py:510
  157.9 0.2 collective-permute-start.4
  158.1 0.0 collective-permute-done.3.refs_3_
  158.1 0.4 collective-permute-start.7
  158.5 0.0 collective-permute-done.2.refs_2_
  158.5 0.1 collective-permute-start.6
  158.6 1.5 collective-permute-done.1.refs_1_
  160.1 0.0 collective-permute-start.5
  160.1 0.1 pad_add_fusion.place_ref
  160.2 3.2 %collective-permute-done.4.refs_4_ = bf16[2,1936,256]{2,1,0:T(8,128)(2,1)} collective-permute-done((bf16[2,1936,256]{2,1,0:T(8,128)(2,1)S(1)}, bf16[2,1936,256]{2,1,0:T(8,128)(2,1)}, u32[]{:S(2)}, u32[]{:S(2)}) %collective-permute-start.4) | collective-permute-done | bytes 1982496 | tf_op jit(solution)/shard_map/ppermute | solution.py:529
  163.4 1.7 collective-permute-done.7.refs_7_
  165.1 2.8 %collective-permute-done.6.refs_6_ = bf16[2,1936,256]{2,1,0:T(8,128)(2,1)} collective-permute-done((bf16[2,1936,256]{2,1,0:T(8,128)(2,1)}, bf16[2,1936,256]{2,1,0:T(8,128)(2,1)}, u32[]{:S(2)}, u32[]{:S(2)}) %collective-permute-start.6) | collective-permute-done | bytes 1982496 | tf_op jit(solution)/shard_map/ppermute | solution.py:529
  168.0 2.8 %collective-permute-done.5.refs_5_ = bf16[2,1936,256]{2,1,0:T(8,128)(2,1)} collective-permute-done((bf16[2,1936,256]{2,1,0:T(8,128)(2,1)}, bf16[2,1936,256]{2,1,0:T(8,128)(2,1)}, u32[]{:S(2)}, u32[]{:S(2)}) %collective-permute-start.5) | collective-permute-done | bytes 1982496 | tf_op jit(solution)/shard_map/ppermute | solution.py:529
  170.8 17.9 %all-to-all-done.1 = bf16[256,16,128]{2,1,0:T(8,128)(2,1)S(1)} async-done(((bf16[256,16,128]{2,1,0:T(8,128)(2,1)}), bf16[256,16,128]{2,1,0:T(8,128)(2,1)S(1)}, u32[]{:S(2)}, u32[]{:S(2)}) %all-to-all-start.1) | async-done | bytes 1048608 | tf_op jit(solution)/shard_map/all_to_all | solution.py:510
  188.7 0.0 copy-done.1
  188.7 9.1 %mlp.1 = bf16[8,256,256]{2,1,0:T(8,128)(2,1)S(1)} custom-call(s32[3]{0:T(128)S(1)} %pad_add_fusion.place_ref, bf16[32,8,16,128]{3,2,1,0:T(8,128)(2,1)S(1)} %bitcast.13, bf16[256,256]{1,0:T(8,128)(2,1)S(1)} %copy-done.1, bf16[2,1936,256]{2,1,0:T(8,128)(2,1)S(1)} %pad_maximum_fusion.refs_0_, bf16[2,1936,256]{2,1,0:T(8,128)(2,1)} %collective-permute-done.1.refs_1_, ...), custom_call_target="tpu_custom_call" | custom-call | tf_op jit(solution)/shard_map/mlp/pallas_call | solution.py:490
  197.8 18.8 %all_to_all.15 = bf16[8,256,256]{2,1,0:T(8,128)(2,1)S(1)} all-to-all(bf16[8,256,256]{2,1,0:T(8,128)(2,1)S(1)} %mlp.1), channel_id=1, replica_groups=mesh['chip'=16,'core'=2,'chan'=8] {'chan'}, dimensions={0} | all-to-all | bytes 2097152 | tf_op jit(solution)/shard_map/all_to_all | solution.py:510
  216.6 1.0 copy.22
Async XLA Ops:
  0.0 77.0 %copy-start = (f32[256]{0:T(256)S(1)}, f32[256]{0:T(256)}, u32[]{:S(2)}) copy-start(f32[256]{0:T(256)} %param.21) | copy-start | bytes 3076
  6.1 11.6 %copy-start.2 = (bf16[1936,256]{1,0:T(8,128)(2,1)S(1)}, bf16[1936,256]{1,0:T(8,128)(2,1)}, u32[]{:S(2)}) copy-start(bf16[1936,256]{1,0:T(8,128)(2,1)} %get-tuple-element.8) | copy-start | bytes 2973700
  6.1 129.2 %all-to-all-start = ((bf16[32,160,512]{2,1,0:T(8,128)(2,1)}), bf16[32,160,512]{2,1,0:T(8,128)(2,1)}, u32[]{:S(2)}, u32[]{:S(2)}) async-start(bf16[32,160,512]{2,1,0:T(8,128)(2,1)} %get-tuple-element.7), calls=%async_computation | async-start | bytes 10485760 | tf_op jit(solution)/shard_map/all_to_all | solution.py:510
  17.7 54.7 %collective-permute-start = (bf16[1936,256]{1,0:T(8,128)(2,1)S(1)}, bf16[1936,256]{1,0:T(8,128)(2,1)S(1)}, u32[]{:S(2)}, u32[]{:S(2)}) collective-permute-start(bf16[1936,256]{1,0:T(8,128)(2,1)S(1)} %copy-done.2), channel_id=1, source_target_pairs={{0,4},{1,5},{2,6},{3,7},{4,0},{5,1},{6,2},{7,3},{8,12},{9,13},{10,... | collective-permute-start | bytes 2973704 | tf_op jit(solution)/shard_map/ppermute | solution.py:524
  72.5 85.6 %collective-permute-start.3 = (bf16[2,1936,256]{2,1,0:T(8,128)(2,1)S(1)}, bf16[2,1936,256]{2,1,0:T(8,128)(2,1)}, u32[]{:S(2)}, u32[]{:S(2)}) collective-permute-start(bf16[2,1936,256]{2,1,0:T(8,128)(2,1)S(1)} %pad_maximum_fusion.refs_0_), channel_id=1, source_target_pairs={{0,3},{1,0},{2,1},{3,2},{4,7},{5,4},{6,5},{7,6},{8,11},{9,8},{10,9... | collective-permute-start | bytes 5947400 | tf_op jit(solution)/shard_map/ppermute | solution.py:528
  75.4 83.1 %collective-permute-start.2 = (bf16[2,1936,256]{2,1,0:T(8,128)(2,1)S(1)}, bf16[2,1936,256]{2,1,0:T(8,128)(2,1)}, u32[]{:S(2)}, u32[]{:S(2)}) collective-permute-start(bf16[2,1936,256]{2,1,0:T(8,128)(2,1)S(1)} %pad_maximum_fusion.refs_0_), channel_id=1, source_target_pairs={{0,2},{1,3},{2,0},{3,1},{4,6},{5,7},{6,4},{7,5},{8,10},{9,11},{10,... | collective-permute-start | bytes 5947400 | tf_op jit(solution)/shard_map/ppermute | solution.py:528
  76.2 84.0 %collective-permute-start.1 = (bf16[2,1936,256]{2,1,0:T(8,128)(2,1)S(1)}, bf16[2,1936,256]{2,1,0:T(8,128)(2,1)}, u32[]{:S(2)}, u32[]{:S(2)}) collective-permute-start(bf16[2,1936,256]{2,1,0:T(8,128)(2,1)S(1)} %pad_maximum_fusion.refs_0_), channel_id=1, source_target_pairs={{0,1},{1,2},{2,3},{3,0},{4,5},{5,6},{6,7},{7,4},{8,9},{9,10},{10,1... | collective-permute-start | bytes 5947400 | tf_op jit(solution)/shard_map/ppermute | solution.py:528
  145.8 42.9 %copy-start.1 = (bf16[256,256]{1,0:T(8,128)(2,1)S(1)}, bf16[256,256]{1,0:T(8,128)(2,1)}, u32[]{:S(2)}) copy-start(bf16[256,256]{1,0:T(8,128)(2,1)} %constant.72.clone.unperm_ref) | copy-start | bytes 393220
  145.8 42.9 %all-to-all-start.1 = ((bf16[256,16,128]{2,1,0:T(8,128)(2,1)}), bf16[256,16,128]{2,1,0:T(8,128)(2,1)S(1)}, u32[]{:S(2)}, u32[]{:S(2)}) async-start(bf16[256,16,128]{2,1,0:T(8,128)(2,1)} %bitcast.7), calls=%async_computation.1 | async-start | bytes 2097152 | tf_op jit(solution)/shard_map/all_to_all | solution.py:510
  157.9 5.5 %collective-permute-start.4 = (bf16[2,1936,256]{2,1,0:T(8,128)(2,1)S(1)}, bf16[2,1936,256]{2,1,0:T(8,128)(2,1)}, u32[]{:S(2)}, u32[]{:S(2)}) collective-permute-start(bf16[2,1936,256]{2,1,0:T(8,128)(2,1)S(1)} %pad_maximum_fusion.refs_0_), channel_id=1, source_target_pairs={{0,8},{8,0},{1,9},{9,1},{2,10},{10,2},{3,11},{11,3},{4,12},{12,4},... | collective-permute-start | bytes 5947400 | tf_op jit(solution)/shard_map/ppermute | solution.py:529
  158.1 7.0 %collective-permute-start.7 = (bf16[2,1936,256]{2,1,0:T(8,128)(2,1)}, bf16[2,1936,256]{2,1,0:T(8,128)(2,1)}, u32[]{:S(2)}, u32[]{:S(2)}) collective-permute-start(bf16[2,1936,256]{2,1,0:T(8,128)(2,1)} %collective-permute-done.3.refs_3_), channel_id=1, source_target_pairs={{0,8},{8,0},{1,9},{9,1},{2,10},{10,2},{3,11},{11,3},{4,12},{12,4},... | collective-permute-start | bytes 5947400 | tf_op jit(solution)/shard_map/ppermute | solution.py:529
  158.5 9.5 %collective-permute-start.6 = (bf16[2,1936,256]{2,1,0:T(8,128)(2,1)}, bf16[2,1936,256]{2,1,0:T(8,128)(2,1)}, u32[]{:S(2)}, u32[]{:S(2)}) collective-permute-start(bf16[2,1936,256]{2,1,0:T(8,128)(2,1)} %collective-permute-done.2.refs_2_), channel_id=1, source_target_pairs={{0,8},{8,0},{1,9},{9,1},{2,10},{10,2},{3,11},{11,3},{4,12},{12,4},... | collective-permute-start | bytes 5947400 | tf_op jit(solution)/shard_map/ppermute | solution.py:529
  160.1 10.7 %collective-permute-start.5 = (bf16[2,1936,256]{2,1,0:T(8,128)(2,1)}, bf16[2,1936,256]{2,1,0:T(8,128)(2,1)}, u32[]{:S(2)}, u32[]{:S(2)}) collective-permute-start(bf16[2,1936,256]{2,1,0:T(8,128)(2,1)} %collective-permute-done.1.refs_1_), channel_id=1, source_target_pairs={{0,8},{8,0},{1,9},{9,1},{2,10},{10,2},{3,11},{11,3},{4,12},{12,4},... | collective-permute-start | bytes 5947400 | tf_op jit(solution)/shard_map/ppermute | solution.py:529

commit v6 on v5

--- a/solution.py
+++ b/solution.py
@@ -226,7 +226,7 @@
         table_copy(n).start()
 
     flip_f[:, :, HALF * OWN :, :] = jnp.zeros((2, 4, OWN, 128), F32)
-    spec_f[:, :, HALF * OWN :, :] = jnp.zeros((2, 4, 16 * OWN, 128), F32)
+    spec_f[:, :, HALF * OWN : C_ROWS * OWN, :] = jnp.zeros((2, 4, 16 * OWN, 128), F32)
     table_copy(6).wait()
     flip = flip_ref[...]
     for part in range(4):
@@ -264,7 +264,7 @@
     x_copy.wait()
     for q in range(4):
         x_q = msg_ref[:, S_ROWS:, q * 128 : q * 128 + 128]
-        x_f[q] = x_q.reshape(HALF * OWN, 128).astype(F32)
+        x_f[q, : HALF * OWN, :] = x_q.reshape(HALF * OWN, 128).astype(F32)
     for n in range(6):
         table_copy(n).wait()
     top = lax.broadcasted_iota(jnp.int32, (16, 128), 0) == 0
@@ -381,10 +381,10 @@
         scratch_shapes=[
             pltpu.VMEM((SEQ, S_ROWS + X_ROWS, COLS), BF16),
             *(pltpu.VMEM(t.shape, t.dtype) for t in tabs),
-            pltpu.VMEM((4, HALF * OWN, 128), F32),
+            pltpu.VMEM((4, HALF * OWN + OWN, 128), F32),
             pltpu.VMEM((2, 4, HALF * OWN + OWN, 128), F32),
-            pltpu.VMEM((2, 4, C_ROWS * OWN, 128), F32),
-            pltpu.VMEM((4, HALF * OWN, 128), F32),
+            pltpu.VMEM((2, 4, C_ROWS * OWN + OWN, 128), F32),
+            pltpu.VMEM((4, HALF * OWN + OWN, 128), F32),
             pltpu.SemaphoreType.DMA((9,)),
             pltpu.SemaphoreType.DMA((7,)),
         ],

time: 220 us -> 220 us (level)
  no operation moved by 1% of the time
where the time goes in v6:
time: 220 us; the launch traced here: 218 us
  waiting for transfers between devices  142 us (65%)
  starting transfers between devices  29.6 us (13%)
  Pallas kernels  25.7 us (12%)
  blocking collectives  18.8 us (9%)
    all_to_all x2, waiting for transfers between devices, exchange(): return lax.all_to_all(value, axis, split_axis=0, concat_axis=0, tiled=True)  76 us
    ppermute x1, waiting for transfers between devices, per_device(): other = lax.ppermute(weights, 'chan', [(n, n ^ 4) for n in range(CHAN)])  53.9 us
    all_to_all x2, starting transfers between devices, exchange(): return lax.all_to_all(value, axis, split_axis=0, concat_axis=0, tiled=True)  23.6 us
    all_to_all x1, blocking collectives, exchange(): return lax.all_to_all(value, axis, split_axis=0, concat_axis=0, tiled=True)  18.8 us
    ppermute x4, waiting for transfers between devices, per_device(): twins = [lax.ppermute(part, 'core', [(0, 1), (1, 0)]) for part in held]  10.6 us
    pallas_call x1, Pallas kernels, convolve(): pl.pallas_call(conv_kernel, in_specs=[hbm, vmem] + [hbm] * len(tabs), out...  10.5 us
    pallas_call x1, Pallas kernels, mlp(): pl.pallas_call(mlp_kernel, in_specs=[pl.BlockSpec(memory_space=pltpu.SMEM...  9.09 us
    pallas_call x1, Pallas kernels, pack(): pl.pallas_call(pack_kernel, in_specs=[pl.BlockSpec(memory_space=pltpu.SME...  6.08 us
  transfers between devices with their start and end apart: 10, of which 8 were waited for; matrix products, arithmetic and copies ran while one was open for 0% of the time, Pallas kernels for 5%

profile of v6, /device:TPU:32, one launch (start us, length us, event | category | flops | bytes accessed | tf_op | source)
XLA Modules:
  0.0 217.6 jit_solution(17403727421604326717)
XLA Ops:
  0.0 0.0 copy-start
  0.0 6.1 %pack.1 = (bf16[32,160,512]{2,1,0:T(8,128)(2,1)}, bf16[1936,256]{1,0:T(8,128)(2,1)}) custom-call(s32[1]{0:T(128)} %bitcast.2.core_ref, bf16[4,512,256]{2,1,0:T(8,128)(2,1)} %bitcast.16, bf16[16,512,256]{2,1,0:T(8,128)(2,1)} %bitcast.14, bf16[512,512]{1,0:T(8,128)(2,1)} %constant.64.clone.perm_hbm, bf16[1,256,256]{2,1,0:T(8,128)(2,1)} %refs_0_.2, ...), custom_call_target="tpu_custom_call" | custom-call | tf_op jit(solution)/shard_map/pack/pallas_call | solution.py:177
  6.1 0.0 copy-start.2
  6.1 11.6 %all-to-all-start = ((bf16[32,160,512]{2,1,0:T(8,128)(2,1)}), bf16[32,160,512]{2,1,0:T(8,128)(2,1)}, u32[]{:S(2)}, u32[]{:S(2)}) async-start(bf16[32,160,512]{2,1,0:T(8,128)(2,1)} %get-tuple-element.7), calls=%async_computation | async-start | bytes 10485760 | tf_op jit(solution)/shard_map/all_to_all | solution.py:510
  17.7 0.0 copy-done.2
  17.7 0.8 collective-permute-start
  18.4 53.9 %collective-permute-done = bf16[1936,256]{1,0:T(8,128)(2,1)S(1)} collective-permute-done((bf16[1936,256]{1,0:T(8,128)(2,1)S(1)}, bf16[1936,256]{1,0:T(8,128)(2,1)S(1)}, u32[]{:S(2)}, u32[]{:S(2)}) %collective-permute-start) | collective-permute-done | bytes 991264 | tf_op jit(solution)/shard_map/ppermute | solution.py:524
  72.3 0.2 pad_maximum_fusion.refs_0_
  72.5 2.8 %collective-permute-start.3 = (bf16[2,1936,256]{2,1,0:T(8,128)(2,1)S(1)}, bf16[2,1936,256]{2,1,0:T(8,128)(2,1)}, u32[]{:S(2)}, u32[]{:S(2)}) collective-permute-start(bf16[2,1936,256]{2,1,0:T(8,128)(2,1)S(1)} %pad_maximum_fusion.refs_0_), channel_id=1, source_target_pairs={{0,3},{1,0},{2,1},{3,2},{4,7},{5,4},{6,5},{7,6},{8,11},{9,8},{10,9... | collective-permute-start | bytes 5947400 | tf_op jit(solution)/shard_map/ppermute | solution.py:528
  75.4 0.8 collective-permute-start.2
  76.2 0.9 collective-permute-start.1
  77.0 0.0 copy-done
  77.0 0.1 dynamic-slice_bitcast_fusion
  77.1 0.1 copy.20.skip_ref
  77.2 58.1 %all-to-all-done.msg_hbm = bf16[32,160,512]{2,1,0:T(8,128)(2,1)} async-done(((bf16[32,160,512]{2,1,0:T(8,128)(2,1)}), bf16[32,160,512]{2,1,0:T(8,128)(2,1)}, u32[]{:S(2)}, u32[]{:S(2)}) %all-to-all-start) | async-done | bytes 5242912 | tf_op jit(solution)/shard_map/all_to_all | solution.py:510
  135.3 10.5 %convolve.1 = bf16[128,2,16,128]{3,2,1,0:T(8,128)(2,1)} custom-call(bf16[32,160,512]{2,1,0:T(8,128)(2,1)} %all-to-all-done.msg_hbm, f32[8,1]{1,0:T(8,128)S(1)} %copy.20.skip_ref, bf16[288,128]{1,0:T(8,128)(2,1)} %constant.65.clone.refs_0_, bf16[128,256]{1,0:T(8,128)(2,1)} %constant.66.clone.refs_1_, f32[144,512]{1,0:T(8,128)} %constant.67.clone.refs_2_, ...), custom_call_target="tpu_custom_call" | custom-call | tf_op jit(solution)/shard_map/convolve/pallas_call | solution.py:376
  145.8 0.0 copy-start.1
  145.8 12.0 %all-to-all-start.1 = ((bf16[256,16,128]{2,1,0:T(8,128)(2,1)}), bf16[256,16,128]{2,1,0:T(8,128)(2,1)S(1)}, u32[]{:S(2)}, u32[]{:S(2)}) async-start(bf16[256,16,128]{2,1,0:T(8,128)(2,1)} %bitcast.7), calls=%async_computation.1 | async-start | bytes 2097152 | tf_op jit(solution)/shard_map/all_to_all | solution.py:510
  157.9 0.2 collective-permute-start.4
  158.1 0.0 collective-permute-done.3.refs_3_
  158.1 0.4 collective-permute-start.7
  158.5 0.0 collective-permute-done.2.refs_2_
  158.5 0.1 collective-permute-start.6
  158.6 1.5 collective-permute-done.1.refs_1_
  160.1 0.0 collective-permute-start.5
  160.1 0.1 pad_add_fusion.place_ref
  160.2 3.2 %collective-permute-done.4.refs_4_ = bf16[2,1936,256]{2,1,0:T(8,128)(2,1)} collective-permute-done((bf16[2,1936,256]{2,1,0:T(8,128)(2,1)S(1)}, bf16[2,1936,256]{2,1,0:T(8,128)(2,1)}, u32[]{:S(2)}, u32[]{:S(2)}) %collective-permute-start.4) | collective-permute-done | bytes 1982496 | tf_op jit(solution)/shard_map/ppermute | solution.py:529
  163.4 1.7 collective-permute-done.7.refs_7_
  165.1 2.8 %collective-permute-done.6.refs_6_ = bf16[2,1936,256]{2,1,0:T(8,128)(2,1)} collective-permute-done((bf16[2,1936,256]{2,1,0:T(8,128)(2,1)}, bf16[2,1936,256]{2,1,0:T(8,128)(2,1)}, u32[]{:S(2)}, u32[]{:S(2)}) %collective-permute-start.6) | collective-permute-done | bytes 1982496 | tf_op jit(solution)/shard_map/ppermute | solution.py:529
  168.0 2.8 %collective-permute-done.5.refs_5_ = bf16[2,1936,256]{2,1,0:T(8,128)(2,1)} collective-permute-done((bf16[2,1936,256]{2,1,0:T(8,128)(2,1)}, bf16[2,1936,256]{2,1,0:T(8,128)(2,1)}, u32[]{:S(2)}, u32[]{:S(2)}) %collective-permute-start.5) | collective-permute-done | bytes 1982496 | tf_op jit(solution)/shard_map/ppermute | solution.py:529
  170.8 17.9 %all-to-all-done.1 = bf16[256,16,128]{2,1,0:T(8,128)(2,1)S(1)} async-done(((bf16[256,16,128]{2,1,0:T(8,128)(2,1)}), bf16[256,16,128]{2,1,0:T(8,128)(2,1)S(1)}, u32[]{:S(2)}, u32[]{:S(2)}) %all-to-all-start.1) | async-done | bytes 1048608 | tf_op jit(solution)/shard_map/all_to_all | solution.py:510
  188.7 0.0 copy-done.1
  188.7 9.1 %mlp.1 = bf16[8,256,256]{2,1,0:T(8,128)(2,1)S(1)} custom-call(s32[3]{0:T(128)S(1)} %pad_add_fusion.place_ref, bf16[32,8,16,128]{3,2,1,0:T(8,128)(2,1)S(1)} %bitcast.13, bf16[256,256]{1,0:T(8,128)(2,1)S(1)} %copy-done.1, bf16[2,1936,256]{2,1,0:T(8,128)(2,1)S(1)} %pad_maximum_fusion.refs_0_, bf16[2,1936,256]{2,1,0:T(8,128)(2,1)} %collective-permute-done.1.refs_1_, ...), custom_call_target="tpu_custom_call" | custom-call | tf_op jit(solution)/shard_map/mlp/pallas_call | solution.py:490
  197.8 18.8 %all_to_all.15 = bf16[8,256,256]{2,1,0:T(8,128)(2,1)S(1)} all-to-all(bf16[8,256,256]{2,1,0:T(8,128)(2,1)S(1)} %mlp.1), channel_id=1, replica_groups=mesh['chip'=16,'core'=2,'chan'=8] {'chan'}, dimensions={0} | all-to-all | bytes 2097152 | tf_op jit(solution)/shard_map/all_to_all | solution.py:510
  216.6 1.0 copy.22
Async XLA Ops:
  0.0 77.0 %copy-start = (f32[256]{0:T(256)S(1)}, f32[256]{0:T(256)}, u32[]{:S(2)}) copy-start(f32[256]{0:T(256)} %param.21) | copy-start | bytes 3076
  6.1 11.6 %copy-start.2 = (bf16[1936,256]{1,0:T(8,128)(2,1)S(1)}, bf16[1936,256]{1,0:T(8,128)(2,1)}, u32[]{:S(2)}) copy-start(bf16[1936,256]{1,0:T(8,128)(2,1)} %get-tuple-element.8) | copy-start | bytes 2973700
  6.1 129.2 %all-to-all-start = ((bf16[32,160,512]{2,1,0:T(8,128)(2,1)}), bf16[32,160,512]{2,1,0:T(8,128)(2,1)}, u32[]{:S(2)}, u32[]{:S(2)}) async-start(bf16[32,160,512]{2,1,0:T(8,128)(2,1)} %get-tuple-element.7), calls=%async_computation | async-start | bytes 10485760 | tf_op jit(solution)/shard_map/all_to_all | solution.py:510
  17.7 54.7 %collective-permute-start = (bf16[1936,256]{1,0:T(8,128)(2,1)S(1)}, bf16[1936,256]{1,0:T(8,128)(2,1)S(1)}, u32[]{:S(2)}, u32[]{:S(2)}) collective-permute-start(bf16[1936,256]{1,0:T(8,128)(2,1)S(1)} %copy-done.2), channel_id=1, source_target_pairs={{0,4},{1,5},{2,6},{3,7},{4,0},{5,1},{6,2},{7,3},{8,12},{9,13},{10,... | collective-permute-start | bytes 2973704 | tf_op jit(solution)/shard_map/ppermute | solution.py:524
  72.5 85.6 %collective-permute-start.3 = (bf16[2,1936,256]{2,1,0:T(8,128)(2,1)S(1)}, bf16[2,1936,256]{2,1,0:T(8,128)(2,1)}, u32[]{:S(2)}, u32[]{:S(2)}) collective-permute-start(bf16[2,1936,256]{2,1,0:T(8,128)(2,1)S(1)} %pad_maximum_fusion.refs_0_), channel_id=1, source_target_pairs={{0,3},{1,0},{2,1},{3,2},{4,7},{5,4},{6,5},{7,6},{8,11},{9,8},{10,9... | collective-permute-start | bytes 5947400 | tf_op jit(solution)/shard_map/ppermute | solution.py:528
  75.4 83.1 %collective-permute-start.2 = (bf16[2,1936,256]{2,1,0:T(8,128)(2,1)S(1)}, bf16[2,1936,256]{2,1,0:T(8,128)(2,1)}, u32[]{:S(2)}, u32[]{:S(2)}) collective-permute-start(bf16[2,1936,256]{2,1,0:T(8,128)(2,1)S(1)} %pad_maximum_fusion.refs_0_), channel_id=1, source_target_pairs={{0,2},{1,3},{2,0},{3,1},{4,6},{5,7},{6,4},{7,5},{8,10},{9,11},{10,... | collective-permute-start | bytes 5947400 | tf_op jit(solution)/shard_map/ppermute | solution.py:528
  76.2 84.0 %collective-permute-start.1 = (bf16[2,1936,256]{2,1,0:T(8,128)(2,1)S(1)}, bf16[2,1936,256]{2,1,0:T(8,128)(2,1)}, u32[]{:S(2)}, u32[]{:S(2)}) collective-permute-start(bf16[2,1936,256]{2,1,0:T(8,128)(2,1)S(1)} %pad_maximum_fusion.refs_0_), channel_id=1, source_target_pairs={{0,1},{1,2},{2,3},{3,0},{4,5},{5,6},{6,7},{7,4},{8,9},{9,10},{10,1... | collective-permute-start | bytes 5947400 | tf_op jit(solution)/shard_map/ppermute | solution.py:528
  145.8 42.9 %copy-start.1 = (bf16[256,256]{1,0:T(8,128)(2,1)S(1)}, bf16[256,256]{1,0:T(8,128)(2,1)}, u32[]{:S(2)}) copy-start(bf16[256,256]{1,0:T(8,128)(2,1)} %constant.72.clone.unperm_ref) | copy-start | bytes 393220
  145.8 42.9 %all-to-all-start.1 = ((bf16[256,16,128]{2,1,0:T(8,128)(2,1)}), bf16[256,16,128]{2,1,0:T(8,128)(2,1)S(1)}, u32[]{:S(2)}, u32[]{:S(2)}) async-start(bf16[256,16,128]{2,1,0:T(8,128)(2,1)} %bitcast.7), calls=%async_computation.1 | async-start | bytes 2097152 | tf_op jit(solution)/shard_map/all_to_all | solution.py:510
  157.9 5.5 %collective-permute-start.4 = (bf16[2,1936,256]{2,1,0:T(8,128)(2,1)S(1)}, bf16[2,1936,256]{2,1,0:T(8,128)(2,1)}, u32[]{:S(2)}, u32[]{:S(2)}) collective-permute-start(bf16[2,1936,256]{2,1,0:T(8,128)(2,1)S(1)} %pad_maximum_fusion.refs_0_), channel_id=1, source_target_pairs={{0,8},{8,0},{1,9},{9,1},{2,10},{10,2},{3,11},{11,3},{4,12},{12,4},... | collective-permute-start | bytes 5947400 | tf_op jit(solution)/shard_map/ppermute | solution.py:529
  158.1 7.0 %collective-permute-start.7 = (bf16[2,1936,256]{2,1,0:T(8,128)(2,1)}, bf16[2,1936,256]{2,1,0:T(8,128)(2,1)}, u32[]{:S(2)}, u32[]{:S(2)}) collective-permute-start(bf16[2,1936,256]{2,1,0:T(8,128)(2,1)} %collective-permute-done.3.refs_3_), channel_id=1, source_target_pairs={{0,8},{8,0},{1,9},{9,1},{2,10},{10,2},{3,11},{11,3},{4,12},{12,4},... | collective-permute-start | bytes 5947400 | tf_op jit(solution)/shard_map/ppermute | solution.py:529
  158.5 9.5 %collective-permute-start.6 = (bf16[2,1936,256]{2,1,0:T(8,128)(2,1)}, bf16[2,1936,256]{2,1,0:T(8,128)(2,1)}, u32[]{:S(2)}, u32[]{:S(2)}) collective-permute-start(bf16[2,1936,256]{2,1,0:T(8,128)(2,1)} %collective-permute-done.2.refs_2_), channel_id=1, source_target_pairs={{0,8},{8,0},{1,9},{9,1},{2,10},{10,2},{3,11},{11,3},{4,12},{12,4},... | collective-permute-start | bytes 5947400 | tf_op jit(solution)/shard_map/ppermute | solution.py:529
  160.1 10.7 %collective-permute-start.5 = (bf16[2,1936,256]{2,1,0:T(8,128)(2,1)}, bf16[2,1936,256]{2,1,0:T(8,128)(2,1)}, u32[]{:S(2)}, u32[]{:S(2)}) collective-permute-start(bf16[2,1936,256]{2,1,0:T(8,128)(2,1)} %collective-permute-done.1.refs_1_), channel_id=1, source_target_pairs={{0,8},{8,0},{1,9},{9,1},{2,10},{10,2},{3,11},{11,3},{4,12},{12,4},... | collective-permute-start | bytes 5947400 | tf_op jit(solution)/shard_map/ppermute | solution.py:529
